TPU v7x, 32 devices: a whole 2x2x4 slice. The times are simulated.
32 devices in a mesh: dp: 4 (over x, core), blk: 4 (over z), fsdp: 2 (over y).
Axes of the slice: x: 2, y: 2, z: 4, core: 2. Of those that a mesh axis runs over, the one named last changes fastest.
Arguments:
- hidden_in: bfloat16 [8, 1024, 2048], P('dp', ('blk', 'fsdp')), may hold values from -6 to 6
- out_grad: bfloat16 [8, 1024, 2048], P('dp', ('blk', 'fsdp')), may hold values from -6 to 6
- doc_lengths: int32 [8, 4], P('dp'), may hold values from 1 to 960, as said below
- norm_attn: bfloat16 [2048], P(('dp', 'blk', 'fsdp')), may hold values from 0.5 to 1.5
- query_gain: bfloat16 [128], P(('dp', 'blk', 'fsdp')), may hold values from 0.5 to 1.5
- key_gain: bfloat16 [128], P(('dp', 'blk', 'fsdp')), may hold values from 0.5 to 1.5
- query_weight: bfloat16 [2048, 2048], P(('dp', 'blk', 'fsdp')), may hold values from -0.125 to 0.125
- key_weight: bfloat16 [2048, 1024], P(('dp', 'blk', 'fsdp')), may hold values from -0.125 to 0.125
- value_weight: bfloat16 [2048, 1024], P(('dp', 'blk', 'fsdp')), may hold values from -0.125 to 0.125
- output_weight: bfloat16 [2048, 2048], P(('dp', 'blk', 'fsdp')), may hold values from -0.75 to 0.75
- norm_mlp: bfloat16 [2048], P(('dp', 'blk', 'fsdp')), may hold values from 0.5 to 1.5
- gate_weight: bfloat16 [2048, 6144], P(('dp', 'blk'), 'fsdp'), may hold values from -0.125 to 0.125
- upward_weight: bfloat16 [2048, 6144], P(('dp', 'blk'), 'fsdp'), may hold values from -0.125 to 0.125
- down_weight: bfloat16 [2048, 6144], P(('dp', 'blk'), 'fsdp'), may hold values from -0.078125 to 0.078125
Outputs:
- layer_out: bfloat16 [8, 1024, 2048], P('dp', ('blk', 'fsdp'))
- input_grad: float32 [8, 1024, 2048], P('dp', ('blk', 'fsdp'))
- norm_attn_grad: float32 [2048], P(('dp', 'blk', 'fsdp'))
- query_gain_grad: float32 [128], P(('dp', 'blk', 'fsdp'))
- key_gain_grad: float32 [128], P(('dp', 'blk', 'fsdp'))
- query_weight_grad: float32 [2048, 2048], P(('dp', 'blk', 'fsdp'))
- key_weight_grad: float32 [2048, 1024], P(('dp', 'blk', 'fsdp'))
- value_weight_grad: float32 [2048, 1024], P(('dp', 'blk', 'fsdp'))
- output_weight_grad: float32 [2048, 2048], P(('dp', 'blk', 'fsdp'))
- norm_mlp_grad: float32 [2048], P(('dp', 'blk', 'fsdp'))
- gate_weight_grad: float32 [2048, 6144], P(('dp', 'blk'), 'fsdp')
- upward_weight_grad: float32 [2048, 6144], P(('dp', 'blk'), 'fsdp')
- down_weight_grad: float32 [2048, 6144], P(('dp', 'blk'), 'fsdp')
Inputs may be any that keep to these rules, and one draw needn't show every extreme that they name: `doc_lengths`: each row's 4 lengths are positive and sum to 1024. In each group of 2 rows on one index of dp, one row's first document has 960 positions.
All inputs are finite; a program needn't handle non-finite values.
Results may differ from a plain program's by a relative error of at most 0.028.
Values may be sent and summed in bfloat16 or wider, within the bound.
No kernel may reach another device: no remote copies, remote signals or barrier semaphores. Data moves between devices by JAX's collectives and lax.ppermute only.
A program may use at most 512 MiB of HBM per device.

v0:
```python
import math

import jax
import jax.numpy as jnp
from jax import lax
from jax.sharding import PartitionSpec as P

EPSILON = 1e-06
ROPE_BASE = 1000000.0
MASKED = -1e30


def normalize(values, gain):
    inverse = lax.rsqrt(jnp.mean(values * values, axis=-1, keepdims=True) + EPSILON)
    return values * inverse * gain


def rotate(values, cos_table, sine_table):
    halfway = values.shape[-1] // 2
    turned = jnp.concatenate([-values[..., halfway:], values[..., :halfway]], axis=-1)
    return values * cos_table + turned * sine_table


def placement_of(lengths, offset, total):
    places = offset + jnp.arange(total, dtype=jnp.int32)
    ends = jnp.cumsum(lengths, axis=1)
    before = (ends[:, None, :] <= places[None, :, None]).astype(jnp.int32)
    document = jnp.sum(before, axis=2)
    doc_start = jnp.sum(before * lengths[:, None, :], axis=2)
    return (document, places[None, :] - doc_start, places)


def rotary_tables(position, head_size):
    frequency = jnp.exp(
        jnp.arange(head_size // 2, dtype=jnp.float32) * (-2.0 / head_size) * math.log(ROPE_BASE)
    )
    angles = position.astype(jnp.float32)[..., None] * frequency
    angles = jnp.concatenate([angles, angles], axis=-1)
    return (jnp.cos(angles)[:, :, None, :], jnp.sin(angles)[:, :, None, :])


def head_path(raw_rows, gain, cos_table, sine_table):
    shaped = raw_rows.reshape(raw_rows.shape[0], raw_rows.shape[1], -1, gain.shape[0])
    return rotate(normalize(shaped, gain), cos_table, sine_table)


def block_size(total):
    return max((divisor for divisor in range(1, min(total, 512) + 1) if total % divisor == 0))


def silu_slope(gate_proj):
    logistic = jax.nn.sigmoid(gate_proj)
    return logistic * (1.0 + gate_proj * (1.0 - logistic))


def shards(
    hidden_in,
    out_grad,
    doc_lengths,
    norm_attn,
    query_gain,
    key_gain,
    query_weight,
    key_weight,
    value_weight,
    output_weight,
    norm_mlp,
    gate_weight,
    upward_weight,
    down_weight,
):
    attn_set = (
        lax.all_gather(query_weight, ("dp", "blk", "fsdp"), axis=0, tiled=True),
        lax.all_gather(key_weight, ("dp", "blk", "fsdp"), axis=0, tiled=True),
        lax.all_gather(value_weight, ("dp", "blk", "fsdp"), axis=0, tiled=True),
        lax.all_gather(output_weight, ("dp", "blk", "fsdp"), axis=0, tiled=True),
        lax.all_gather(norm_attn, ("dp", "blk", "fsdp"), axis=0, tiled=True),
        lax.all_gather(query_gain, ("dp", "blk", "fsdp"), axis=0, tiled=True),
        lax.all_gather(key_gain, ("dp", "blk", "fsdp"), axis=0, tiled=True),
        lax.all_gather(norm_mlp, ("dp", "blk", "fsdp"), axis=0, tiled=True),
    )
    query_mat, key_mat, value_mat, out_mat = (attn_set[0], attn_set[1], attn_set[2], attn_set[3])
    gain_attn = attn_set[4].astype(jnp.float32)
    gain_query = attn_set[5].astype(jnp.float32)
    gain_key = attn_set[6].astype(jnp.float32)
    gain_mlp = attn_set[7].astype(jnp.float32)
    gate_mat, upward_mat, down_mat = (
        lax.all_gather(gate_weight, ("dp", "blk"), axis=0, tiled=True),
        lax.all_gather(upward_weight, ("dp", "blk"), axis=0, tiled=True),
        lax.all_gather(down_weight, ("dp", "blk"), axis=0, tiled=True),
    )
    seq_count, local_rows, _width = hidden_in.shape
    head_size = gain_key.shape[0]
    heads_kv = key_mat.shape[1] // head_size
    heads_q = query_mat.shape[1] // head_size
    group_size = heads_q // heads_kv
    softmax_scale = 1.0 / math.sqrt(head_size)
    offset = lax.axis_index(("blk", "fsdp")) * local_rows
    query_doc, query_pos, query_place = placement_of(doc_lengths, offset, local_rows)
    cos_table, sine_table = rotary_tables(query_pos, head_size)
    layer_in = hidden_in.astype(jnp.float32)
    first_norm = normalize(layer_in, gain_attn).astype(jnp.bfloat16)
    query_raw = jnp.dot(first_norm, query_mat, preferred_element_type=jnp.float32)
    key_raw = jnp.dot(first_norm, key_mat, preferred_element_type=jnp.float32)
    value_rows = jnp.dot(first_norm, value_mat, preferred_element_type=jnp.float32).astype(
        jnp.bfloat16
    )
    query_rows = head_path(query_raw, gain_query, cos_table, sine_table).astype(jnp.bfloat16)
    query_rows = query_rows.reshape(seq_count, local_rows, heads_kv, group_size, head_size)
    key_rows = head_path(key_raw, gain_key, cos_table, sine_table).astype(jnp.bfloat16)
    key_rows = key_rows.reshape(seq_count, local_rows, heads_kv * head_size)

    def score_block(key_part, first_key):
        key_count = key_part.shape[1]
        key_heads = key_part.reshape(seq_count, key_count, heads_kv, head_size)
        scores = (
            jnp.einsum(
                "sckgd,spkd->skgcp", query_rows, key_heads, preferred_element_type=jnp.float32
            )
            * softmax_scale
        )
        key_doc, _key_pos, key_place = placement_of(doc_lengths, first_key, key_count)
        visible = (query_doc[:, None, None, :, None] == key_doc[:, None, None, None, :]) & (
            key_place[None, None, None, None, :] <= query_place[None, None, None, :, None]
        )
        return (scores, visible)

    def attend_block(running, key_part, value_part, first_key):
        run_max, run_total, run_sum = running
        scores, visible = score_block(key_part, first_key)
        masked = jnp.where(visible, scores, MASKED)
        new_max = jnp.maximum(run_max, jnp.max(masked, axis=-1))
        weights = jnp.where(visible, jnp.exp(masked - new_max[..., None]), 0.0)
        rescale = jnp.exp(run_max - new_max)
        value_heads = value_part.reshape(seq_count, -1, heads_kv, head_size)
        update = jnp.einsum(
            "skgcp,spkd->sckgd",
            weights.astype(jnp.bfloat16),
            value_heads,
            preferred_element_type=jnp.float32,
        )
        rescale_rows = jnp.transpose(rescale, (0, 3, 1, 2))[..., None]
        return (
            new_max,
            run_total * rescale + jnp.sum(weights, axis=-1),
            run_sum * rescale_rows + update,
        )

    start_carry = (
        jnp.full((seq_count, heads_kv, group_size, local_rows), MASKED, jnp.float32),
        jnp.zeros((seq_count, heads_kv, group_size, local_rows), jnp.float32),
        jnp.zeros((seq_count, local_rows, heads_kv, group_size, head_size), jnp.float32),
    )
    first_key = jnp.int32(0)
    key_part = lax.all_gather(key_rows, ("blk", "fsdp"), axis=1, tiled=True)
    value_part = lax.all_gather(value_rows, ("blk", "fsdp"), axis=1, tiled=True)
    piece_rows = key_part.shape[1]
    fold_block_len = block_size(piece_rows)

    def one_block(block_index, inner):
        begin_row = block_index * fold_block_len
        return attend_block(
            inner,
            lax.dynamic_slice_in_dim(key_part, begin_row, fold_block_len, 1),
            lax.dynamic_slice_in_dim(value_part, begin_row, fold_block_len, 1),
            first_key + begin_row,
        )

    running = lax.fori_loop(0, piece_rows // fold_block_len, one_block, start_carry)
    run_max, run_total, run_sum = running
    attn_mix = run_sum / jnp.transpose(run_total, (0, 3, 1, 2))[..., None]
    log_total = run_max + jnp.log(run_total)
    mix_rows = attn_mix.reshape(seq_count, local_rows, heads_q * head_size).astype(jnp.bfloat16)
    residual = layer_in + jnp.dot(mix_rows, out_mat, preferred_element_type=jnp.float32)
    second_norm = normalize(residual, gain_mlp).astype(jnp.bfloat16)
    pair_rows = lax.all_gather(second_norm, "fsdp", axis=1, tiled=True)
    gate_proj = jnp.dot(pair_rows, gate_mat, preferred_element_type=jnp.float32)
    upward_proj = jnp.dot(pair_rows, upward_mat, preferred_element_type=jnp.float32)
    hidden_rows = (jax.nn.silu(gate_proj) * upward_proj).astype(jnp.bfloat16)
    down_part = jnp.einsum("scf,df->scd", hidden_rows, down_mat, preferred_element_type=jnp.float32)
    mlp_out = lax.psum_scatter(
        down_part.astype(jnp.bfloat16), "fsdp", scatter_dimension=1, tiled=True
    ).astype(jnp.float32)
    layer_out = (residual + mlp_out).astype(jnp.bfloat16)
    top_grad = out_grad.astype(jnp.float32)
    gate_back, upward_back, down_back = (
        lax.all_gather(gate_weight, ("dp", "blk"), axis=0, tiled=True),
        lax.all_gather(upward_weight, ("dp", "blk"), axis=0, tiled=True),
        lax.all_gather(down_weight, ("dp", "blk"), axis=0, tiled=True),
    )
    pair_grad = lax.all_gather(out_grad, "fsdp", axis=1, tiled=True)
    hidden_grad = jnp.einsum(
        "scd,df->scf", pair_grad, down_back, preferred_element_type=jnp.float32
    )
    down_wgrad = jnp.einsum(
        "scd,scf->df", pair_grad, hidden_rows, preferred_element_type=jnp.float32
    )
    gate_grad = (hidden_grad * upward_proj * silu_slope(gate_proj)).astype(jnp.bfloat16)
    upward_grad = (hidden_grad * jax.nn.silu(gate_proj)).astype(jnp.bfloat16)
    gate_wgrad = jnp.einsum("scd,scf->df", pair_rows, gate_grad, preferred_element_type=jnp.float32)
    upward_wgrad = jnp.einsum(
        "scd,scf->df", pair_rows, upward_grad, preferred_element_type=jnp.float32
    )
    norm_part = jnp.einsum("scf,df->scd", gate_grad, gate_back, preferred_element_type=jnp.float32)
    norm_part = norm_part + jnp.einsum(
        "scf,df->scd", upward_grad, upward_back, preferred_element_type=jnp.float32
    )
    second_grad = lax.psum_scatter(
        norm_part.astype(jnp.bfloat16), "fsdp", scatter_dimension=1, tiled=True
    ).astype(jnp.float32)
    mlp_wgrads = (
        lax.psum_scatter(gate_wgrad, ("dp", "blk"), scatter_dimension=0, tiled=True),
        lax.psum_scatter(upward_wgrad, ("dp", "blk"), scatter_dimension=0, tiled=True),
        lax.psum_scatter(down_wgrad, ("dp", "blk"), scatter_dimension=0, tiled=True),
    )
    _second_value, second_pull = jax.vjp(normalize, residual, gain_mlp)
    residual_part, gain_mlp_grad = second_pull(second_grad)
    residual_grad = top_grad + residual_part
    query_back, key_back, value_back, out_back = (
        lax.all_gather(query_weight, ("dp", "blk", "fsdp"), axis=0, tiled=True),
        lax.all_gather(key_weight, ("dp", "blk", "fsdp"), axis=0, tiled=True),
        lax.all_gather(value_weight, ("dp", "blk", "fsdp"), axis=0, tiled=True),
        lax.all_gather(output_weight, ("dp", "blk", "fsdp"), axis=0, tiled=True),
    )
    residual_low = residual_grad.astype(jnp.bfloat16)
    out_wgrad = jnp.einsum(
        "sce,scd->ed", mix_rows, residual_low, preferred_element_type=jnp.float32
    )
    mix_grad = jnp.einsum("scd,ed->sce", residual_low, out_back, preferred_element_type=jnp.float32)
    mix_grad = mix_grad.astype(jnp.bfloat16).reshape(
        seq_count, local_rows, heads_kv, group_size, head_size
    )
    delta = jnp.transpose(jnp.sum(mix_grad.astype(jnp.float32) * attn_mix, axis=-1), (0, 2, 3, 1))
    key_all, value_all = (
        lax.all_gather(key_rows, ("blk", "fsdp"), axis=1, tiled=True),
        lax.all_gather(value_rows, ("blk", "fsdp"), axis=1, tiled=True),
    )
    full_rows = key_all.shape[1]
    block_len = block_size(full_rows)

    def back_block(block_index, running_back):
        query_acc, key_buffer, value_buffer = running_back
        first_key = block_index * block_len
        key_part = lax.dynamic_slice_in_dim(key_all, first_key, block_len, 1)
        value_part = lax.dynamic_slice_in_dim(value_all, first_key, block_len, 1)
        key_heads = key_part.reshape(seq_count, block_len, heads_kv, head_size)
        value_heads = value_part.reshape(seq_count, block_len, heads_kv, head_size)
        scores, visible = score_block(key_part, first_key)
        probs = jnp.where(
            visible, jnp.exp(jnp.where(visible, scores, MASKED) - log_total[..., None]), 0.0
        )
        probs_grad = jnp.einsum(
            "sckgd,spkd->skgcp", mix_grad, value_heads, preferred_element_type=jnp.float32
        )
        score_grad = (probs * (probs_grad - delta[..., None])).astype(jnp.bfloat16)
        query_acc = (
            query_acc
            + jnp.einsum(
                "skgcp,spkd->sckgd", score_grad, key_heads, preferred_element_type=jnp.float32
            )
            * softmax_scale
        )
        key_piece = (
            jnp.einsum(
                "skgcp,sckgd->spkd", score_grad, query_rows, preferred_element_type=jnp.float32
            )
            * softmax_scale
        )
        value_piece = jnp.einsum(
            "skgcp,sckgd->spkd",
            probs.astype(jnp.bfloat16),
            mix_grad,
            preferred_element_type=jnp.float32,
        )
        key_buffer = lax.dynamic_update_slice_in_dim(
            key_buffer, key_piece.reshape(seq_count, block_len, -1), first_key, 1
        )
        value_buffer = lax.dynamic_update_slice_in_dim(
            value_buffer, value_piece.reshape(seq_count, block_len, -1), first_key, 1
        )
        return (query_acc, key_buffer, value_buffer)

    back_init = (
        jnp.zeros((seq_count, local_rows, heads_kv, group_size, head_size), jnp.float32),
        jnp.zeros((seq_count, full_rows, heads_kv * head_size), jnp.float32),
        jnp.zeros((seq_count, full_rows, heads_kv * head_size), jnp.float32),
    )
    query_acc, key_buffer, value_buffer = lax.fori_loop(
        0, full_rows // block_len, back_block, back_init
    )
    key_grad, value_grad = (
        lax.psum_scatter(
            key_buffer.astype(jnp.bfloat16), ("blk", "fsdp"), scatter_dimension=1, tiled=True
        ).astype(jnp.float32),
        lax.psum_scatter(
            value_buffer.astype(jnp.bfloat16), ("blk", "fsdp"), scatter_dimension=1, tiled=True
        ).astype(jnp.float32),
    )

    def query_path(raw_rows, gain):
        return head_path(raw_rows, gain, cos_table, sine_table)

    _query_value, query_pull = jax.vjp(query_path, query_raw, gain_query)
    query_raw_grad, gain_query_grad = query_pull(
        query_acc.reshape(seq_count, local_rows, heads_q, head_size)
    )
    _key_value, key_pull = jax.vjp(query_path, key_raw, gain_key)
    key_raw_grad, gain_key_grad = key_pull(
        key_grad.reshape(seq_count, local_rows, heads_kv, head_size)
    )
    query_low = query_raw_grad.astype(jnp.bfloat16)
    key_low = key_raw_grad.astype(jnp.bfloat16)
    value_low = value_grad.astype(jnp.bfloat16)
    query_wgrad = jnp.einsum(
        "scd,sce->de", first_norm, query_low, preferred_element_type=jnp.float32
    )
    key_wgrad = jnp.einsum("scd,sce->de", first_norm, key_low, preferred_element_type=jnp.float32)
    value_wgrad = jnp.einsum(
        "scd,sce->de", first_norm, value_low, preferred_element_type=jnp.float32
    )
    first_grad = jnp.einsum(
        "sce,de->scd", query_low, query_back, preferred_element_type=jnp.float32
    )
    first_grad = first_grad + jnp.einsum(
        "sce,de->scd", key_low, key_back, preferred_element_type=jnp.float32
    )
    first_grad = first_grad + jnp.einsum(
        "sce,de->scd", value_low, value_back, preferred_element_type=jnp.float32
    )
    _first_value, first_pull = jax.vjp(normalize, layer_in, gain_attn)
    layer_part, gain_attn_grad = first_pull(first_grad)
    input_grad = residual_grad + layer_part
    attn_wgrads = (
        lax.psum_scatter(query_wgrad, ("dp", "blk", "fsdp"), scatter_dimension=0, tiled=True),
        lax.psum_scatter(key_wgrad, ("dp", "blk", "fsdp"), scatter_dimension=0, tiled=True),
        lax.psum_scatter(value_wgrad, ("dp", "blk", "fsdp"), scatter_dimension=0, tiled=True),
        lax.psum_scatter(out_wgrad, ("dp", "blk", "fsdp"), scatter_dimension=0, tiled=True),
        lax.psum_scatter(gain_attn_grad, ("dp", "blk", "fsdp"), scatter_dimension=0, tiled=True),
        lax.psum_scatter(gain_query_grad, ("dp", "blk", "fsdp"), scatter_dimension=0, tiled=True),
        lax.psum_scatter(gain_key_grad, ("dp", "blk", "fsdp"), scatter_dimension=0, tiled=True),
        lax.psum_scatter(gain_mlp_grad, ("dp", "blk", "fsdp"), scatter_dimension=0, tiled=True),
    )
    return (
        layer_out,
        input_grad,
        attn_wgrads[4],
        attn_wgrads[5],
        attn_wgrads[6],
        attn_wgrads[0],
        attn_wgrads[1],
        attn_wgrads[2],
        attn_wgrads[3],
        attn_wgrads[7],
        mlp_wgrads[0],
        mlp_wgrads[1],
        mlp_wgrads[2],
    )


def solution(mesh):
    return jax.shard_map(
        shards,
        mesh=mesh,
        in_specs=(
            P("dp", ("blk", "fsdp"), None),
            P("dp", ("blk", "fsdp"), None),
            P("dp", None),
            P(("dp", "blk", "fsdp")),
            P(("dp", "blk", "fsdp")),
            P(("dp", "blk", "fsdp")),
            P(("dp", "blk", "fsdp"), None),
            P(("dp", "blk", "fsdp"), None),
            P(("dp", "blk", "fsdp"), None),
            P(("dp", "blk", "fsdp"), None),
            P(("dp", "blk", "fsdp")),
            P(("dp", "blk"), "fsdp"),
            P(("dp", "blk"), "fsdp"),
            P(("dp", "blk"), "fsdp"),
        ),
        out_specs=(
            P("dp", ("blk", "fsdp"), None),
            P("dp", ("blk", "fsdp"), None),
            P(("dp", "blk", "fsdp")),
            P(("dp", "blk", "fsdp")),
            P(("dp", "blk", "fsdp")),
            P(("dp", "blk", "fsdp"), None),
            P(("dp", "blk", "fsdp"), None),
            P(("dp", "blk", "fsdp"), None),
            P(("dp", "blk", "fsdp"), None),
            P(("dp", "blk", "fsdp")),
            P(("dp", "blk"), "fsdp"),
            P(("dp", "blk"), "fsdp"),
            P(("dp", "blk"), "fsdp"),
        ),
        check_vma=False,
    )
```

profile of v0, /device:TPU:0, one launch (start us, length us, event | category | flops | bytes accessed | tf_op | source)
XLA Modules:
  0.0 3038.5 jit_solution(5530015417132679523)
XLA Ops:
  12.1 42.3 %all-reduce.13 = (bf16[2048]{0:T(1024)(128)(2,1)S(1)}, bf16[128]{0:T(256)(128)(2,1)S(1)}, bf16[128]{0:T(256)(128)(2,1)}, bf16[2048]{0:T(1024)(128)(2,1)}) all-reduce(bf16[2048]{0:T(1024)(128)(2,1)S(1)} %dynamic-update-slice, bf16[128]{0:T(256)(128)(2,1)S(1)} %dynamic-update-slice.1, ...), channel_id=1, replica_groups=mesh['dp'=4,'blk'=4,'fsdp'=2] {'dp','blk','fsdp'}, use_global_device_ids=true, to_apply=%add.4 | all-reduce | flops 4352 | bytes 17408
  59.3 16.7 all-gather.12.cloned.1.call-done
  91.9 48.0 %all-gather.18.cloned.1.call-done = bf16[2048,1024]{1,0:T(8,128)(2,1)} async-done(((bf16[64,1024]{1,0:T(8,128)(2,1)}), bf16[2048,1024]{1,0:T(8,128)(2,1)}) %all-gather.18.cloned.1.call-update) | async-done | bytes 4194320 | tf_op jit(solution)/shard_map/all_gather | solution.py:75
  145.9 68.7 %all-gather.14.cloned.1.call-done = bf16[2,1024,1024]{2,1,0:T(8,128)(2,1)} async-done(((bf16[2,128,1024]{2,1,0:T(8,128)(2,1)}), bf16[2,1024,1024]{2,1,0:T(8,128)(2,1)}) %all-gather.14.cloned.1.call-update) | async-done | bytes 4194320 | tf_op jit(solution)/shard_map/all_gather | solution.py:155
  214.6 6.2 copy.225
  220.8 68.1 %all-gather.20.cloned.1.call-done = bf16[2,1024,1024]{2,1,0:T(8,128)(2,1)} async-done(((bf16[2,128,1024]{2,1,0:T(8,128)(2,1)}), bf16[2,1024,1024]{2,1,0:T(8,128)(2,1)}) %all-gather.20.cloned.1.call-update) | async-done | bytes 4194320 | tf_op jit(solution)/shard_map/all_gather | solution.py:156
  288.9 6.2 copy.227
  295.1 72.2 %all-gather.16.cloned.1.call-done = bf16[2048,2048]{1,0:T(8,128)(2,1)} async-done(((bf16[64,2048]{1,0:T(8,128)(2,1)}), bf16[2048,2048]{1,0:T(8,128)(2,1)}) %all-gather.16.cloned.1.call-update) | async-done | bytes 8388624 | tf_op jit(solution)/shard_map/all_gather | solution.py:73
  367.3 5.9 multiply_reduce_fusion.4
  376.1 38.8 %while.40 = (s32[]{:T(128)}, f32[2,8,2,128]{3,2,1,0:T(2,128)S(1)}, f32[2,8,2,128]{3,2,1,0:T(2,128)S(1)}, f32[2,128,8,2,128]{1,4,3,2,0:T(8,128)}, s32[2,128]{1,0:...) while((s32[]{:T(128)}, f32[2,8,2,128]{3,2,1,0:T(2,128)S(1)}, ...), condition=%wide.region_10.11_spmd.clone, body=%wide.region_6.10_spmd.clone.sunk | while | flops 1102941824 | bytes 77480200 | solution.py:169
  385.4 7.8 bitcast_add_fusion.4
  404.4 8.4 bitcast_add_fusion.4
  416.9 29.1 all-gather.22.cloned.1.call-done
  446.0 5.8 multiply_reduce_fusion.3
  457.5 28.8 all-gather.24.cloned.1.call-done
  486.3 103.1 %all-gather.28.cloned.1.call-done = bf16[2048,3072]{1,0:T(8,128)(2,1)} async-done(((bf16[128,3072]{1,0:T(8,128)(2,1)}), bf16[2048,3072]{1,0:T(8,128)(2,1)}) %all-gather.28.cloned.1.call-update) | async-done | bytes 12582928 | tf_op jit(solution)/shard_map/all_gather | solution.py:89
  589.4 11.9 fusion.40
  601.4 20.9 all-gather.32.cloned.1.call-done
  622.3 102.9 %all-gather.30.cloned.1.call-done = bf16[2048,3072]{1,0:T(8,128)(2,1)} async-done(((bf16[128,3072]{1,0:T(8,128)(2,1)}), bf16[2048,3072]{1,0:T(8,128)(2,1)}) %all-gather.30.cloned.1.call-update) | async-done | bytes 12582928 | tf_op jit(solution)/shard_map/all_gather | solution.py:90
  725.2 12.0 fusion.34
  737.2 89.3 %all-gather.26.cloned.1.call-done = bf16[2048,3072]{1,0:T(8,128)(2,1)} async-done(((bf16[128,3072]{1,0:T(8,128)(2,1)}), bf16[2048,3072]{1,0:T(8,128)(2,1)}) %all-gather.26.cloned.1.call-update) | async-done | bytes 12582928 | tf_op jit(solution)/shard_map/all_gather | solution.py:88
  826.5 16.9 multiply_convert_fusion.1
  843.5 13.3 fusion.38
  856.8 13.5 add_convert_fusion
  870.4 10.7 fusion.65
  881.2 19.3 reduce-scatter.18.cloned.1.call-done
  903.0 31.7 %reduce-scatter.16.cloned.1.call-done = bf16[2,128,2048]{2,1,0:T(8,128)(2,1)} async-done(((bf16[2,256,2048]{2,1,0:T(8,128)(2,1)}), bf16[2,128,2048]{2,1,0:T(8,128)(2,1)}) %reduce-scatter.16.cloned.1.call-update) | async-done | bytes 1048592 | tf_op jit(solution)/shard_map/reduce_scatter | solution.py:181
  939.4 6.7 fusion.76
  954.3 42.9 %while.41 = (s32[]{:T(128)}, f32[2,128,8,2,128]{1,4,3,2,0:T(8,128)}, bf16[2,1024,1024]{1,2,0:T(8,128)(2,1)}, bf16[2,1024,1024]{1,2,0:T(8,128)(2,1)}, bf16[2,1024...) while((s32[]{:T(128)}, ...), condition=%wide.region_18.19_spmd.clone, body=%wide.region_16.18_spmd.clone.sunk | while | flops 2713529856 | bytes 145293712 | solution.py:288
  997.2 11.3 copy.279
  1014.3 11.6 copy.281
  1025.9 5.6 copy.286
  1033.1 13.8 convolution_bitcast_fusion
  1047.1 55.2 %reduce-scatter.34.cloned.1.call-done = bf16[128,2048]{1,0:T(8,128)(2,1)} async-done(((bf16[1024,2048]{1,0:T(8,128)(2,1)}), bf16[128,2048]{1,0:T(8,128)(2,1)}) %reduce-scatter.34.cloned.1.call-update) | async-done | bytes 524304
  1114.8 79.2 %reduce-scatter.36.cloned.1.call-done = bf16[128,2048]{1,0:T(8,128)(2,1)} async-done(((bf16[1024,2048]{1,0:T(8,128)(2,1)}), bf16[128,2048]{1,0:T(8,128)(2,1)}) %reduce-scatter.36.cloned.1.call-update) | async-done | bytes 524304
  1202.1 12.8 convolution_bitcast_fusion.3
  1221.6 10.9 convolution_bitcast_fusion.4
  1232.6 14.6 convolution_bitcast_fusion.2
  1247.3 14.3 convolution_bitcast_fusion.1
  1261.6 6.0 fusion.50
  1272.9 45.7 %all-reduce.12 = (f32[2048]{0:T(1024)S(1)}, f32[128]{0:T(128)S(1)}, f32[128]{0:T(128)S(1)}, f32[2048]{0:T(1024)S(1)}) all-reduce(f32[2048]{0:T(1024)S(1)} %get-tuple-element.851, f32[128]{0:T(128)S(1)} %get-tuple-element.855, f32[128]{0:T(128)S(1)} %get-tuple-element.853, ...), channel_id=6, replica_groups=mesh['dp'=4,'blk'=4,'fsdp'=2] {'dp','blk','fsdp'}, use_global_device_ids=true, to_apply=%region_25.26.clone | all-reduce | flops 4352 | bytes 34816
  1324.5 117.6 %reduce-scatter.32.cloned.1.call-done = f32[128,3072]{0,1:T(8,128)} async-done(((f32[2048,3072]{0,1:T(8,128)}), f32[128,3072]{0,1:T(8,128)}) %reduce-scatter.32.cloned.1.call-update) | async-done | bytes 1572880 | tf_op jit(solution)/shard_map/reduce_scatter | solution.py:214
  1445.2 183.1 %reduce-scatter.22.cloned.1.call-done = f32[64,1024]{1,0:T(8,128)} async-done(((f32[2048,1024]{1,0:T(8,128)}), f32[64,1024]{1,0:T(8,128)}) %reduce-scatter.22.cloned.1.call-update) | async-done | bytes 262160 | tf_op jit(solution)/shard_map/reduce_scatter | solution.py:335
  1628.3 186.6 %reduce-scatter.24.cloned.1.call-done = f32[64,1024]{1,0:T(8,128)} async-done(((f32[2048,1024]{1,0:T(8,128)}), f32[64,1024]{1,0:T(8,128)}) %reduce-scatter.24.cloned.1.call-update) | async-done | bytes 262160 | tf_op jit(solution)/shard_map/reduce_scatter | solution.py:336
  1814.9 360.7 %reduce-scatter.26.cloned.1.call-done = f32[64,2048]{1,0:T(8,128)} async-done(((f32[2048,2048]{1,0:T(8,128)}), f32[64,2048]{1,0:T(8,128)}) %reduce-scatter.26.cloned.1.call-update) | async-done | bytes 524304 | tf_op jit(solution)/shard_map/reduce_scatter | solution.py:337
  2175.6 360.1 %reduce-scatter.20.cloned.1.call-done = f32[64,2048]{1,0:T(8,128)} async-done(((f32[2048,2048]{1,0:T(8,128)}), f32[64,2048]{1,0:T(8,128)}) %reduce-scatter.20.cloned.1.call-update) | async-done | bytes 524304 | tf_op jit(solution)/shard_map/reduce_scatter | solution.py:334
  2535.7 247.9 %reduce-scatter.28.cloned.1.call-done = f32[128,3072]{1,0:T(8,128)} async-done(((f32[2048,3072]{1,0:T(8,128)}), f32[128,3072]{1,0:T(8,128)}) %reduce-scatter.28.cloned.1.call-update) | async-done | bytes 1572880 | tf_op jit(solution)/shard_map/reduce_scatter | solution.py:212
  2783.6 247.6 %reduce-scatter.30.cloned.1.call-done = f32[128,3072]{1,0:T(8,128)} async-done(((f32[2048,3072]{1,0:T(8,128)}), f32[128,3072]{1,0:T(8,128)}) %reduce-scatter.30.cloned.1.call-update) | async-done | bytes 1572880 | tf_op jit(solution)/shard_map/reduce_scatter | solution.py:213
  (326 shorter events, 171.2 us)
Async XLA Ops:
  7.2 68.8 %all-gather.12.cloned.1.call-start = ((), (), s32[]{:S(2)}) async-start(), calls=%async_computation.11 | async-start | bytes 4325376 | tf_op jit(solution)/shard_map/all_gather | solution.py:74
  7.9 131.9 %all-gather.18.cloned.1.call-start = ((), (), s32[]{:S(2)}) async-start(), calls=%async_computation.14 | async-start | bytes 4325376 | tf_op jit(solution)/shard_map/all_gather | solution.py:75
  8.7 205.9 %all-gather.14.cloned.1.call-start = ((), (), s32[]{:S(2)}) async-start(), calls=%async_computation.12 | async-start | bytes 4718592 | tf_op jit(solution)/shard_map/all_gather | solution.py:155
  54.4 312.9 %copy-start.41 = (f32[2048]{0:T(1024)}, f32[2048]{0:T(1024)S(1)}, u32[]{:S(2)}) copy-start(f32[2048]{0:T(1024)S(1)} %convert_element_type.152) | copy-start | bytes 24580
  56.6 317.3 %copy-start.33 = (f32[2,128,128]{1,2,0:T(8,128)}, f32[2,128,128]{1,2,0:T(8,128)S(1)}, u32[]{:S(2)}) copy-start(f32[2,128,128]{1,2,0:T(8,128)S(1)} %get-tuple-element.936) | copy-start | bytes 393220
  56.6 317.3 %copy-start.35 = (f32[2,128,128]{1,2,0:T(8,128)}, f32[2,128,128]{1,2,0:T(8,128)S(1)}, u32[]{:S(2)}) copy-start(f32[2,128,128]{1,2,0:T(8,128)S(1)} %get-tuple-element.937) | copy-start | bytes 393220
  58.7 20.8 copy-start.53
  58.7 20.8 copy-start.45
  80.7 4.5 copy-start.12
  88.7 51.1 %copy-start.46 = (f32[2,128]{1,0:T(2,128)S(1)}, f32[2,128]{1,0:T(2,128)}, u32[]{:S(2)}) copy-start(f32[2,128]{1,0:T(2,128)} %copy-done.45) | copy-start | bytes 3076
  91.8 54.1 %copy-start.62 = (bf16[128]{0:T(256)(128)(2,1)S(1)}, bf16[128]{0:T(256)(128)(2,1)}, u32[]{:S(2)}) copy-start(bf16[128]{0:T(256)(128)(2,1)} %get-tuple-element.911) | copy-start | bytes 772
  91.8 54.1 %copy-start.59 = (bf16[2048]{0:T(1024)(128)(2,1)S(1)}, bf16[2048]{0:T(1024)(128)(2,1)}, u32[]{:S(2)}) copy-start(bf16[2048]{0:T(1024)(128)(2,1)} %get-tuple-element.912) | copy-start | bytes 12292
  91.8 197.0 %all-gather.20.cloned.1.call-start = ((), (), s32[]{:S(2)}) async-start(), calls=%async_computation.15 | async-start | bytes 4718592 | tf_op jit(solution)/shard_map/all_gather | solution.py:156
  144.1 223.1 %all-gather.16.cloned.1.call-start = ((), (), s32[]{:S(2)}) async-start(), calls=%async_computation.13 | async-start | bytes 8650752 | tf_op jit(solution)/shard_map/all_gather | solution.py:73
  144.7 301.3 %all-gather.22.cloned.1.call-start = ((), (), s32[]{:S(2)}) async-start(), calls=%async_computation.16 | async-start | bytes 8650752 | tf_op jit(solution)/shard_map/all_gather | solution.py:76
  145.3 341.0 %all-gather.24.cloned.1.call-start = ((), (), s32[]{:S(2)}) async-start(), calls=%async_computation.17 | async-start | bytes 3145728 | tf_op jit(solution)/shard_map/all_gather | solution.py:176
  145.9 228.0 %copy-start.57 = (f32[128]{0:T(128)}, f32[128]{0:T(128)S(1)}, u32[]{:S(2)}) copy-start(f32[128]{0:T(128)S(1)} %convert_element_type.157) | copy-start | bytes 1540
  385.4 7.8 copy-start
  404.4 8.4 copy-start
  416.9 34.9 %copy-start.19 = (bf16[2,128,8,2,128]{1,4,3,2,0:T(8,128)(2,1)}, bf16[2,128,8,2,128]{1,4,3,2,0:T(8,128)(2,1)S(1)}, u32[]{:S(2)}) copy-start(bf16[2,128,8,2,128]{1,4,3,2,0:T(8,128)(2,1)S(1)} %fusion.101) | copy-start | bytes 3145732
  454.4 135.0 %all-gather.28.cloned.1.call-start = ((), (), s32[]{:S(2)}) async-start(), calls=%async_computation.19 | async-start | bytes 13369344 | tf_op jit(solution)/shard_map/all_gather | solution.py:89
  455.2 167.1 %all-gather.32.cloned.1.call-start = ((), (), s32[]{:S(2)}) async-start(), calls=%async_computation.22 | async-start | bytes 3145728 | tf_op jit(solution)/shard_map/all_gather | solution.py:191
  455.9 269.3 %all-gather.30.cloned.1.call-start = ((), (), s32[]{:S(2)}) async-start(), calls=%async_computation.20 | async-start | bytes 13369344 | tf_op jit(solution)/shard_map/all_gather | solution.py:90
  456.5 370.0 %all-gather.26.cloned.1.call-start = ((), (), s32[]{:S(2)}) async-start(), calls=%async_computation.18 | async-start | bytes 13369344 | tf_op jit(solution)/shard_map/all_gather | solution.py:88
  457.2 443.2 %reduce-scatter.18.cloned.1.call-start = ((), (), s32[]{:S(2)}) async-start(), calls=%async_computation.23 | async-start | bytes 3145728 | tf_op jit(solution)/shard_map/reduce_scatter | solution.py:208
  601.3 225.2 %copy-start.60 = (bf16[2,256,2048]{2,1,0:T(8,128)(2,1)S(1)}, bf16[2,256,2048]{2,1,0:T(8,128)(2,1)}, u32[]{:S(2)}) copy-start(bf16[2,256,2048]{2,1,0:T(8,128)(2,1)} %all-gather.24.cloned.1.call-done) | copy-start | bytes 6291460
  843.5 13.3 copy-start.64
  843.5 13.3 copy-start.65
  856.8 13.6 copy-start.63
  870.3 64.4 %reduce-scatter.16.cloned.1.call-start = ((), (), s32[]{:S(2)}) async-start(), calls=%async_computation.21 | async-start | bytes 3145728 | tf_op jit(solution)/shard_map/reduce_scatter | solution.py:181
  881.1 19.4 copy-start.11
  881.1 53.6 %copy-start.30 = (bf16[2,128,2048]{2,1,0:T(8,128)(2,1)S(1)}, bf16[2,128,2048]{2,1,0:T(8,128)(2,1)}, u32[]{:S(2)}) copy-start(bf16[2,128,2048]{2,1,0:T(8,128)(2,1)} %param.19) | copy-start | bytes 3145732
  881.1 221.2 %reduce-scatter.34.cloned.1.call-start = ((), (), s32[]{:S(2)}) async-start(), calls=%async_computation.31 | async-start | bytes 4718592
  1014.2 179.7 %reduce-scatter.36.cloned.1.call-start = ((), (), s32[]{:S(2)}) async-start(), calls=%async_computation.32 | async-start | bytes 4718592
  1031.5 410.6 %reduce-scatter.32.cloned.1.call-start = ((), (), s32[]{:S(2)}) async-start(), calls=%async_computation.30 | async-start | bytes 26738688 | tf_op jit(solution)/shard_map/reduce_scatter | solution.py:214
  1047.0 57.6 %copy-start.40 = (f32[2,128,128]{2,1,0:T(8,128)S(1)}, f32[2,128,128]{2,1,0:T(8,128)}, u32[]{:S(2)}) copy-start(f32[2,128,128]{2,1,0:T(8,128)} %copy.222) | copy-start | bytes 393220
  1047.0 581.3 %reduce-scatter.22.cloned.1.call-start = ((), (), s32[]{:S(2)}) async-start(), calls=%async_computation.25 | async-start | bytes 8650752 | tf_op jit(solution)/shard_map/reduce_scatter | solution.py:335
  1110.0 4.7 copy-start.21
  1114.7 700.2 %reduce-scatter.24.cloned.1.call-start = ((), (), s32[]{:S(2)}) async-start(), calls=%async_computation.26 | async-start | bytes 8650752 | tf_op jit(solution)/shard_map/reduce_scatter | solution.py:336
  1195.9 4.7 copy-start.23
  1200.6 975.1 %reduce-scatter.26.cloned.1.call-start = ((), (), s32[]{:S(2)}) async-start(), calls=%async_computation.27 | async-start | bytes 17301504 | tf_op jit(solution)/shard_map/reduce_scatter | solution.py:337
  1215.0 1320.7 %reduce-scatter.20.cloned.1.call-start = ((), (), s32[]{:S(2)}) async-start(), calls=%async_computation.24 | async-start | bytes 17301504 | tf_op jit(solution)/shard_map/reduce_scatter | solution.py:334
  1232.5 1551.1 %reduce-scatter.28.cloned.1.call-start = ((), (), s32[]{:S(2)}) async-start(), calls=%async_computation.28 | async-start | bytes 26738688 | tf_op jit(solution)/shard_map/reduce_scatter | solution.py:212
  1247.2 1784.0 %reduce-scatter.30.cloned.1.call-start = ((), (), s32[]{:S(2)}) async-start(), calls=%async_computation.29 | async-start | bytes 26738688 | tf_op jit(solution)/shard_map/reduce_scatter | solution.py:213
  1261.6 6.0 copy-start.22
  1261.6 6.0 copy-start.28
  1270.0 51.0 %copy-start.54 = (f32[2,128]{1,0:T(2,128)S(1)}, f32[2,128]{1,0:T(2,128)}, u32[]{:S(2)}) copy-start(f32[2,128]{1,0:T(2,128)} %copy-done.53) | copy-start | bytes 3076
  1270.0 51.1 %copy-start.16 = (f32[2,128,2048]{2,1,0:T(8,128)S(1)}, f32[2,128,2048]{2,1,0:T(8,128)}, u32[]{:S(2)}) copy-start(f32[2,128,2048]{2,1,0:T(8,128)} %copy-done.14) | copy-start | bytes 6291460
  (46 other events, 83.5 us)
Sparse Core Ops, SparseCore 0:
  11.1 64.8 all-gather.11
  79.1 60.7 all-gather.17
  142.6 71.9 all-gather.13
  217.2 71.6 all-gather.19
  291.7 75.5 all-gather.15
  370.1 75.8 all-gather.21
  454.6 31.6 all-gather.23
  488.6 100.7 all-gather.27
  590.9 31.2 all-gather.31
  624.4 100.7 all-gather.29
  727.5 98.9 all-gather.25
  870.4 29.9 reduce-scatter.17
  902.8 31.8 reduce-scatter.15
  1014.3 87.9 reduce-scatter.33
  1106.2 87.6 reduce-scatter.35
  1197.9 244.2 reduce-scatter.31
  1444.8 183.4 reduce-scatter.21
  1631.0 183.8 reduce-scatter.23
  1817.8 357.7 reduce-scatter.25
  2178.3 357.3 reduce-scatter.19
  2540.4 243.1 reduce-scatter.27
  2788.3 242.8 reduce-scatter.29
where the time goes:
time: 3050 us; the launch traced here: 3040 us
  waiting for transfers between devices  2540 us (83%)
  matrix products  243 us (8%)
  local copies, waits for them, and re-layouts  112 us (4%)
  blocking collectives  88 us (3%)
  other arithmetic  35.4 us (1%)
    reduce_scatter x1, waiting for transfers between devices, shards(): lax.psum_scatter(out_wgrad, ('dp', 'blk', 'fsdp'), scatter_dimension=0, t...  361 us
    reduce_scatter x1, waiting for transfers between devices, shards(): lax.psum_scatter(query_wgrad, ('dp', 'blk', 'fsdp'), scatter_dimension=0,...  360 us
    reduce_scatter x1, waiting for transfers between devices, shards(): lax.psum_scatter(gate_wgrad, ('dp', 'blk'), scatter_dimension=0, tiled=True)  248 us
    reduce_scatter x1, waiting for transfers between devices, shards(): lax.psum_scatter(upward_wgrad, ('dp', 'blk'), scatter_dimension=0, tiled=...  248 us
    reduce_scatter x1, waiting for transfers between devices, shards(): lax.psum_scatter(value_wgrad, ('dp', 'blk', 'fsdp'), scatter_dimension=0,...  187 us
    reduce_scatter x1, waiting for transfers between devices, shards(): lax.psum_scatter(key_wgrad, ('dp', 'blk', 'fsdp'), scatter_dimension=0, t...  183 us
    unnamed x24, waiting for transfers between devices  140 us
    reduce_scatter x1, waiting for transfers between devices, shards(): lax.psum_scatter(down_wgrad, ('dp', 'blk'), scatter_dimension=0, tiled=True)  118 us
  transfers between devices with their start and end apart: 22, of which 22 were waited for; matrix products, arithmetic and copies ran while one was open for 8% of the time, Pallas kernels for 0%

commit v1 on v0

--- a/solution.py
+++ b/solution.py
@@ -1,13 +1,819 @@
+import functools
 import math
 
 import jax
 import jax.numpy as jnp
 from jax import lax
+from jax.experimental import pallas as pl
+from jax.experimental.pallas import tpu as pltpu
 from jax.sharding import PartitionSpec as P
 
 EPSILON = 1e-06
 ROPE_BASE = 1000000.0
 MASKED = -1e30
+BF = jnp.bfloat16
+F32 = jnp.float32
+EVERY = ("dp", "blk", "fsdp")
+
+
+def running_ends(lengths):
+    parts = [lengths[..., :1]]
+    for index in range(1, lengths.shape[-1]):
+        parts.append(parts[-1] + lengths[..., index : index + 1])
+    return jnp.concatenate(parts, axis=-1)
+
+
+SWAP_X = [(0, 2), (2, 0), (1, 3), (3, 1)]
+SWAP_C = [(0, 1), (1, 0), (2, 3), (3, 2)]
+SWAP_Y = [(0, 1), (1, 0)]
+BLOCK = 128
+PIECES = 8
+
+
+def over_x(value):
+    return lax.ppermute(value, "dp", SWAP_X)
+
+
+def over_c(value):
+    return lax.ppermute(value, "dp", SWAP_C)
+
+
+def over_y(value):
+    return lax.ppermute(value, "fsdp", SWAP_Y)
+
+
+def after(value, *before):
+    return lax.optimization_barrier((value, *before))[0]
+
+
+def sum_low(*parts):
+    return functools.reduce(lambda a, b: a + b, [p.astype(F32) for p in parts]).astype(BF)
+
+
+def by_bit(bit, zero, one):
+    return jnp.where(bit == 1, one, zero)
+
+
+def pick(value, index, axis):
+    return lax.dynamic_index_in_dim(value, index, axis, keepdims=False)
+
+
+def flip_where(bit, value, axis):
+    first, second = jnp.split(value, 2, axis)
+    return jnp.where(bit == 1, jnp.concatenate([second, first], axis), value)
+
+
+def together(*values):
+    return lax.optimization_barrier(values)
+
+
+def layer_gather(low, high, core_after=()):
+    low_x, high_y = together(over_x(low), over_y(high))
+    low_row, high_row = together(jnp.concatenate([low, low_x]), jnp.concatenate([high, high_y]))
+    low_both, high_both = together(over_y(low_row), over_x(high_row))
+    near = [low_row, low_both, high_row, high_both]
+    last = [after(piece, *core_after) if core_after else piece for piece in (low_both, high_both)]
+    sent = [low_row, last[0], high_row, last[1]]
+    return near + [over_c(piece) for piece in sent], (low_row, high_row)
+
+
+def layer_scatter(product, core_after=()):
+    sent_low, sent_high = product(1024, 1536), product(1536, 2048)
+    here = product(0, 1024, sent_low, sent_high)
+    far_low, far_high = together(
+        over_c(after(sent_low, *core_after)), over_c(after(sent_high, *core_after))
+    )
+    second = together(sum_low(here[256:512], far_low[256:]), sum_low(here[768:], far_high[256:]))
+    low_back, high_back = together(over_y(second[0]), over_x(second[1]))
+    third = together(
+        sum_low(here[128:256], far_low[128:256], low_back[128:]),
+        sum_low(here[640:768], far_high[128:256], high_back[128:]),
+    )
+    low_last, high_last = together(over_x(third[0]), over_y(third[1]))
+    parts = (
+        (here[:128], far_low[:128], low_back[:128], low_last),
+        (here[512:640], far_high[:128], high_back[:128], high_last),
+    )
+    return parts, here, second, third
+
+
+def product_of(rows, matrix, dims, more=None):
+    def product(first, last, *before):
+        part = rows[first:last]
+        part = after(part, *before) if before else part
+        out = lax.dot_general(part, matrix, dims, preferred_element_type=F32)
+        return (out if more is None else out + more[first].astype(F32)).astype(BF)
+
+    return product
+
+
+def total_of(parts):
+    return functools.reduce(lambda a, b: a + b, [p.astype(F32) for p in parts])
+
+
+def blk_gather(own):
+    return lax.all_gather(own, "blk", axis=0, tiled=True)
+
+
+def blk_scatter(partial):
+    return lax.psum_scatter(partial, "blk", scatter_dimension=0, tiled=True)
+
+
+def swap_z(value, step):
+    return lax.ppermute(value, "blk", [(z, z ^ step) for z in range(4)])
+
+
+def small_gather_z(value, z):
+    for bit, step in ((z % 2, 1), (z // 2, 2)):
+        value = flip_where(bit, jnp.stack([value, swap_z(value, step)]), 0)
+    return value
+
+
+def small_gather(value, coords):
+    x_bit, c_bit, y_bit = coords
+    for bit, move in ((y_bit, over_y), (c_bit, over_c), (x_bit, over_x)):
+        value = flip_where(bit, jnp.stack([value, move(value)]), 0)
+    return value.reshape(2, 2, 2, 4, -1)
+
+
+def small_scatter(value, coords, z):
+    x_bit, c_bit, y_bit = coords
+    value = value.reshape(2, 2, 2, 2, 2, -1)
+    moves = (
+        (z // 2, functools.partial(swap_z, step=2), 2),
+        (z % 2, functools.partial(swap_z, step=1), 2),
+        (x_bit, over_x, 0),
+        (c_bit, over_c, 0),
+        (y_bit, over_y, 0),
+    )
+    for bit, move, axis in moves:
+        value = pick(value, bit, axis) + move(pick(value, 1 - bit, axis))
+    return value
+
+
+def width_blocks(value):
+    step = value.shape[-1] // 16
+    return [value[..., i * step : (i + 1) * step] for i in range(16)]
+
+
+def model_order(value):
+    blocks = width_blocks(value)
+    return jnp.concatenate([blocks[j * 4 + i] for i in range(4) for j in range(4)], axis=-1)
+
+
+def trade(value, bit, move, axis):
+    keep, got = pick(value, bit, axis), move(pick(value, 1 - bit, axis))
+    return by_bit(bit, jnp.stack([keep, got], axis), jnp.stack([got, keep], axis))
+
+
+def join(keep, got, bit, axis):
+    return by_bit(bit, jnp.stack([keep, got], axis), jnp.stack([got, keep], axis))
+
+
+def row_moves():
+    first, second = [], []
+    for d in range(4):
+        for z in range(4):
+            for y in range(2):
+                source = d * 8 + z * 2 + y
+                target = (d // 2) * 2 + z // 2
+                first.append((source, target * 8 + (2 * (d % 2) + z % 2) * 2 + y))
+                second.append((source, target * 8 + (2 * (d % 2) + 1 - z % 2) * 2 + y))
+    return first, second
+
+
+def sort_width(read, write, width):
+    step = width // 16
+    for i in range(4):
+        for j in range(4):
+            write(slice((i * 4 + j) * step, (i * 4 + j + 1) * step), read(slice((j * 4 + i) * step, (j * 4 + i + 1) * step)))
+
+
+def send_rows_kernel(odd_ref, value_ref, first_ref, second_ref):
+    odd = odd_ref[0]
+    for out, at in ((first_ref, odd), (second_ref, 1 - odd)):
+
+        def write(cols, value, out=out):
+            out[:, cols] = value
+
+        sort_width(lambda cols, at=at: value_ref[at, :, cols], write, out.shape[1])
+
+
+def send_rows(value, odd):
+    shape = jax.ShapeDtypeStruct(value.shape[1:], value.dtype)
+    return pl.pallas_call(
+        send_rows_kernel,
+        in_specs=[pl.BlockSpec(memory_space=pltpu.SMEM), pl.BlockSpec(memory_space=pltpu.VMEM)],
+        out_specs=[pl.BlockSpec(memory_space=pltpu.VMEM)] * 2,
+        out_shape=[shape, shape],
+    )(odd.reshape(1), value)
+
+
+def keep_rows_kernel(odd_ref, first_ref, second_ref, out_ref):
+    odd = odd_ref[0]
+    for got, at in ((first_ref, odd), (second_ref, 1 - odd)):
+
+        def write(cols, value, at=at):
+            out_ref[at, :, cols] = value.astype(out_ref.dtype)
+
+        sort_width(lambda cols, got=got: got[:, cols], write, got.shape[1])
+
+
+def keep_rows(first, second, odd, dtype):
+    return pl.pallas_call(
+        keep_rows_kernel,
+        in_specs=[pl.BlockSpec(memory_space=pltpu.SMEM)] + [pl.BlockSpec(memory_space=pltpu.VMEM)] * 2,
+        out_specs=pl.BlockSpec(memory_space=pltpu.VMEM),
+        out_shape=jax.ShapeDtypeStruct((2, *first.shape), dtype),
+    )(odd.reshape(1), first, second)
+
+
+def sort_kernel(value_ref, out_ref):
+    def write(cols, value):
+        out_ref[:, cols] = value.astype(out_ref.dtype)
+
+    sort_width(lambda cols: value_ref[:, cols], write, value_ref.shape[1])
+
+
+def sort_model(value, dtype):
+    return pl.pallas_call(
+        sort_kernel,
+        in_specs=[pl.BlockSpec(memory_space=pltpu.VMEM)],
+        out_specs=pl.BlockSpec(memory_space=pltpu.VMEM),
+        out_shape=jax.ShapeDtypeStruct(value.shape, dtype),
+    )(value)
+
+
+def rows_in(sent, odd):
+    moves = row_moves()
+    got_first = lax.ppermute(sent[0], EVERY, moves[0])
+    got_second = lax.ppermute(sent[1], EVERY, moves[1])
+    return by_bit(odd, got_first, got_second), by_bit(odd, got_second, got_first)
+
+
+def rows_out(low, high, odd, dtype):
+    moves = row_moves()
+    got_first = lax.ppermute(by_bit(odd, low, high), EVERY, [(b, a) for a, b in moves[0]])
+    got_second = lax.ppermute(by_bit(odd, high, low), EVERY, [(b, a) for a, b in moves[1]])
+    return keep_rows(got_first, got_second, odd, dtype)
+
+
+def block_rows(scalars, row, block):
+    c_bit, y_bit = scalars[0], scalars[1]
+    far_c = jnp.where(c_bit == (block >> 2), 0, 1)
+    far_y = jnp.where(y_bit == (block & 1), 0, 1)
+    if (block >> 1) & 1:
+        at = far_c * 8 + 4 + row * 2 + far_y
+    else:
+        at = far_c * 8 + far_y * 2 + row
+    return pl.ds(pl.multiple_of(at * BLOCK, BLOCK), BLOCK)
+
+
+def swap_halves(value):
+    return pltpu.roll(value, value.shape[-1] // 2, 1)
+
+
+def head_forward(raw, gain, cos, sine):
+    inverse = lax.rsqrt(jnp.mean(raw * raw, axis=-1, keepdims=True) + EPSILON)
+    scaled = raw * inverse * gain
+    return scaled * cos + swap_halves(scaled) * sine
+
+
+def head_backward(grad, raw, gain, cos, sine):
+    inverse = lax.rsqrt(jnp.mean(raw * raw, axis=-1, keepdims=True) + EPSILON)
+    unit = raw * inverse
+    back = grad * cos + swap_halves(grad * sine)
+    gain_grad = jnp.sum(back * unit, axis=0, keepdims=True)
+    scaled = back * gain
+    return inverse * (scaled - unit * jnp.mean(scaled * unit, axis=-1, keepdims=True)), gain_grad
+
+
+def visible_pairs(scalars, row, first_query, queries, keys, docs):
+    place = first_query + lax.broadcasted_iota(jnp.int32, (queries, 1), 0)
+    start = jnp.zeros_like(place)
+    for doc in range(docs - 1):
+        end = scalars[2 + row * docs + doc]
+        start = jnp.where(place >= end, end, start)
+    key_place = lax.broadcasted_iota(jnp.int32, (queries, keys), 1)
+    return (key_place >= start) & (key_place <= place)
+
+
+def fetch(pieces, held, sems, base=0):
+    size = held.shape[0] // len(pieces)
+    return [
+        pltpu.make_async_copy(piece, held.at[pl.ds(i * size, size), :], sems.at[base + i])
+        for i, piece in enumerate(pieces)
+    ]
+
+
+def load_row(scalars, row, raw_ref, cos_ref, sine_ref, gain_ref, q_s, k_s, v_s, groups, blocks):
+    width = 128
+    for block in range(blocks):
+        rel = block_rows(scalars, row, block)
+        rows = slice(block * BLOCK, block * BLOCK + BLOCK)
+        cos, sine = cos_ref[0, rows, :], sine_ref[0, rows, :]
+        for g in range(groups):
+            raw = raw_ref[rel, g * width : (g + 1) * width]
+            q_s[rows, g * width : (g + 1) * width] = head_forward(
+                raw, gain_ref[0:1, :], cos, sine
+            ).astype(BF)
+        raw = raw_ref[rel, groups * width : (groups + 1) * width]
+        k_s[rows, :] = head_forward(raw, gain_ref[1:2, :], cos, sine).astype(BF)
+        v_s[rows, :] = raw_ref[rel, (groups + 1) * width : (groups + 2) * width].astype(BF)
+
+
+ROWS_C = (((1,), (1,)), ((), ()))
+COLS_C = (((0,), (0,)), ((), ()))
+
+
+def attend_kernel(scalars, cos_ref, sine_ref, gain_ref, *refs, groups, docs, step):
+    raw_s, mix_ref, q_s, k_s, v_s = refs
+    row = pl.program_id(0)
+    total = k_s.shape[0]
+    load_row(scalars, row, raw_s, cos_ref, sine_ref, gain_ref, q_s, k_s, v_s, groups, total // BLOCK)
+    scale = 1.0 / math.sqrt(128)
+    for first in range(0, total, step):
+        keys = first + step
+        visible = visible_pairs(scalars, row, first, step, keys, docs)
+        for g in range(groups):
+            query = q_s[first : first + step, g * 128 : (g + 1) * 128]
+            scores = lax.dot_general(query, k_s[:keys, :], ROWS_C, preferred_element_type=F32) * scale
+            scores = jnp.where(visible, scores, MASKED)
+            weights = jnp.exp(scores - jnp.max(scores, axis=-1, keepdims=True))
+            norm = jnp.sum(weights, axis=-1, keepdims=True)
+            mixed = jnp.dot(weights.astype(BF), v_s[:keys, :], preferred_element_type=F32) / norm
+            for part in range(step // BLOCK):
+                rel = block_rows(scalars, row, first // BLOCK + part)
+                mix_ref[rel, g * 128 : (g + 1) * 128] = mixed[part * BLOCK : (part + 1) * BLOCK].astype(BF)
+
+
+def attend_back_kernel(scalars, cos_ref, sine_ref, gain_ref, *refs, groups, docs, step):
+    raw_s, dmix_s, draw_ref, dgain_ref, q_s, k_s, v_s, dk_s, dv_s = refs
+    row = pl.program_id(0)
+    total = k_s.shape[0]
+    load_row(scalars, row, raw_s, cos_ref, sine_ref, gain_ref, q_s, k_s, v_s, groups, total // BLOCK)
+    scale = 1.0 / math.sqrt(128)
+    dk_s[...] = jnp.zeros_like(dk_s)
+    dv_s[...] = jnp.zeros_like(dv_s)
+    query_gain = jnp.zeros((1, 128), F32)
+    for first in range(0, total, step):
+        keys = first + step
+        visible = visible_pairs(scalars, row, first, step, keys, docs)
+        order = [block_rows(scalars, row, first // BLOCK + part) for part in range(step // BLOCK)]
+        for g in range(groups):
+            cols = slice(g * 128, (g + 1) * 128)
+            query = q_s[first : first + step, cols]
+            dmix = jnp.concatenate([dmix_s[rel, cols] for rel in order], axis=0)
+            scores = lax.dot_general(query, k_s[:keys, :], ROWS_C, preferred_element_type=F32) * scale
+            scores = jnp.where(visible, scores, MASKED)
+            weights = jnp.exp(scores - jnp.max(scores, axis=-1, keepdims=True))
+            probs = weights / jnp.sum(weights, axis=-1, keepdims=True)
+            dprobs = lax.dot_general(dmix, v_s[:keys, :], ROWS_C, preferred_element_type=F32)
+            delta = jnp.sum(probs * dprobs, axis=-1, keepdims=True)
+            dscores = (probs * (dprobs - delta)).astype(BF)
+            dquery = jnp.dot(dscores, k_s[:keys, :], preferred_element_type=F32) * scale
+            dk_s[:keys, :] += lax.dot_general(dscores, query, COLS_C, preferred_element_type=F32)
+            dv_s[:keys, :] += lax.dot_general(probs.astype(BF), dmix, COLS_C, preferred_element_type=F32)
+            for part, rel in enumerate(order):
+                rows = slice(first + part * BLOCK, first + (part + 1) * BLOCK)
+                draw, gain_part = head_backward(
+                    dquery[part * BLOCK : (part + 1) * BLOCK], raw_s[rel, cols], gain_ref[0:1, :],
+                    cos_ref[0, rows, :], sine_ref[0, rows, :],
+                )
+                draw_ref[rel, cols] = draw.astype(BF)
+                query_gain += gain_part
+    key_gain = jnp.zeros((1, 128), F32)
+    cols = slice(groups * 128, (groups + 1) * 128)
+    for block in range(total // BLOCK):
+        rel = block_rows(scalars, row, block)
+        rows = slice(block * BLOCK, (block + 1) * BLOCK)
+        draw, gain_part = head_backward(
+            dk_s[rows, :] * scale, raw_s[rel, cols], gain_ref[1:2, :], cos_ref[0, rows, :], sine_ref[0, rows, :]
+        )
+        draw_ref[rel, cols] = draw.astype(BF)
+        draw_ref[rel, (groups + 1) * 128 : (groups + 2) * 128] = dv_s[rows, :].astype(BF)
+        key_gain += gain_part
+    dgain_ref[0, :, :] = jnp.concatenate([query_gain, key_gain, jnp.zeros((6, 128), F32)], axis=0)
+
+
+ATTEND_STEP = 256
+
+
+def attend(scalars, raw, cos, sine, gains, groups, docs, dmix=None):
+    total, width = cos.shape[1], raw.shape[1]
+    by_row = pl.BlockSpec((1, total, 128), lambda r, s: (r, 0, 0))
+    back = dmix is not None
+    given = [raw, dmix] if back else [raw]
+    once = lambda columns: pl.BlockSpec((2 * total, columns), lambda r, s: (0, 0))
+    out_specs = [once(width if back else groups * 128)]
+    out_shape = [jax.ShapeDtypeStruct((2 * total, width if back else groups * 128), BF)]
+    if back:
+        out_specs.append(pl.BlockSpec((1, 8, 128), lambda r, s: (r, 0, 0)))
+        out_shape.append(jax.ShapeDtypeStruct((2, 8, 128), F32))
+    scratch = [
+        pltpu.VMEM((total, groups * 128), BF),
+        pltpu.VMEM((total, 128), BF),
+        pltpu.VMEM((total, 128), BF),
+    ]
+    if back:
+        scratch += [pltpu.VMEM((total, 128), F32), pltpu.VMEM((total, 128), F32)]
+    return pl.pallas_call(
+        functools.partial(
+            attend_back_kernel if back else attend_kernel, groups=groups, docs=docs, step=ATTEND_STEP
+        ),
+        grid_spec=pltpu.PrefetchScalarGridSpec(
+            num_scalar_prefetch=1,
+            grid=(2,),
+            in_specs=[by_row, by_row, pl.BlockSpec((8, 128), lambda r, s: (0, 0))]
+            + [once(part.shape[1]) for part in given],
+            out_specs=out_specs,
+            scratch_shapes=scratch,
+        ),
+        out_shape=out_shape,
+        compiler_params=pltpu.CompilerParams(vmem_limit_bytes=40 * 2**20),
+        cost_estimate=pl.CostEstimate(
+            flops=groups * total * total * 128 * 2 * (5 if back else 2) * 2 * 5 // 8,
+            bytes_accessed=(40 if back else 12) * 2**20,
+            transcendentals=groups * total * total * 2,
+        ),
+    )(scalars, cos, sine, gains, *given)
+
+
+def pieces_kernel(matrix_ref, *refs, dims):
+    pieces, (out_ref, whole_ref, held, sems, out_sem) = refs[:PIECES], refs[PIECES:]
+    copies = fetch(pieces, held, sems)
+    for copy in copies:
+        copy.start()
+    size = held.shape[0] // PIECES
+    for at, copy in enumerate(copies):
+        copy.wait()
+        rows = slice(at * size, (at + 1) * size)
+        out_ref[rows, :] = lax.dot_general(
+            held[rows, :], matrix_ref[...], dims, preferred_element_type=F32
+        ).astype(out_ref.dtype)
+    out = pltpu.make_async_copy(held, whole_ref, out_sem)
+    out.start()
+    out.wait()
+
+
+def pieces_dot(pieces, matrix, dims, dtype):
+    rows, width = pieces[0].shape
+    columns = matrix.shape[1 - dims[0][1][0]]
+    vmem, anywhere = pl.BlockSpec(memory_space=pltpu.VMEM), pl.BlockSpec(memory_space=pl.ANY)
+    return pl.pallas_call(
+        functools.partial(pieces_kernel, dims=dims),
+        in_specs=[vmem] + [anywhere] * PIECES,
+        out_specs=[vmem, anywhere],
+        out_shape=[
+            jax.ShapeDtypeStruct((PIECES * rows, columns), dtype),
+            jax.ShapeDtypeStruct((PIECES * rows, width), BF),
+        ],
+        scratch_shapes=[
+            pltpu.VMEM((PIECES * rows, width), BF),
+            pltpu.SemaphoreType.DMA((PIECES,)),
+            pltpu.SemaphoreType.DMA,
+        ],
+        compiler_params=pltpu.CompilerParams(vmem_limit_bytes=32 * 2**20),
+        cost_estimate=pl.CostEstimate(
+            flops=2 * PIECES * rows * width * columns,
+            bytes_accessed=4 * PIECES * rows * width + 4 * PIECES * rows * columns,
+            transcendentals=0,
+        ),
+    )(matrix, *pieces)
+
+
+UNIT_TILE = 256
+TOKEN_TILE = 512
+
+
+def units_kernel(both_ref, down_ref, *refs, given):
+    normed, tops = refs[:given], refs[given : 2 * given]
+    hidden_ref, dboth_ref = refs[2 * given : 2 * given + 2]
+    *wholes, normed_s, top_s, sems, out_sems = refs[2 * given + 2 :]
+    at = pl.program_id(0)
+    last = pl.num_programs(0) - 1
+    size = normed_s.shape[0] // PIECES
+    if given == 1:
+        normed, tops = ([r[0].at[pl.ds(i * size, size), :] for i in range(PIECES)] for r in (normed, tops))
+    copies = fetch(normed, normed_s, sems), fetch(tops, top_s, sems, PIECES)
+    outs = [
+        pltpu.make_async_copy(held, whole, out_sems.at[i])
+        for i, (held, whole) in enumerate(zip((normed_s, top_s), wholes))
+    ]
+
+    @pl.when(at == 0)
+    def _():
+        for one, other in zip(*copies, strict=True):
+            one.start()
+            other.start()
+
+    per = TOKEN_TILE // size
+    for tile in range(normed_s.shape[0] // TOKEN_TILE):
+
+        @pl.when(at == 0)
+        def _(tile=tile):
+            for piece in range(tile * per, (tile + 1) * per):
+                copies[0][piece].wait()
+                copies[1][piece].wait()
+
+        rows = slice(tile * TOKEN_TILE, (tile + 1) * TOKEN_TILE)
+        both = jnp.dot(normed_s[rows, :], both_ref[...], preferred_element_type=F32)
+        gate, upward = both[:, :UNIT_TILE], both[:, UNIT_TILE:]
+        dhidden = jnp.dot(top_s[rows, :], down_ref[...], preferred_element_type=F32)
+        logistic = 1.0 / (1.0 + jnp.exp(-gate))
+        swish = gate * logistic
+        hidden_ref[rows, :] = (swish * upward).astype(BF)
+        dgate = dhidden * upward * (logistic * (1.0 + gate * (1.0 - logistic)))
+        dboth_ref[rows, :UNIT_TILE] = dgate.astype(BF)
+        dboth_ref[rows, UNIT_TILE:] = (dhidden * swish).astype(BF)
+
+    if outs:
+
+        @pl.when(at == 0)
+        def _():
+            for out in outs:
+                out.start()
+
+        @pl.when(at == last)
+        def _():
+            for out in outs:
+                out.wait()
+
+
+def units_pass(normed, tops, mat):
+    given = len(normed)
+    width, units = mat.shape[0], mat.shape[1] // 3
+    tiles = units // UNIT_TILE
+    tokens = given * normed[0].shape[0]
+    anywhere = pl.BlockSpec(memory_space=pl.ANY)
+    whole = jax.ShapeDtypeStruct((tokens, width), BF)
+    wholes = 0 if given == 1 else 2
+    return pl.pallas_call(
+        functools.partial(units_kernel, given=given),
+        grid=(tiles,),
+        in_specs=[
+            pl.BlockSpec((width, 2 * UNIT_TILE), lambda i: (0, i)),
+            pl.BlockSpec((width, UNIT_TILE), lambda i: (0, 2 * tiles + i)),
+        ]
+        + [anywhere] * (2 * given),
+        out_specs=[
+            pl.BlockSpec((tokens, UNIT_TILE), lambda i: (0, i)),
+            pl.BlockSpec((tokens, 2 * UNIT_TILE), lambda i: (0, i)),
+        ]
+        + [anywhere] * wholes,
+        out_shape=[
+            jax.ShapeDtypeStruct((tokens, units), BF),
+            jax.ShapeDtypeStruct((tokens, 2 * units), BF),
+        ]
+        + [whole] * wholes,
+        scratch_shapes=[
+            pltpu.VMEM((tokens, width), BF),
+            pltpu.VMEM((tokens, width), BF),
+            pltpu.SemaphoreType.DMA((2 * PIECES,)),
+            pltpu.SemaphoreType.DMA((2,)),
+        ],
+        compiler_params=pltpu.CompilerParams(vmem_limit_bytes=48 * 2**20),
+        cost_estimate=pl.CostEstimate(
+            flops=2 * tokens * width * units * 3,
+            bytes_accessed=4 * tokens * width * 2 + 6 * width * units + 6 * tokens * units,
+            transcendentals=tokens * units,
+        ),
+    )(mat, mat, *normed, *tops)
+
+
+def norm_inverse(values):
+    return lax.rsqrt(jnp.mean(values * values, axis=-1, keepdims=True) + EPSILON)
+
+
+def norm_back(grad, unit, inverse, gain):
+    scaled = grad * gain
+    return inverse * (scaled - unit * jnp.mean(scaled * unit, axis=-1, keepdims=True))
+
+
+def wgrad(rows, columns):
+    return lax.dot_general(rows, columns, COLS_C, preferred_element_type=F32).astype(BF)
+
+
+CHUNKS = ((0, 2), (2, 3))
+
+
+def layer_shards(
+    hidden_in, out_grad, doc_lengths, norm_attn, query_gain, key_gain, query_weight, key_weight,
+    value_weight, output_weight, norm_mlp, gate_weight, upward_weight, down_weight,
+):
+    d, z, y = lax.axis_index("dp"), lax.axis_index("blk"), lax.axis_index("fsdp")
+    x_bit, c_bit, odd = d // 2, d % 2, z % 2
+    coords = (x_bit, c_bit, y)
+    width = hidden_in.shape[-1]
+    docs = doc_lengths.shape[1]
+    head = query_gain.shape[0] * 32
+    groups = query_weight.shape[1] // key_weight.shape[1]
+    total = hidden_in.shape[1] * 8
+    hidden_units = gate_weight.shape[1]
+    share = width // 32
+    transposed = (((1,), (1,)), ((), ()))
+    plain = (((1,), (0,)), ((), ()))
+
+    small = jnp.concatenate(
+        [v.astype(F32) for v in (norm_attn, norm_mlp, query_gain, key_gain)]
+        + [doc_lengths.astype(F32).reshape(-1)]
+    )
+    small_z = small_gather_z(small, z)
+    tokens = rows_in(send_rows(after(hidden_in, small_z), odd), odd)
+    small_all = small_gather(small_z, coords)
+    top_own = rows_in(send_rows(after(out_grad, *tokens), odd), odd)
+
+    pieces = jnp.concatenate(
+        [w.reshape(share, 8, -1) for w in (query_weight, key_weight, value_weight)], axis=-1
+    )
+    pieces = jnp.transpose(pieces, (1, 0, 2)).reshape(2, 2, 2, share, -1)
+    pieces = trade(pieces, x_bit, over_x, 0)
+    pieces = trade(pieces, y, over_y, 2)
+    qkv_own = trade(pieces, c_bit, over_c, 1)
+
+    n_attn, n_head = norm_attn.shape[0], query_gain.shape[0]
+    by_device = jnp.transpose(small_all, (0, 1, 3, 2, 4)).reshape(32, -1)
+    by_blk = jnp.transpose(small_all, (3, 0, 1, 2, 4)).reshape(32, -1)
+    gain_attn = by_blk[:, :n_attn].reshape(-1)
+    gain_mlp = by_blk[:, n_attn : 2 * n_attn].reshape(-1)
+    gain_query = by_device[:, 2 * n_attn : 2 * n_attn + n_head].reshape(-1)
+    gain_key = by_device[:, 2 * n_attn + n_head : 2 * n_attn + 2 * n_head].reshape(-1)
+    lengths = by_device[::8, 2 * n_attn + 2 * n_head :].astype(jnp.int32).reshape(4, 2, docs)
+    ends_all = running_ends(lengths)
+    ends = jnp.stack(
+        [ends_all[(x_bit ^ dx) * 2 + z // 2, odd] for dx in range(2)]
+    )
+    place = jnp.arange(total, dtype=jnp.int32)
+    start = jnp.zeros((2, total), jnp.int32)
+    for doc in range(docs - 1):
+        start = jnp.where(place[None] >= ends[:, doc : doc + 1], ends[:, doc : doc + 1], start)
+    frequency = jnp.exp(
+        jnp.arange(head // 2, dtype=F32) * (-2.0 / head) * math.log(ROPE_BASE)
+    )
+    angles = (place[None] - start).astype(F32)[..., None] * frequency
+    cos_half, sine_half = jnp.cos(angles), jnp.sin(angles)
+    cos_table = jnp.concatenate([cos_half, cos_half], axis=-1)
+    sine_table = jnp.concatenate([-sine_half, sine_half], axis=-1)
+    scalars = jnp.concatenate([jnp.stack([c_bit, y]), ends.reshape(-1)]).astype(jnp.int32)
+    head_gains = jnp.concatenate(
+        [gain_query[None], gain_key[None], jnp.zeros((6, head), F32)], axis=0
+    )
+
+    quarter = hidden_units // 4
+    by_quarter = [w.reshape(-1, 4, quarter // UNIT_TILE, UNIT_TILE) for w in (gate_weight, upward_weight, down_weight)]
+    weight_pieces = []
+    for first, last in CHUNKS:
+        gates, upwards, downs = (w[:, :, first:last] for w in by_quarter)
+        piece = jnp.concatenate(
+            [jnp.stack([gates, upwards], axis=3).reshape(*gates.shape[:2], -1), downs.reshape(*gates.shape[:2], -1)],
+            axis=-1,
+        )
+        weight_pieces.append(jnp.transpose(piece, (1, 0, 2)).reshape(2, 2, piece.shape[0], -1))
+
+    def layer_weights(piece, *before):
+        half = over_x(after(pick(piece, 1 - x_bit, 0), *before))
+        half = join(pick(piece, x_bit, 0), half, x_bit, 0)
+        return trade(half, c_bit, over_c, 1).reshape(width // 4, -1)
+
+    owns = [layer_weights(weight_pieces[0], qkv_own, small_all)]
+    qkv_own = after(qkv_own, *top_own)
+    qkv_mat = blk_gather(qkv_own.reshape(8 * share, -1))
+    out_all = blk_gather(after(output_weight, qkv_own)).reshape(2, 2, share, width)
+
+    tokens = [after(t, small_all, owns[0]) for t in tokens]
+    layer_in = [t.astype(F32) for t in tokens]
+    inverse_attn = [norm_inverse(t) for t in layer_in]
+    unit_attn = [t * i for t, i in zip(layer_in, inverse_attn, strict=True)]
+    normed1, _ = layer_gather(*[(u * gain_attn).astype(BF) for u in unit_attn])
+    owns += [layer_weights(piece, normed1[1], normed1[3]) for piece in weight_pieces[1:]]
+    mats = [blk_gather(after(own, qkv_own)) for own in owns]
+    tops, top_rows = layer_gather(*[after(t, normed1[1], normed1[3]) for t in top_own])
+    raw, normed1_all = pieces_dot(normed1, after(qkv_mat, owns[1], *top_rows), plain, F32)
+    raw = after(raw, tops[1], tops[3])
+    out_all = trade(out_all, y, over_y, 0)
+    out_mat = sort_model(jnp.swapaxes(out_all, 0, 1).reshape(-1, width), BF)
+    (mix,) = attend(scalars, raw, cos_table, sine_table, head_gains, groups, docs)
+    mixed, *_ = layer_scatter(product_of(mix, out_mat, plain))
+    residual = [t + total_of(parts) for t, parts in zip(layer_in, mixed, strict=True)]
+    inverse_mlp = [norm_inverse(t) for t in residual]
+    unit_mlp = [t * i for t, i in zip(residual, inverse_mlp, strict=True)]
+    normed2, _ = layer_gather(*[after((u * gain_mlp).astype(BF), *tops) for u in unit_mlp])
+
+    hiddens, dboths, boths, downs, down_wgrads, both_wgrads = [], [], [], [], [], []
+    dnormed2_part = mlp_part = None
+    normed2_all = top_all = None
+    for (first, last), mat in zip(CHUNKS, mats, strict=True):
+        units = (last - first) * UNIT_TILE
+        boths.append(mat[:, : 2 * units])
+        downs.append(mat[:, 2 * units :])
+        if normed2_all is None:
+            hidden, dboth, normed2_all, top_all = units_pass(normed2, tops, mat)
+        else:
+            normed2_all = after(normed2_all, *down_wgrads, *both_wgrads, *dnormed2_part.values())
+            hidden, dboth = units_pass([normed2_all], [top_all], mat)
+        hiddens.append(hidden)
+        dboths.append(dboth)
+        if last != CHUNKS[-1][1]:
+            both_wgrads.append(wgrad(normed2_all, dboth))
+            down_wgrads.append(wgrad(top_all, after(hidden, both_wgrads[-1])))
+            part = product_of(after(dboth, down_wgrads[-1]), boths[-1], transposed, dnormed2_part)
+            dnormed2_part = {1024: part(1024, 1536), 1536: part(1536, 2048), 0: part(0, 1024)}
+    dnormed2, here, second, third = layer_scatter(
+        product_of(dboths[-1], boths[-1], transposed, dnormed2_part)
+    )
+    dnormed2 = [total_of(parts) for parts in dnormed2]
+    both_wgrads.append(wgrad(after(normed2_all, here), dboths[-1]))
+    down_wgrads.append(wgrad(top_all, after(hiddens[-1], *second)))
+
+    gain_mlp_grad = sum(jnp.sum(g * u, axis=0) for g, u in zip(dnormed2, unit_mlp, strict=True))
+    dresidual = [
+        t.astype(F32) + norm_back(g, u, i, gain_mlp)
+        for t, g, u, i in zip(top_own, dnormed2, unit_mlp, inverse_mlp, strict=True)
+    ]
+    both_last, down_last = both_wgrads[-1], down_wgrads[-1]
+    both_wgrads = [blk_scatter(part) for part in both_wgrads]
+    down_wgrads = [blk_scatter(part) for part in down_wgrads]
+    for hidden, down in zip(hiddens[:-1], downs[:-1], strict=True):
+        part = product_of(after(hidden, *second), down, transposed, mlp_part)
+        mlp_part = {1024: part(1024, 1536), 1536: part(1536, 2048), 0: part(0, 1024)}
+    mlp_product = product_of(after(hiddens[-1], *third), downs[-1], transposed, mlp_part)
+    mlp_product = {first: mlp_product(first, last) for first, last in ((1024, 1536), (1536, 2048), (0, 1024))}
+    dres, _ = layer_gather(
+        *[after(t.astype(BF), both_last, down_last) for t in dresidual], (*mlp_product.values(),)
+    )
+    mlp_out, _, second, _ = layer_scatter(lambda first, *_: mlp_product[first], (dres[1], dres[3]))
+    layer_out = [(t + total_of(parts)).astype(BF) for t, parts in zip(residual, mlp_out, strict=True)]
+    dmix, dres_all = pieces_dot(dres, out_mat, transposed, BF)
+    dmix = after(dmix, *second, *both_wgrads[:-1], *down_wgrads[:-1])
+    draw, dgains = attend(scalars, raw, cos_table, sine_table, head_gains, groups, docs, dmix)
+    dnormed1, here, second, third = layer_scatter(product_of(draw, qkv_mat, transposed))
+    dnormed1 = [total_of(parts) for parts in dnormed1]
+    qkv_wgrad = wgrad(normed1_all, after(draw, here))
+    out_wgrad = wgrad(mix, after(dres_all, *second))
+    out_wgrad = trade(out_wgrad.reshape(2, 2, share, width), y, over_y, 1)
+    out_wgrad = jnp.swapaxes(out_wgrad, 0, 1).reshape(4 * share, width)
+    qkv_wgrad = blk_scatter(after(qkv_wgrad, *both_wgrads, *down_wgrads))
+    out_wgrad = blk_scatter(after(out_wgrad, *both_wgrads, *down_wgrads))
+    out_wgrad = sort_model(out_wgrad, F32)
+    layer_out = rows_out(*[after(t, *third) for t in layer_out], odd, BF)
+
+    swapped = []
+    for own in (*both_wgrads, *down_wgrads):
+        own = after(own, *third).reshape(2, 2, width // 16, -1)
+        own = trade(trade(own, c_bit, over_c, 1), x_bit, over_x, 0)
+        swapped.append(own.reshape(4, width // 16, -1))
+    gate_parts, upward_parts, down_parts = [], [], []
+    for q in range(4):
+        for at, (first, last) in enumerate(CHUNKS):
+            for tile in range(last - first):
+                cut = lambda i: slice(i * UNIT_TILE, (i + 1) * UNIT_TILE)
+                gate_parts.append(swapped[at][q][:, cut(2 * tile)])
+                upward_parts.append(swapped[at][q][:, cut(2 * tile + 1)])
+                down_parts.append(swapped[len(CHUNKS) + at][q][:, cut(tile)])
+    gate_wgrad, upward_wgrad, down_wgrad = (
+        jnp.concatenate(parts, axis=1).astype(F32) for parts in (gate_parts, upward_parts, down_parts)
+    )
+    qkv_wgrad = qkv_wgrad.reshape(2, 2, 2, share, -1)
+    qkv_wgrad = trade(trade(trade(qkv_wgrad, c_bit, over_c, 1), y, over_y, 2), x_bit, over_x, 0)
+    qkv_wgrad = qkv_wgrad.reshape(8, share, -1)
+    q_cols = groups * head
+    query_wgrad = jnp.concatenate([qkv_wgrad[i][:, :q_cols] for i in range(8)], axis=1).astype(F32)
+    key_wgrad = jnp.concatenate([qkv_wgrad[i][:, q_cols : q_cols + head] for i in range(8)], axis=1).astype(F32)
+    value_wgrad = jnp.concatenate([qkv_wgrad[i][:, q_cols + head :] for i in range(8)], axis=1).astype(F32)
+
+    gain_attn_grad = sum(jnp.sum(g * u, axis=0) for g, u in zip(dnormed1, unit_attn, strict=True))
+    input_grad = [
+        t + norm_back(g, u, i, gain_attn)
+        for t, g, u, i in zip(dresidual, dnormed1, unit_attn, inverse_attn, strict=True)
+    ]
+    input_grad = rows_out(*[t.astype(BF) for t in input_grad], odd, F32)
+
+    dgains = jnp.sum(dgains, axis=0)
+    small_grads = jnp.concatenate(
+        [
+            model_order(gain_attn_grad).reshape(32, -1),
+            model_order(gain_mlp_grad).reshape(32, -1),
+            dgains[0].reshape(32, -1),
+            dgains[1].reshape(32, -1),
+        ],
+        axis=1,
+    )
+    small_grads = small_scatter(small_grads, coords, z)
+    return (
+        layer_out,
+        input_grad,
+        small_grads[:n_attn],
+        small_grads[2 * n_attn : 2 * n_attn + n_head],
+        small_grads[2 * n_attn + n_head :],
+        query_wgrad,
+        key_wgrad,
+        value_wgrad,
+        out_wgrad,
+        small_grads[n_attn : 2 * n_attn],
+        gate_wgrad,
+        upward_wgrad,
+        down_wgrad,
+    )
 
 
 def normalize(values, gain):
@@ -23,7 +829,7 @@
 
 def placement_of(lengths, offset, total):
     places = offset + jnp.arange(total, dtype=jnp.int32)
-    ends = jnp.cumsum(lengths, axis=1)
+    ends = running_ends(lengths)
     before = (ends[:, None, :] <= places[None, :, None]).astype(jnp.int32)
     document = jnp.sum(before, axis=2)
     doc_start = jnp.sum(before * lengths[:, None, :], axis=2)
@@ -358,8 +1164,10 @@
 
 
 def solution(mesh):
+    sizes = dict(mesh.shape)
+    layered = (sizes["dp"], sizes["blk"], sizes["fsdp"]) == (4, 4, 2)
     return jax.shard_map(
-        shards,
+        layer_shards if layered else shards,
         mesh=mesh,
         in_specs=(
             P("dp", ("blk", "fsdp"), None),

time: 3050 us -> 728 us (0.24)
  waiting for transfers between devices: 2540 us -> 252 us
  matrix products: 243 us -> 104 us
  Pallas kernels: 0 us -> 102 us
  starting transfers between devices: 1.52 us -> 100 us
  blocking collectives: 88 us -> 0 us
  local copies, waits for them, and re-layouts: 112 us -> 49.6 us
  other arithmetic: 35.4 us -> 92.1 us
    reduce_scatter x9 -> x6, waiting for transfers between devices: 1750 us -> 2.49 us  [blk_scatter(): return lax.psum_scatter(partial, 'blk', scatter_dimension=0, tiled=True)]
    all_gather x11 -> x4, waiting for transfers between devices: 648 us -> 2.1 us  [blk_gather(): return lax.all_gather(own, 'blk', axis=0, tiled=True)]
    ppermute x0 -> x94, waiting for transfers between devices: none -> 247 us  [the longest x22 136 us: over_y(): return lax.ppermute(value, 'fsdp', SWAP_Y)]
    unnamed x24 -> x10, waiting for transfers between devices: 140 us -> 0.67 us
    dot_general x34 -> x24, matrix products: 237 us -> 104 us  [the longest x18 55.8 us: product(): out = lax.dot_general(part, matrix, dims, preferred_element_type=F32)]
    pallas_call x0 -> x12, Pallas kernels: none -> 102 us  [the longest x2 39.5 us: units_pass(): pl.pallas_call(functools.partial(units_kernel, given=given), grid=(tiles,...]
    ppermute x0 -> x94, starting transfers between devices: none -> 98.8 us  [the longest x26 26.6 us: over_x(): return lax.ppermute(value, 'dp', SWAP_X)]
    unnamed x2 -> x0, blocking collectives: 88 us -> none
  transfers between devices with their start and end apart: 22 -> 104, of which waited for: 22 -> 49; matrix products, arithmetic and copies ran while one was open for 8% -> 31% of each run, Pallas kernels for 0% -> 14%
where the time goes in v1:
time: 728 us; the launch traced here: 718 us
  waiting for transfers between devices  252 us (35%)
  matrix products  104 us (14%)
  Pallas kernels  102 us (14%)
  starting transfers between devices  100 us (14%)
  other arithmetic  92.1 us (13%)
  local copies, waits for them, and re-layouts  49.6 us (7%)
  between operations  16.9 us (2%)
    ppermute x22, waiting for transfers between devices, over_y(): return lax.ppermute(value, 'fsdp', SWAP_Y)  136 us
    ppermute x26, waiting for transfers between devices, over_x(): return lax.ppermute(value, 'dp', SWAP_X)  68.1 us
    dot_general x18, matrix products, product(): out = lax.dot_general(part, matrix, dims, preferred_element_type=F32)  55.8 us
    dot_general x6, matrix products, wgrad(): lax.dot_general(rows, columns, COLS_C, preferred_element_type=F32)  48.7 us
    pallas_call x2, Pallas kernels, units_pass(): pl.pallas_call(functools.partial(units_kernel, given=given), grid=(tiles,...  39.5 us
    pallas_call x2, Pallas kernels, attend(): pl.pallas_call(functools.partial(attend_back_kernel if back else attend_k...  31.8 us
    select_n x25, other arithmetic, by_bit(): return jnp.where(bit == 1, one, zero)  27.6 us
    ppermute x26, starting transfers between devices, over_x(): return lax.ppermute(value, 'dp', SWAP_X)  26.6 us
  transfers between devices with their start and end apart: 104, of which 49 were waited for; matrix products, arithmetic and copies ran while one was open for 31% of the time, Pallas kernels for 14%

profile of v1, /device:TPU:0, one launch (start us, length us, event | category | flops | bytes accessed | tf_op | source)
XLA Modules:
  0.0 717.9 jit_solution(11128132309781145908)
XLA Ops:
  32.4 5.3 collective-permute-start.2
  40.2 6.4 collective-permute-done.8
  62.0 5.3 collective-permute-start.13
  67.4 5.4 collective-permute-done.10
  86.4 5.3 collective-permute-done.15
  96.7 5.7 fusion.56
  102.4 12.5 %collective-permute-done.16.refs_1_ = bf16[256,2048]{1,0:T(8,128)(2,1)} collective-permute-done((bf16[256,2048]{1,0:T(8,128)(2,1)S(1)}, bf16[256,2048]{1,0:T(8,128)(2,1)}, u32[]{:S(2)}, u32[]{:S(2)}) %collective-permute-start.16) | collective-permute-done | bytes 1048608 | tf_op jit(solution)/shard_map/ppermute | solution.py:42
  122.1 12.7 %collective-permute-start.22 = (bf16[256,2048]{1,0:T(8,128)(2,1)S(1)}, bf16[256,2048]{1,0:T(8,128)(2,1)}, u32[]{:S(2)}, u32[]{:S(2)}) collective-permute-start(bf16[256,2048]{1,0:T(8,128)(2,1)S(1)} %pad_maximum_fusion.4.refs_0_), channel_id=1, source_target_pairs={{0,8},{8,0},{16,24},{24,16},{1,9},{9,1},{17,25},{25,17},{2,10},{10... | collective-permute-start | bytes 3145736 | tf_op jit(solution)/shard_map/ppermute | solution.py:38
  141.7 7.3 %collective-permute-done.20 = bf16[128,2048]{1,0:T(8,128)(2,1)} collective-permute-done((bf16[128,2048]{1,0:T(8,128)(2,1)}, bf16[128,2048]{1,0:T(8,128)(2,1)}, u32[]{:S(2)}, u32[]{:S(2)}) %collective-permute-start.20) | collective-permute-done | bytes 524320 | tf_op jit(solution)/shard_map/ppermute | solution.py:34
  173.9 9.5 %shard_map.239 = (f32[2048,512]{1,0:T(8,128)S(1)}, bf16[2048,2048]{1,0:T(8,128)(2,1)}) custom-call(bf16[2048,512]{1,0:T(8,128)(2,1)S(1)} %copy-done.14, bf16[256,2048]{1,0:T(8,128)(2,1)S(1)} %pad_maximum_fusion.4.refs_0_, bf16[256,2048]{1,0:T(8,128)(2,1)} %collective-permute-done.16.refs_1_, bf16[256,2048]{1,0:T(8,128)(2,1)S(1)} %copy-done.11, ...), custom_call_target="tpu_custom_call" | custom-call | flops 4294967296 | bytes 20971520 | tf_op jit(solution)/shard_map/pallas_call | solution.py:463
  185.1 11.1 %shard_map.240 = bf16[2048,256]{1,0:T(8,128)(2,1)S(1)} custom-call(s32[10]{0:T(128)S(1)} %pad_add_fusion.2.scalars, f32[2,1024,128]{2,1,0:T(8,128)S(1)} %get-tuple-element.467.cos_ref, f32[2,1024,128]{2,1,0:T(8,128)S(1)} %get-tuple-element.468.sine_ref, f32[8,128]{1,0:T(8,128)S(1)} %maximum_maximum_fusion.gain_ref, f32[2048,512]{1,0:T(8,128)S(1)} %get-tuple-element.163.refs_0_), custom_call_target="tpu_custom_call" | custom-call | flops 1342177280 | bytes 12582912 | tf_op jit(solution)/shard_map/pallas_call | solution.py:420
  207.5 23.6 %collective-permute-done.31 = bf16[256,2048]{1,0:T(8,128)(2,1)S(1)} collective-permute-done((bf16[256,2048]{1,0:T(8,128)(2,1)S(1)}, bf16[256,2048]{1,0:T(8,128)(2,1)S(1)}, u32[]{:S(2)}, u32[]{:S(2)}) %collective-permute-start.31) | collective-permute-done | bytes 1048608 | tf_op jit(solution)/shard_map/ppermute | solution.py:42
  236.2 10.1 %collective-permute-done.33 = bf16[128,2048]{1,0:T(8,128)(2,1)} collective-permute-done((bf16[128,2048]{1,0:T(8,128)(2,1)}, bf16[128,2048]{1,0:T(8,128)(2,1)}, u32[]{:S(2)}, u32[]{:S(2)}) %collective-permute-start.33) | collective-permute-done | bytes 524320 | tf_op jit(solution)/shard_map/ppermute | solution.py:34
  252.8 11.2 %collective-permute-done.39 = bf16[128,2048]{1,0:T(8,128)(2,1)S(1)} collective-permute-done((bf16[128,2048]{1,0:T(8,128)(2,1)S(1)}, bf16[128,2048]{1,0:T(8,128)(2,1)S(1)}, u32[]{:S(2)}, u32[]{:S(2)}) %collective-permute-start.39) | collective-permute-done | bytes 524320 | tf_op jit(solution)/shard_map/ppermute | solution.py:34
  268.0 21.1 %collective-permute-done.41.refs_1_ = bf16[256,2048]{1,0:T(8,128)(2,1)} collective-permute-done((bf16[256,2048]{1,0:T(8,128)(2,1)S(1)}, bf16[256,2048]{1,0:T(8,128)(2,1)}, u32[]{:S(2)}, u32[]{:S(2)}) %collective-permute-start.41) | collective-permute-done | bytes 1048608 | tf_op jit(solution)/shard_map/ppermute | solution.py:42
  294.7 25.1 %shard_map.242 = (bf16[2048,512]{1,0:T(8,128)(2,1)}, bf16[2048,1024]{1,0:T(8,128)(2,1)}, bf16[2048,2048]{1,0:T(8,128)(2,1)}, bf16[2048,2048]{1,0:T(8,128)(2,1)}) custom-call(bf16[2048,1536]{1,0:T(8,128)(2,1)} %all-gather.11.cloned.1.call-done.both_ref.down_ref, bf16[2048,1536]{1,0:T(8,128)(2,1)} %all-gather.11.cloned.1.call-done.both_ref.down_ref, ...), custom_call_target="tpu_custom_call" | custom-call | flops 12884901888 | bytes 46137344 | tf_op jit(solution)/shard_map/pallas_call | solution.py:551
  319.9 14.1 %convolution_convert_fusion.3 = bf16[2048,1024]{1,0:T(8,128)(2,1)} fusion(bf16[2048,2048]{1,0:T(8,128)(2,1)} %get-tuple-element.207.refs_0_, bf16[2048,1024]{1,0:T(8,128)(2,1)} %get-tuple-element.191), kind=kOutput, calls=%fused_computation.9 | convolution fusion | flops 8592031744 | bytes 16777216 | tf_op jit(solution)/shard_map/dot_general | solution.py:594
  334.0 9.9 %convolution_convert_fusion.12 = bf16[2048,512]{1,0:T(8,128)(2,1)} fusion(bf16[2048,2048]{1,0:T(8,128)(2,1)} %get-tuple-element.187.refs_1_, bf16[2048,512]{1,0:T(8,128)(2,1)S(1)} %copy-done.97), kind=kOutput, calls=%fused_computation.25 | convolution fusion | flops 4296015872 | bytes 12582912 | tf_op jit(solution)/shard_map/dot_general | solution.py:594
  344.6 6.4 fusion.8
  350.9 6.1 fusion.5
  357.0 6.3 convolution_convert_fusion.2
  363.4 14.3 %shard_map.243 = (bf16[2048,256]{1,0:T(8,128)(2,1)S(1)}, bf16[2048,512]{1,0:T(8,128)(2,1)S(1)}) custom-call(bf16[2048,768]{1,0:T(8,128)(2,1)} %all-gather.9.cloned.1.call-done.both_ref.down_ref, bf16[2048,768]{1,0:T(8,128)(2,1)} %all-gather.9.cloned.1.call-done.both_ref.down_ref, bf16[2048,2048]{1,0:T(8,128)(2,1)} %get-tuple-element.207.refs_0_, ...), custom_call_target="tpu_custom_call" | custom-call | flops 6442450944 | bytes 39845888 | tf_op jit(solution)/shard_map/pallas_call | solution.py:551
  381.7 4.7 add_convert_fusion.1
  391.9 6.0 convolution_convert_fusion.10
  397.9 17.8 %collective-permute-done.49 = bf16[256,2048]{1,0:T(8,128)(2,1)} collective-permute-done((bf16[256,2048]{1,0:T(8,128)(2,1)}, bf16[256,2048]{1,0:T(8,128)(2,1)}, u32[]{:S(2)}, u32[]{:S(2)}) %collective-permute-start.49) | collective-permute-done | bytes 1048608 | tf_op jit(solution)/shard_map/ppermute | solution.py:42
  421.5 7.0 convolution_convert_fusion.14
  428.5 4.1 collective-permute-done.51
  433.2 3.5 multiply_reduce_fusion
  436.8 3.6 fusion.80
  446.3 6.0 collective-permute-done.53
  464.8 12.6 %collective-permute-done.55.refs_1_ = bf16[256,2048]{1,0:T(8,128)(2,1)} collective-permute-done((bf16[256,2048]{1,0:T(8,128)(2,1)S(1)}, bf16[256,2048]{1,0:T(8,128)(2,1)}, u32[]{:S(2)}, u32[]{:S(2)}) %collective-permute-start.55) | collective-permute-done | bytes 1048608 | tf_op jit(solution)/shard_map/ppermute | solution.py:42
  478.9 4.0 fusion.14
  493.4 7.2 shard_map.244
  503.8 4.2 add_convert_fusion.8
  513.1 20.7 %shard_map.245 = (bf16[2048,512]{1,0:T(8,128)(2,1)S(1)}, f32[2,8,128]{2,1,0:T(8,128)S(1)}) custom-call(s32[10]{0:T(128)S(1)} %pad_add_fusion.2.scalars, f32[2,1024,128]{2,1,0:T(8,128)S(1)} %copy-done.5, f32[2,1024,128]{2,1,0:T(8,128)S(1)} %copy-done.7, f32[8,128]{1,0:T(8,128)S(1)} %maximum_maximum_fusion.gain_ref, f32[2048,512]{1,0:T(8,128)S(1)} %copy-done.19, ...), custom_call_target="tpu_custom_call" | custom-call | flops 3355443200 | bytes 41943040 | tf_op jit(solution)/shard_map/pallas_call | solution.py:420
  540.7 4.4 convolution_convert_fusion
  545.6 5.8 convolution_convert_fusion.6
  554.2 3.6 add_convert_fusion.18
  562.4 9.1 %collective-permute-done.61 = bf16[128,2048]{1,0:T(8,128)(2,1)S(1)} collective-permute-done((bf16[128,2048]{1,0:T(8,128)(2,1)}, bf16[128,2048]{1,0:T(8,128)(2,1)S(1)}, u32[]{:S(2)}, u32[]{:S(2)}) %collective-permute-start.61) | collective-permute-done | bytes 524320 | tf_op jit(solution)/shard_map/ppermute | solution.py:34
  572.7 5.0 add_convert_fusion.6
  579.9 5.9 convolution_convert_fusion.13
  590.8 22.1 %collective-permute-done.85 = bf16[2,64,2048]{2,1,0:T(8,128)(2,1)S(1)} collective-permute-done((bf16[2,64,2048]{2,1,0:T(8,128)(2,1)S(1)}, bf16[2,64,2048]{2,1,0:T(8,128)(2,1)S(1)}, u32[]{:S(2)}, u32[]{:S(2)}) %collective-permute-start.85) | collective-permute-done | bytes 524320 | tf_op jit(solution)/shard_map/ppermute | solution.py:42
  627.1 3.9 collective-permute-done.93
  630.9 5.3 collective-permute-start.71
  642.9 4.0 broadcast_select_fusion
  653.7 15.0 %collective-permute-done.77 = f32[2,2,2,2,136]{4,3,2,1,0:T(2,128)S(1)} collective-permute-done((f32[2,2,2,2,136]{4,3,2,1,0:T(2,128)S(1)}, f32[2,2,2,2,136]{4,3,2,1,0:T(2,128)S(1)}, u32[]{:S(2)}, u32[]{:S(2)}) %collective-permute-start.77) | collective-permute-done | bytes 8736 | tf_op jit(solution)/shard_map/ppermute | solution.py:123
  668.8 5.6 collective-permute-done.78
  689.5 8.1 %collective-permute-done.83 = bf16[2,2,64,512]{3,2,1,0:T(8,128)(2,1)S(1)} collective-permute-done((bf16[2,2,64,512]{3,2,1,0:T(8,128)(2,1)S(1)}, bf16[2,2,64,512]{3,2,1,0:T(8,128)(2,1)S(1)}, u32[]{:S(2)}, u32[]{:S(2)}) %collective-permute-start.83) | collective-permute-done | bytes 262176 | tf_op jit(solution)/shard_map/ppermute | solution.py:42
  (669 shorter events, 267.1 us)
Async XLA Ops:
  7.2 110.9 %all-gather.7.cloned.1.call-start = ((), (), s32[]{:S(2)}) async-start(), calls=%async_computation.7 | async-start | bytes 1310720 | tf_op jit(solution)/shard_map/all_gather | solution.py:115
  17.8 20.4 %collective-permute-start.7 = (bf16[2,2,64,512]{3,2,1,0:T(8,128)(2,1)}, bf16[2,2,64,512]{3,2,1,0:T(8,128)(2,1)}, u32[]{:S(2)}, u32[]{:S(2)}) collective-permute-start(bf16[2,2,64,512]{3,2,1,0:T(8,128)(2,1)} %get-tuple-element.365), channel_id=1, source_target_pairs={{0,16},{16,0},{8,24},{24,8},{1,17},{17,1},{9,25},{25,9},{2,18},{18... | collective-permute-start | bytes 786440 | tf_op jit(solution)/shard_map/ppermute | solution.py:34
  32.4 23.5 %collective-permute-start.2 = (bf16[128,2048]{1,0:T(8,128)(2,1)}, bf16[128,2048]{1,0:T(8,128)(2,1)}, u32[]{:S(2)}, u32[]{:S(2)}) collective-permute-start(bf16[128,2048]{1,0:T(8,128)(2,1)} %get-tuple-element.137), channel_id=1, source_target_pairs={{0,0},{1,1},{2,2},{3,3},{4,8},{5,9},{6,10},{7,11},{8,4},{9,5},{10,... | collective-permute-start | bytes 1572872 | tf_op jit(solution)/shard_map/ppermute | solution.py:249
  37.8 20.2 %collective-permute-start.3 = (bf16[128,2048]{1,0:T(8,128)(2,1)}, bf16[128,2048]{1,0:T(8,128)(2,1)}, u32[]{:S(2)}, u32[]{:S(2)}) collective-permute-start(bf16[128,2048]{1,0:T(8,128)(2,1)} %get-tuple-element.138), channel_id=1, source_target_pairs={{0,2},{1,3},{2,0},{3,1},{4,10},{5,11},{6,8},{7,9},{8,6},{9,7},{10,... | collective-permute-start | bytes 1572872 | tf_op jit(solution)/shard_map/ppermute | solution.py:250
  78.9 91.9 %all-gather.5.cloned.1.call-start = ((), (), s32[]{:S(2)}) async-start(), calls=%async_computation.6 | async-start | bytes 2621440 | tf_op jit(solution)/shard_map/all_gather | solution.py:115
  86.4 208.3 %all-gather.11.cloned.1.call-start = ((), (), s32[]{:S(2)}) async-start(), calls=%async_computation.9 | async-start | bytes 7864320 | tf_op jit(solution)/shard_map/all_gather | solution.py:115
  93.9 21.0 %collective-permute-start.16 = (bf16[256,2048]{1,0:T(8,128)(2,1)S(1)}, bf16[256,2048]{1,0:T(8,128)(2,1)}, u32[]{:S(2)}, u32[]{:S(2)}) collective-permute-start(bf16[256,2048]{1,0:T(8,128)(2,1)S(1)} %pad_maximum_fusion.4.refs_0_), channel_id=1, source_target_pairs={{0,1},{1,0},{2,3},{3,2},{4,5},{5,4},{6,7},{7,6},{8,9},{9,8},{10,11... | collective-permute-start | bytes 3145736 | tf_op jit(solution)/shard_map/ppermute | solution.py:42
  115.1 25.3 %collective-permute-start.18 = (bf16[2,128,768]{2,1,0:T(8,128)(2,1)}, bf16[2,128,768]{2,1,0:T(8,128)(2,1)}, u32[]{:S(2)}, u32[]{:S(2)}) collective-permute-start(bf16[2,128,768]{2,1,0:T(8,128)(2,1)} %bitcast.49), channel_id=1, source_target_pairs={{0,16},{16,0},{8,24},{24,8},{1,17},{17,1},{9,25},{25,9},{2,18},{18... | collective-permute-start | bytes 1179656 | tf_op jit(solution)/shard_map/ppermute | solution.py:34
  120.5 32.9 %collective-permute-start.28 = (bf16[2,64,2048]{2,1,0:T(8,128)(2,1)}, bf16[2,64,2048]{2,1,0:T(8,128)(2,1)}, u32[]{:S(2)}, u32[]{:S(2)}) collective-permute-start(bf16[2,64,2048]{2,1,0:T(8,128)(2,1)} %get-tuple-element.325), channel_id=1, source_target_pairs={{0,1},{1,0},{2,3},{3,2},{4,5},{5,4},{6,7},{7,6},{8,9},{9,8},{10,11... | collective-permute-start | bytes 1572872 | tf_op jit(solution)/shard_map/ppermute | solution.py:42
  122.1 35.9 %collective-permute-start.22 = (bf16[256,2048]{1,0:T(8,128)(2,1)S(1)}, bf16[256,2048]{1,0:T(8,128)(2,1)}, u32[]{:S(2)}, u32[]{:S(2)}) collective-permute-start(bf16[256,2048]{1,0:T(8,128)(2,1)S(1)} %pad_maximum_fusion.4.refs_0_), channel_id=1, source_target_pairs={{0,8},{8,0},{16,24},{24,16},{1,9},{9,1},{17,25},{25,17},{2,10},{10... | collective-permute-start | bytes 3145736 | tf_op jit(solution)/shard_map/ppermute | solution.py:38
  140.3 30.5 %collective-permute-start.24 = (bf16[256,2048]{1,0:T(8,128)(2,1)}, bf16[256,2048]{1,0:T(8,128)(2,1)}, u32[]{:S(2)}, u32[]{:S(2)}) collective-permute-start(bf16[256,2048]{1,0:T(8,128)(2,1)} %copy-done.10), channel_id=1, source_target_pairs={{0,8},{8,0},{16,24},{24,16},{1,9},{9,1},{17,25},{25,17},{2,10},{10... | collective-permute-start | bytes 3145736 | tf_op jit(solution)/shard_map/ppermute | solution.py:38
  148.9 21.9 %collective-permute-start.23 = (bf16[256,2048]{1,0:T(8,128)(2,1)}, bf16[256,2048]{1,0:T(8,128)(2,1)}, u32[]{:S(2)}, u32[]{:S(2)}) collective-permute-start(bf16[256,2048]{1,0:T(8,128)(2,1)} %collective-permute-done.16.refs_1_), channel_id=1, source_target_pairs={{0,8},{8,0},{16,24},{24,16},{1,9},{9,1},{17,25},{25,17},{2,10},{10... | collective-permute-start | bytes 3145736 | tf_op jit(solution)/shard_map/ppermute | solution.py:38
  158.0 25.9 %collective-permute-start.26 = (bf16[256,2048]{1,0:T(8,128)(2,1)}, bf16[256,2048]{1,0:T(8,128)(2,1)}, u32[]{:S(2)}, u32[]{:S(2)}) collective-permute-start(bf16[256,2048]{1,0:T(8,128)(2,1)} %pad_maximum_fusion.6.refs_8_), channel_id=1, source_target_pairs={{0,1},{1,0},{2,3},{3,2},{4,5},{5,4},{6,7},{7,6},{8,9},{9,8},{10,11... | collective-permute-start | bytes 3145736 | tf_op jit(solution)/shard_map/ppermute | solution.py:42
  159.5 25.6 %collective-permute-start.27 = (bf16[256,2048]{1,0:T(8,128)(2,1)}, bf16[256,2048]{1,0:T(8,128)(2,1)}, u32[]{:S(2)}, u32[]{:S(2)}) collective-permute-start(bf16[256,2048]{1,0:T(8,128)(2,1)} %pad_maximum_fusion.7.refs_10_), channel_id=1, source_target_pairs={{0,16},{16,0},{8,24},{24,8},{1,17},{17,1},{9,25},{25,9},{2,18},{18... | collective-permute-start | bytes 3145736 | tf_op jit(solution)/shard_map/ppermute | solution.py:34
  163.1 200.3 %all-gather.9.cloned.1.call-start = ((), (), s32[]{:S(2)}) async-start(), calls=%async_computation.8 | async-start | bytes 3932160 | tf_op jit(solution)/shard_map/all_gather | solution.py:115
  205.9 25.3 %collective-permute-start.31 = (bf16[256,2048]{1,0:T(8,128)(2,1)S(1)}, bf16[256,2048]{1,0:T(8,128)(2,1)S(1)}, u32[]{:S(2)}, u32[]{:S(2)}) collective-permute-start(bf16[256,2048]{1,0:T(8,128)(2,1)S(1)} %get-tuple-element.168), channel_id=1, source_target_pairs={{0,1},{1,0},{2,3},{3,2},{4,5},{5,4},{6,7},{7,6},{8,9},{9,8},{10,11... | collective-permute-start | bytes 3145736 | tf_op jit(solution)/shard_map/ppermute | solution.py:42
  206.5 24.9 %collective-permute-start.32 = (bf16[256,2048]{1,0:T(8,128)(2,1)S(1)}, bf16[256,2048]{1,0:T(8,128)(2,1)S(1)}, u32[]{:S(2)}, u32[]{:S(2)}) collective-permute-start(bf16[256,2048]{1,0:T(8,128)(2,1)S(1)} %get-tuple-element.169), channel_id=1, source_target_pairs={{0,16},{16,0},{8,24},{24,8},{1,17},{17,1},{9,25},{25,9},{2,18},{18... | collective-permute-start | bytes 3145736 | tf_op jit(solution)/shard_map/ppermute | solution.py:34
  265.1 24.0 %collective-permute-start.41 = (bf16[256,2048]{1,0:T(8,128)(2,1)S(1)}, bf16[256,2048]{1,0:T(8,128)(2,1)}, u32[]{:S(2)}, u32[]{:S(2)}) collective-permute-start(bf16[256,2048]{1,0:T(8,128)(2,1)S(1)} %pad_maximum_fusion.8.refs_0_), channel_id=1, source_target_pairs={{0,1},{1,0},{2,3},{3,2},{4,5},{5,4},{6,7},{7,6},{8,9},{9,8},{10,11... | collective-permute-start | bytes 3145736 | tf_op jit(solution)/shard_map/ppermute | solution.py:42
  266.5 23.7 %collective-permute-start.42 = (bf16[256,2048]{1,0:T(8,128)(2,1)S(1)}, bf16[256,2048]{1,0:T(8,128)(2,1)}, u32[]{:S(2)}, u32[]{:S(2)}) collective-permute-start(bf16[256,2048]{1,0:T(8,128)(2,1)S(1)} %pad_maximum_fusion.9.refs_2_), channel_id=1, source_target_pairs={{0,16},{16,0},{8,24},{24,8},{1,17},{17,1},{9,25},{25,9},{2,18},{18... | collective-permute-start | bytes 3145736 | tf_op jit(solution)/shard_map/ppermute | solution.py:34
  267.5 23.3 %collective-permute-start.43 = (bf16[256,2048]{1,0:T(8,128)(2,1)S(1)}, bf16[256,2048]{1,0:T(8,128)(2,1)}, u32[]{:S(2)}, u32[]{:S(2)}) collective-permute-start(bf16[256,2048]{1,0:T(8,128)(2,1)S(1)} %pad_maximum_fusion.8.refs_0_), channel_id=1, source_target_pairs={{0,8},{8,0},{16,24},{24,16},{1,9},{9,1},{17,25},{25,17},{2,10},{10... | collective-permute-start | bytes 3145736 | tf_op jit(solution)/shard_map/ppermute | solution.py:38
  267.5 23.3 %collective-permute-start.45 = (bf16[256,2048]{1,0:T(8,128)(2,1)S(1)}, bf16[256,2048]{1,0:T(8,128)(2,1)}, u32[]{:S(2)}, u32[]{:S(2)}) collective-permute-start(bf16[256,2048]{1,0:T(8,128)(2,1)S(1)} %pad_maximum_fusion.9.refs_2_), channel_id=1, source_target_pairs={{0,8},{8,0},{16,24},{24,16},{1,9},{9,1},{17,25},{25,17},{2,10},{10... | collective-permute-start | bytes 3145736 | tf_op jit(solution)/shard_map/ppermute | solution.py:38
  290.7 219.0 %reduce-scatter.9.cloned.1.call-start = ((), (), s32[]{:S(2)}) async-start(), calls=%async_computation.11 | async-start | bytes 2621440 | tf_op jit(solution)/shard_map/reduce_scatter | solution.py:119
  343.9 165.8 %reduce-scatter.7.cloned.1.call-start = ((), (), s32[]{:S(2)}) async-start(), calls=%async_computation.10 | async-start | bytes 5242880 | tf_op jit(solution)/shard_map/reduce_scatter | solution.py:119
  344.5 206.9 %reduce-scatter.13.cloned.1.call-start = ((), (), s32[]{:S(2)}) async-start(), calls=%async_computation.13 | async-start | bytes 1310720 | tf_op jit(solution)/shard_map/reduce_scatter | solution.py:119
  390.0 25.6 %collective-permute-start.49 = (bf16[256,2048]{1,0:T(8,128)(2,1)}, bf16[256,2048]{1,0:T(8,128)(2,1)}, u32[]{:S(2)}, u32[]{:S(2)}) collective-permute-start(bf16[256,2048]{1,0:T(8,128)(2,1)} %get-tuple-element.198), channel_id=1, source_target_pairs={{0,1},{1,0},{2,3},{3,2},{4,5},{5,4},{6,7},{7,6},{8,9},{9,8},{10,11... | collective-permute-start | bytes 3145736 | tf_op jit(solution)/shard_map/ppermute | solution.py:42
  391.0 25.0 %collective-permute-start.50 = (bf16[256,2048]{1,0:T(8,128)(2,1)S(1)}, bf16[256,2048]{1,0:T(8,128)(2,1)}, u32[]{:S(2)}, u32[]{:S(2)}) collective-permute-start(bf16[256,2048]{1,0:T(8,128)(2,1)S(1)} %get-tuple-element.199), channel_id=1, source_target_pairs={{0,16},{16,0},{8,24},{24,8},{1,17},{17,1},{9,25},{25,9},{2,18},{18... | collective-permute-start | bytes 3145736 | tf_op jit(solution)/shard_map/ppermute | solution.py:34
  442.8 111.1 %reduce-scatter.11.cloned.1.call-start = ((), (), s32[]{:S(2)}) async-start(), calls=%async_computation.12 | async-start | bytes 2621440 | tf_op jit(solution)/shard_map/reduce_scatter | solution.py:119
  455.6 21.8 %collective-permute-start.55 = (bf16[256,2048]{1,0:T(8,128)(2,1)S(1)}, bf16[256,2048]{1,0:T(8,128)(2,1)}, u32[]{:S(2)}, u32[]{:S(2)}) collective-permute-start(bf16[256,2048]{1,0:T(8,128)(2,1)S(1)} %pad_maximum_fusion.10.refs_0_), channel_id=1, source_target_pairs={{0,1},{1,0},{2,3},{3,2},{4,5},{5,4},{6,7},{7,6},{8,9},{9,8},{10,11... | collective-permute-start | bytes 3145736 | tf_op jit(solution)/shard_map/ppermute | solution.py:42
  456.9 21.5 %collective-permute-start.56 = (bf16[256,2048]{1,0:T(8,128)(2,1)S(1)}, bf16[256,2048]{1,0:T(8,128)(2,1)}, u32[]{:S(2)}, u32[]{:S(2)}) collective-permute-start(bf16[256,2048]{1,0:T(8,128)(2,1)S(1)} %pad_maximum_fusion.11.refs_2_), channel_id=1, source_target_pairs={{0,16},{16,0},{8,24},{24,8},{1,17},{17,1},{9,25},{25,9},{2,18},{18... | collective-permute-start | bytes 3145736 | tf_op jit(solution)/shard_map/ppermute | solution.py:34
  462.8 23.9 %collective-permute-start.63 = (bf16[256,2048]{1,0:T(8,128)(2,1)S(1)}, bf16[256,2048]{1,0:T(8,128)(2,1)S(1)}, u32[]{:S(2)}, u32[]{:S(2)}) collective-permute-start(bf16[256,2048]{1,0:T(8,128)(2,1)S(1)} %pad_maximum_fusion.10.refs_0_), channel_id=1, source_target_pairs={{0,8},{8,0},{16,24},{24,16},{1,9},{9,1},{17,25},{25,17},{2,10},{10... | collective-permute-start | bytes 3145736 | tf_op jit(solution)/shard_map/ppermute | solution.py:38
  478.4 25.4 %collective-permute-start.57 = (bf16[512,2048]{1,0:T(8,128)(2,1)}, bf16[512,2048]{1,0:T(8,128)(2,1)}, u32[]{:S(2)}, u32[]{:S(2)}) collective-permute-start(bf16[512,2048]{1,0:T(8,128)(2,1)} %add_convert_fusion.3), channel_id=1, source_target_pairs={{0,8},{8,0},{16,24},{24,16},{1,9},{9,1},{17,25},{25,17},{2,10},{10... | collective-permute-start | bytes 6291464 | tf_op jit(solution)/shard_map/ppermute | solution.py:38
  478.4 25.4 %collective-permute-start.58 = (bf16[512,2048]{1,0:T(8,128)(2,1)}, bf16[512,2048]{1,0:T(8,128)(2,1)}, u32[]{:S(2)}, u32[]{:S(2)}) collective-permute-start(bf16[512,2048]{1,0:T(8,128)(2,1)} %add_convert_fusion.2), channel_id=1, source_target_pairs={{0,8},{8,0},{16,24},{24,16},{1,9},{9,1},{17,25},{25,17},{2,10},{10... | collective-permute-start | bytes 6291464 | tf_op jit(solution)/shard_map/ppermute | solution.py:38
  487.7 198.1 %reduce-scatter.15.cloned.1.call-start = ((), (), s32[]{:S(2)}) async-start(), calls=%async_computation.14 | async-start | bytes 2621440 | tf_op jit(solution)/shard_map/reduce_scatter | solution.py:119
  508.0 46.2 %collective-permute-start.59 = (bf16[256,2048]{1,0:T(8,128)(2,1)}, bf16[256,2048]{1,0:T(8,128)(2,1)S(1)}, u32[]{:S(2)}, u32[]{:S(2)}) collective-permute-start(bf16[256,2048]{1,0:T(8,128)(2,1)} %get-tuple-element.222), channel_id=1, source_target_pairs={{0,1},{1,0},{2,3},{3,2},{4,5},{5,4},{6,7},{7,6},{8,9},{9,8},{10,11... | collective-permute-start | bytes 3145736 | tf_op jit(solution)/shard_map/ppermute | solution.py:42
  508.8 45.4 %collective-permute-start.60 = (bf16[256,2048]{1,0:T(8,128)(2,1)}, bf16[256,2048]{1,0:T(8,128)(2,1)}, u32[]{:S(2)}, u32[]{:S(2)}) collective-permute-start(bf16[256,2048]{1,0:T(8,128)(2,1)} %get-tuple-element.223), channel_id=1, source_target_pairs={{0,16},{16,0},{8,24},{24,8},{1,17},{17,1},{9,25},{25,9},{2,18},{18... | collective-permute-start | bytes 3145736 | tf_op jit(solution)/shard_map/ppermute | solution.py:34
  545.1 27.6 %collective-permute-start.67 = (bf16[512,2048]{1,0:T(8,128)(2,1)}, bf16[512,2048]{1,0:T(8,128)(2,1)S(1)}, u32[]{:S(2)}, u32[]{:S(2)}) collective-permute-start(bf16[512,2048]{1,0:T(8,128)(2,1)} %convolution_convert_fusion.8), channel_id=1, source_target_pairs={{0,8},{8,0},{16,24},{24,16},{1,9},{9,1},{17,25},{25,17},{2,10},{10... | collective-permute-start | bytes 6291464 | tf_op jit(solution)/shard_map/ppermute | solution.py:38
  545.1 27.6 %collective-permute-start.68 = (bf16[512,2048]{1,0:T(8,128)(2,1)}, bf16[512,2048]{1,0:T(8,128)(2,1)}, u32[]{:S(2)}, u32[]{:S(2)}) collective-permute-start(bf16[512,2048]{1,0:T(8,128)(2,1)} %convolution_convert_fusion.7), channel_id=1, source_target_pairs={{0,8},{8,0},{16,24},{24,16},{1,9},{9,1},{17,25},{25,17},{2,10},{10... | collective-permute-start | bytes 6291464 | tf_op jit(solution)/shard_map/ppermute | solution.py:38
  553.9 152.2 %reduce-scatter.17.cloned.1.call-start = ((), (), s32[]{:S(2)}) async-start(), calls=%async_computation.15 | async-start | bytes 1310720 | tf_op jit(solution)/shard_map/reduce_scatter | solution.py:119
  577.8 36.4 %collective-permute-start.69 = (bf16[256,2048]{1,0:T(8,128)(2,1)}, bf16[256,2048]{1,0:T(8,128)(2,1)S(1)}, u32[]{:S(2)}, u32[]{:S(2)}) collective-permute-start(bf16[256,2048]{1,0:T(8,128)(2,1)} %get-tuple-element.237), channel_id=1, source_target_pairs={{0,1},{1,0},{2,3},{3,2},{4,5},{5,4},{6,7},{7,6},{8,9},{9,8},{10,11... | collective-permute-start | bytes 3145736 | tf_op jit(solution)/shard_map/ppermute | solution.py:42
  579.3 34.9 %collective-permute-start.70 = (bf16[256,2048]{1,0:T(8,128)(2,1)}, bf16[256,2048]{1,0:T(8,128)(2,1)}, u32[]{:S(2)}, u32[]{:S(2)}) collective-permute-start(bf16[256,2048]{1,0:T(8,128)(2,1)} %get-tuple-element.238), channel_id=1, source_target_pairs={{0,16},{16,0},{8,24},{24,8},{1,17},{17,1},{9,25},{25,9},{2,18},{18... | collective-permute-start | bytes 3145736 | tf_op jit(solution)/shard_map/ppermute | solution.py:34
  586.0 27.0 %collective-permute-start.85 = (bf16[2,64,2048]{2,1,0:T(8,128)(2,1)S(1)}, bf16[2,64,2048]{2,1,0:T(8,128)(2,1)S(1)}, u32[]{:S(2)}, u32[]{:S(2)}) collective-permute-start(bf16[2,64,2048]{2,1,0:T(8,128)(2,1)S(1)} %get-tuple-element.321), channel_id=1, source_target_pairs={{0,1},{1,0},{2,3},{3,2},{4,5},{5,4},{6,7},{7,6},{8,9},{9,8},{10,11... | collective-permute-start | bytes 1572872 | tf_op jit(solution)/shard_map/ppermute | solution.py:42
  616.5 22.0 %collective-permute-start.73 = (bf16[128,2048]{1,0:T(8,128)(2,1)S(1)}, bf16[128,2048]{1,0:T(8,128)(2,1)S(1)}, u32[]{:S(2)}, u32[]{:S(2)}) collective-permute-start(bf16[128,2048]{1,0:T(8,128)(2,1)S(1)} %get-tuple-element.241), channel_id=1, source_target_pairs={{0,16},{16,0},{8,24},{24,8},{1,17},{17,1},{9,25},{25,9},{2,18},{18... | collective-permute-start | bytes 1572872 | tf_op jit(solution)/shard_map/ppermute | solution.py:34
  617.3 22.3 %collective-permute-start.74 = (bf16[128,2048]{1,0:T(8,128)(2,1)S(1)}, bf16[128,2048]{1,0:T(8,128)(2,1)S(1)}, u32[]{:S(2)}, u32[]{:S(2)}) collective-permute-start(bf16[128,2048]{1,0:T(8,128)(2,1)S(1)} %get-tuple-element.242), channel_id=1, source_target_pairs={{0,1},{1,0},{2,3},{3,2},{4,5},{5,4},{6,7},{7,6},{8,9},{9,8},{10,11... | collective-permute-start | bytes 1572872 | tf_op jit(solution)/shard_map/ppermute | solution.py:42
  620.8 61.4 %collective-permute-start.72 = (bf16[128,2048]{1,0:T(8,128)(2,1)}, bf16[128,2048]{1,0:T(8,128)(2,1)}, u32[]{:S(2)}, u32[]{:S(2)}) collective-permute-start(bf16[128,2048]{1,0:T(8,128)(2,1)} %get-tuple-element.323), channel_id=1, source_target_pairs={{2,0},{3,1},{0,2},{1,3},{10,4},{11,5},{8,6},{9,7},{6,8},{7,9},{4,1... | collective-permute-start | bytes 1572872 | tf_op jit(solution)/shard_map/ppermute | solution.py:257
  630.9 51.3 %collective-permute-start.71 = (bf16[128,2048]{1,0:T(8,128)(2,1)}, bf16[128,2048]{1,0:T(8,128)(2,1)}, u32[]{:S(2)}, u32[]{:S(2)}) collective-permute-start(bf16[128,2048]{1,0:T(8,128)(2,1)} %get-tuple-element.324), channel_id=1, source_target_pairs={{0,0},{1,1},{2,2},{3,3},{8,4},{9,5},{10,6},{11,7},{4,8},{5,9},{6,1... | collective-permute-start | bytes 1572872 | tf_op jit(solution)/shard_map/ppermute | solution.py:256
  639.7 47.4 %collective-permute-start.87 = (bf16[2,128,1024]{2,1,0:T(8,128)(2,1)}, bf16[2,128,1024]{2,1,0:T(8,128)(2,1)}, u32[]{:S(2)}, u32[]{:S(2)}) collective-permute-start(bf16[2,128,1024]{2,1,0:T(8,128)(2,1)} %get-tuple-element.317), channel_id=1, source_target_pairs={{0,16},{16,0},{8,24},{24,8},{1,17},{17,1},{9,25},{25,9},{2,18},{18... | collective-permute-start | bytes 1572872 | tf_op jit(solution)/shard_map/ppermute | solution.py:34
  648.5 20.1 %collective-permute-start.77 = (f32[2,2,2,2,136]{4,3,2,1,0:T(2,128)S(1)}, f32[2,2,2,2,136]{4,3,2,1,0:T(2,128)S(1)}, u32[]{:S(2)}, u32[]{:S(2)}) collective-permute-start(f32[2,2,2,2,136]{4,3,2,1,0:T(2,128)S(1)} %dynamic-slice_bitcast_fusion.20), channel_id=1, source_target_pairs={{0,4},{2,6},{4,0},{6,2},{1,5},{3,7},{5,1},{7,3},{8,12},{10,14},{12... | collective-permute-start | bytes 26120 | tf_op jit(solution)/shard_map/ppermute | solution.py:123
  651.6 50.3 %collective-permute-start.75 = (bf16[128,2048]{1,0:T(8,128)(2,1)S(1)}, bf16[128,2048]{1,0:T(8,128)(2,1)S(1)}, u32[]{:S(2)}, u32[]{:S(2)}) collective-permute-start(bf16[128,2048]{1,0:T(8,128)(2,1)S(1)} %broadcast_select_fusion.1), channel_id=1, source_target_pairs={{0,0},{1,1},{2,2},{3,3},{8,4},{9,5},{10,6},{11,7},{4,8},{5,9},{6,1... | collective-permute-start | bytes 1572872 | tf_op jit(solution)/shard_map/ppermute | solution.py:256
  (162 other events, 1569.3 us)
Sparse Core Ops, SparseCore 0:
  79.0 39.0 all-gather.6
  120.2 45.3 all-gather.4
  167.8 114.0 all-gather.10
  290.9 65.0 all-gather.8
  358.1 42.4 reduce-scatter.8
  402.9 76.0 reduce-scatter.6
  481.3 27.6 reduce-scatter.12
  511.4 42.4 reduce-scatter.10
  556.2 42.8 reduce-scatter.14
  614.3 39.7 reduce-scatter.16

commit v2 on v1

--- a/solution.py
+++ b/solution.py
@@ -74,27 +74,38 @@
     near = [low_row, low_both, high_row, high_both]
     last = [after(piece, *core_after) if core_after else piece for piece in (low_both, high_both)]
     sent = [low_row, last[0], high_row, last[1]]
-    return near + [over_c(piece) for piece in sent], (low_row, high_row)
-
-
-def layer_scatter(product, core_after=()):
+    return near + [over_c(piece) for piece in sent]
+
+
+def scatter_start(product, core_after=(), middle=None):
     sent_low, sent_high = product(1024, 1536), product(1536, 2048)
-    here = product(0, 1024, sent_low, sent_high)
+    more = middle((sent_low[0], sent_high[0])) if middle else ()
+    here = product(0, 1024, sent_low[0], sent_high[0], *more)
     far_low, far_high = together(
-        over_c(after(sent_low, *core_after)), over_c(after(sent_high, *core_after))
-    )
-    second = together(sum_low(here[256:512], far_low[256:]), sum_low(here[768:], far_high[256:]))
+        over_c(after(sent_low[0], *core_after)), over_c(after(sent_high[0], *core_after))
+    )
+    second = together(
+        sum_low(*[part[256:512] for part in here], far_low[256:]),
+        sum_low(*[part[768:] for part in here], far_high[256:]),
+    )
     low_back, high_back = together(over_y(second[0]), over_x(second[1]))
+    return here, (far_low, far_high), second, (low_back, high_back)
+
+
+def scatter_end(state, before=()):
+    here, (far_low, far_high), _, (low_back, high_back) = state
+    if before:
+        low_back, high_back, *_ = together(low_back, high_back, *before)
     third = together(
-        sum_low(here[128:256], far_low[128:256], low_back[128:]),
-        sum_low(here[640:768], far_high[128:256], high_back[128:]),
+        sum_low(*[part[128:256] for part in here], far_low[128:256], low_back[128:]),
+        sum_low(*[part[640:768] for part in here], far_high[128:256], high_back[128:]),
     )
     low_last, high_last = together(over_x(third[0]), over_y(third[1]))
     parts = (
-        (here[:128], far_low[:128], low_back[:128], low_last),
-        (here[512:640], far_high[:128], high_back[:128], high_last),
-    )
-    return parts, here, second, third
+        (*[part[:128] for part in here], far_low[:128], low_back[:128], low_last),
+        (*[part[512:640] for part in here], far_high[:128], high_back[:128], high_last),
+    )
+    return parts, third
 
 
 def product_of(rows, matrix, dims, more=None):
@@ -102,7 +113,9 @@
         part = rows[first:last]
         part = after(part, *before) if before else part
         out = lax.dot_general(part, matrix, dims, preferred_element_type=F32)
-        return (out if more is None else out + more[first].astype(F32)).astype(BF)
+        if more is None or first == 0:
+            return [out.astype(BF)] + (more[first] if more else [])
+        return [(out + more[first][0].astype(F32)).astype(BF)]
 
     return product
 
@@ -123,31 +136,28 @@
     return lax.ppermute(value, "blk", [(z, z ^ step) for z in range(4)])
 
 
-def small_gather_z(value, z):
-    for bit, step in ((z % 2, 1), (z // 2, 2)):
-        value = flip_where(bit, jnp.stack([value, swap_z(value, step)]), 0)
-    return value
-
-
-def small_gather(value, coords):
+def small_gather(value, coords, z):
     x_bit, c_bit, y_bit = coords
-    for bit, move in ((y_bit, over_y), (c_bit, over_c), (x_bit, over_x)):
-        value = flip_where(bit, jnp.stack([value, move(value)]), 0)
-    return value.reshape(2, 2, 2, 4, -1)
-
-
-def small_scatter(value, coords, z):
+    for bit, move in (
+        (y_bit, over_y),
+        (c_bit, over_c),
+        (x_bit, over_x),
+        (z % 2, functools.partial(swap_z, step=1)),
+        (z // 2, functools.partial(swap_z, step=2)),
+    ):
+        got = move(value)
+        value = flip_where(bit, jnp.stack([value, got]), 0)
+    return value.reshape(4, 2, 2, 2, -1), got
+
+
+def small_scatter(value, coords, z, before):
     x_bit, c_bit, y_bit = coords
     value = value.reshape(2, 2, 2, 2, 2, -1)
-    moves = (
-        (z // 2, functools.partial(swap_z, step=2), 2),
-        (z % 2, functools.partial(swap_z, step=1), 2),
-        (x_bit, over_x, 0),
-        (c_bit, over_c, 0),
-        (y_bit, over_y, 0),
-    )
-    for bit, move, axis in moves:
+    for bit, move, axis in ((x_bit, over_x, 0), (c_bit, over_c, 0), (y_bit, over_y, 2)):
         value = pick(value, bit, axis) + move(pick(value, 1 - bit, axis))
+    value = after(value, *before)
+    for bit, step in ((z // 2, 2), (z % 2, 1)):
+        value = pick(value, bit, 0) + swap_z(pick(value, 1 - bit, 0), step)
     return value
 
 
@@ -251,11 +261,13 @@
     return by_bit(odd, got_first, got_second), by_bit(odd, got_second, got_first)
 
 
-def rows_out(low, high, odd, dtype):
+def rows_back(sent):
     moves = row_moves()
-    got_first = lax.ppermute(by_bit(odd, low, high), EVERY, [(b, a) for a, b in moves[0]])
-    got_second = lax.ppermute(by_bit(odd, high, low), EVERY, [(b, a) for a, b in moves[1]])
-    return keep_rows(got_first, got_second, odd, dtype)
+    return [lax.ppermute(s, EVERY, [(b, a) for a, b in m]) for s, m in zip(sent, moves, strict=True)]
+
+
+def rows_out(low, high, odd):
+    return rows_back((by_bit(odd, low, high), by_bit(odd, high, low)))
 
 
 def block_rows(scalars, row, block):
@@ -594,7 +606,12 @@
     return lax.dot_general(rows, columns, COLS_C, preferred_element_type=F32).astype(BF)
 
 
-CHUNKS = ((0, 2), (2, 3))
+def scaled_wgrad(rows, columns, gain):
+    out = lax.dot_general(rows, columns, COLS_C, preferred_element_type=F32)
+    return (out * gain[:, None]).astype(BF)
+
+
+CHUNKS = ((0, 3),)
 
 
 def layer_shards(
@@ -614,17 +631,16 @@
     transposed = (((1,), (1,)), ((), ()))
     plain = (((1,), (0,)), ((), ()))
 
+    sent = *send_rows(hidden_in, odd), *send_rows(out_grad, odd)
     small = jnp.concatenate(
         [v.astype(F32) for v in (norm_attn, norm_mlp, query_gain, key_gain)]
-        + [doc_lengths.astype(F32).reshape(-1)]
-    )
-    small_z = small_gather_z(small, z)
-    tokens = rows_in(send_rows(after(hidden_in, small_z), odd), odd)
-    small_all = small_gather(small_z, coords)
-    top_own = rows_in(send_rows(after(out_grad, *tokens), odd), odd)
+        + [after(doc_lengths, *sent).astype(F32).reshape(-1)]
+    )
+    tokens, top_own = rows_in(sent[:2], odd), rows_in(sent[2:], odd)
+    small_all, small_last = small_gather(small, coords, z)
 
     pieces = jnp.concatenate(
-        [w.reshape(share, 8, -1) for w in (query_weight, key_weight, value_weight)], axis=-1
+        [w.reshape(share, 8, -1) for w in (after(query_weight, *sent), key_weight, value_weight)], axis=-1
     )
     pieces = jnp.transpose(pieces, (1, 0, 2)).reshape(2, 2, 2, share, -1)
     pieces = trade(pieces, x_bit, over_x, 0)
@@ -632,8 +648,8 @@
     qkv_own = trade(pieces, c_bit, over_c, 1)
 
     n_attn, n_head = norm_attn.shape[0], query_gain.shape[0]
-    by_device = jnp.transpose(small_all, (0, 1, 3, 2, 4)).reshape(32, -1)
-    by_blk = jnp.transpose(small_all, (3, 0, 1, 2, 4)).reshape(32, -1)
+    by_device = jnp.transpose(small_all, (1, 2, 0, 3, 4)).reshape(32, -1)
+    by_blk = small_all.reshape(32, -1)
     gain_attn = by_blk[:, :n_attn].reshape(-1)
     gain_mlp = by_blk[:, n_attn : 2 * n_attn].reshape(-1)
     gain_query = by_device[:, 2 * n_attn : 2 * n_attn + n_head].reshape(-1)
@@ -675,29 +691,32 @@
         half = join(pick(piece, x_bit, 0), half, x_bit, 0)
         return trade(half, c_bit, over_c, 1).reshape(width // 4, -1)
 
-    owns = [layer_weights(weight_pieces[0], qkv_own, small_all)]
-    qkv_own = after(qkv_own, *top_own)
-    qkv_mat = blk_gather(qkv_own.reshape(8 * share, -1))
-    out_all = blk_gather(after(output_weight, qkv_own)).reshape(2, 2, share, width)
-
-    tokens = [after(t, small_all, owns[0]) for t in tokens]
+    owns = [layer_weights(weight_pieces[0], qkv_own)]
+    arrived = tokens
+    tokens = [after(t, qkv_own, *top_own, *owns) for t in tokens]
+    attn_own = jnp.concatenate([qkv_own.reshape(8 * share, -1), output_weight.reshape(4 * share, -1)])
+    attn_all = blk_gather(after(attn_own, small_last, *arrived, *top_own)).reshape(4, 12 * share, -1)
+
     layer_in = [t.astype(F32) for t in tokens]
     inverse_attn = [norm_inverse(t) for t in layer_in]
     unit_attn = [t * i for t, i in zip(layer_in, inverse_attn, strict=True)]
-    normed1, _ = layer_gather(*[(u * gain_attn).astype(BF) for u in unit_attn])
-    owns += [layer_weights(piece, normed1[1], normed1[3]) for piece in weight_pieces[1:]]
-    mats = [blk_gather(after(own, qkv_own)) for own in owns]
-    tops, top_rows = layer_gather(*[after(t, normed1[1], normed1[3]) for t in top_own])
-    raw, normed1_all = pieces_dot(normed1, after(qkv_mat, owns[1], *top_rows), plain, F32)
-    raw = after(raw, tops[1], tops[3])
+    units1 = layer_gather(*[u.astype(BF) for u in unit_attn], (cos_table, sine_table))
+    owns += [layer_weights(piece, units1[1], units1[3]) for piece in weight_pieces[1:]]
+    mats = [blk_gather(after(own, *arrived, *top_own)) for own in owns]
+    tops = layer_gather(*[after(t, units1[1], units1[3]) for t in top_own])
+    qkv_mat = attn_all[:, : 8 * share].reshape(width, -1)
+    scaled_mat = (qkv_mat.astype(F32) * gain_attn[:, None]).astype(BF)
+    raw, units1_all = pieces_dot(units1, scaled_mat, plain, F32)
+    out_all = after(attn_all, raw)[:, 8 * share :].reshape(2, 2, share, width)
     out_all = trade(out_all, y, over_y, 0)
     out_mat = sort_model(jnp.swapaxes(out_all, 0, 1).reshape(-1, width), BF)
     (mix,) = attend(scalars, raw, cos_table, sine_table, head_gains, groups, docs)
-    mixed, *_ = layer_scatter(product_of(mix, out_mat, plain))
+    mix = after(mix, tops[1], tops[3])
+    mixed, _ = scatter_end(scatter_start(product_of(mix, out_mat, plain)))
     residual = [t + total_of(parts) for t, parts in zip(layer_in, mixed, strict=True)]
     inverse_mlp = [norm_inverse(t) for t in residual]
     unit_mlp = [t * i for t, i in zip(residual, inverse_mlp, strict=True)]
-    normed2, _ = layer_gather(*[after((u * gain_mlp).astype(BF), *tops) for u in unit_mlp])
+    normed2 = layer_gather(*[after((u * gain_mlp).astype(BF), *tops) for u in unit_mlp])
 
     hiddens, dboths, boths, downs, down_wgrads, both_wgrads = [], [], [], [], [], []
     dnormed2_part = mlp_part = None
@@ -709,7 +728,9 @@
         if normed2_all is None:
             hidden, dboth, normed2_all, top_all = units_pass(normed2, tops, mat)
         else:
-            normed2_all = after(normed2_all, *down_wgrads, *both_wgrads, *dnormed2_part.values())
+            normed2_all = after(
+                normed2_all, *down_wgrads, *both_wgrads, *(part[0] for part in dnormed2_part.values())
+            )
             hidden, dboth = units_pass([normed2_all], [top_all], mat)
         hiddens.append(hidden)
         dboths.append(dboth)
@@ -718,12 +739,14 @@
             down_wgrads.append(wgrad(top_all, after(hidden, both_wgrads[-1])))
             part = product_of(after(dboth, down_wgrads[-1]), boths[-1], transposed, dnormed2_part)
             dnormed2_part = {1024: part(1024, 1536), 1536: part(1536, 2048), 0: part(0, 1024)}
-    dnormed2, here, second, third = layer_scatter(
-        product_of(dboths[-1], boths[-1], transposed, dnormed2_part)
-    )
+    down_wgrads.append(wgrad(top_all, hiddens[-1]))
+    state = scatter_start(
+        product_of(after(dboths[-1], down_wgrads[-1]), boths[-1], transposed, dnormed2_part)
+    )
+    here, _, second, _ = state
+    both_wgrads.append(wgrad(after(normed2_all, *second), dboths[-1]))
+    dnormed2, third = scatter_end(state, both_wgrads[-1:])
     dnormed2 = [total_of(parts) for parts in dnormed2]
-    both_wgrads.append(wgrad(after(normed2_all, here), dboths[-1]))
-    down_wgrads.append(wgrad(top_all, after(hiddens[-1], *second)))
 
     gain_mlp_grad = sum(jnp.sum(g * u, axis=0) for g, u in zip(dnormed2, unit_mlp, strict=True))
     dresidual = [
@@ -733,43 +756,70 @@
     both_last, down_last = both_wgrads[-1], down_wgrads[-1]
     both_wgrads = [blk_scatter(part) for part in both_wgrads]
     down_wgrads = [blk_scatter(part) for part in down_wgrads]
+    spans = ((1024, 1536), (1536, 2048), (0, 1024))
     for hidden, down in zip(hiddens[:-1], downs[:-1], strict=True):
         part = product_of(after(hidden, *second), down, transposed, mlp_part)
-        mlp_part = {1024: part(1024, 1536), 1536: part(1536, 2048), 0: part(0, 1024)}
+        mlp_part = {first: part(first, last) for first, last in spans}
     mlp_product = product_of(after(hiddens[-1], *third), downs[-1], transposed, mlp_part)
-    mlp_product = {first: mlp_product(first, last) for first, last in ((1024, 1536), (1536, 2048), (0, 1024))}
-    dres, _ = layer_gather(
-        *[after(t.astype(BF), both_last, down_last) for t in dresidual], (*mlp_product.values(),)
-    )
-    mlp_out, _, second, _ = layer_scatter(lambda first, *_: mlp_product[first], (dres[1], dres[3]))
-    layer_out = [(t + total_of(parts)).astype(BF) for t, parts in zip(residual, mlp_out, strict=True)]
+    mlp_product = {first: mlp_product(first, last) for first, last in spans}
+    dres = layer_gather(
+        *[after(t.astype(BF), down_last) for t in dresidual],
+        [both_last] + [part[0] for part in mlp_product.values()],
+    )
+    mlp_state = scatter_start(lambda first, *_: mlp_product[first], (dres[1], dres[3]))
     dmix, dres_all = pieces_dot(dres, out_mat, transposed, BF)
-    dmix = after(dmix, *second, *both_wgrads[:-1], *down_wgrads[:-1])
+    out_wgrad = wgrad(mix, dres_all).reshape(2, 2, share, width)
+    out_away = pick(out_wgrad, 1 - y, 1)
+    dmix = after(dmix, out_away, *mlp_state[2], *both_wgrads[:-1], *down_wgrads[:-1])
     draw, dgains = attend(scalars, raw, cos_table, sine_table, head_gains, groups, docs, dmix)
-    dnormed1, here, second, third = layer_scatter(product_of(draw, qkv_mat, transposed))
+    mlp_out, mlp_third = scatter_end(mlp_state, (draw,))
+    draw = after(draw, *mlp_third)
+    beside = {}
+
+    def after_attention(sent):
+        beside["qkv"] = scaled_wgrad(units1_all, after(draw, *sent), gain_attn)
+        return beside["qkv"], *both_wgrads, *down_wgrads
+
+    state = scatter_start(product_of(draw, qkv_mat, transposed), (), after_attention)
+    second = state[2]
+    dnormed1, third = scatter_end(state)
     dnormed1 = [total_of(parts) for parts in dnormed1]
-    qkv_wgrad = wgrad(normed1_all, after(draw, here))
-    out_wgrad = wgrad(mix, after(dres_all, *second))
-    out_wgrad = trade(out_wgrad.reshape(2, 2, share, width), y, over_y, 1)
-    out_wgrad = jnp.swapaxes(out_wgrad, 0, 1).reshape(4 * share, width)
-    qkv_wgrad = blk_scatter(after(qkv_wgrad, *both_wgrads, *down_wgrads))
-    out_wgrad = blk_scatter(after(out_wgrad, *both_wgrads, *down_wgrads))
-    out_wgrad = sort_model(out_wgrad, F32)
-    layer_out = rows_out(*[after(t, *third) for t in layer_out], odd, BF)
-
-    swapped = []
-    for own in (*both_wgrads, *down_wgrads):
-        own = after(own, *third).reshape(2, 2, width // 16, -1)
-        own = trade(trade(own, c_bit, over_c, 1), x_bit, over_x, 0)
-        swapped.append(own.reshape(4, width // 16, -1))
+    out_wgrad = join(pick(out_wgrad, y, 1), after(over_y(out_away), draw), y, 0).reshape(4 * share, width)
+    attn_wgrad = jnp.concatenate(
+        [beside["qkv"].reshape(4, 8 * share, -1), out_wgrad.reshape(4, 4 * share, -1)], axis=1
+    )
+    attn_wgrad = after(attn_wgrad.reshape(48 * share, -1), *both_wgrads, *down_wgrads)
+    attn_wgrad = blk_scatter(attn_wgrad)
+    qkv_wgrad, out_low = attn_wgrad[: 8 * share], attn_wgrad[8 * share :].reshape(share, width)
+    out_wgrad = sort_model(out_low, F32)
+
+    gain_attn_grad = sum(jnp.sum(g * u, axis=0) for g, u in zip(dnormed1, unit_attn, strict=True))
+    input_grad = [
+        (t + norm_back(g, u, i, gain_attn)).astype(BF)
+        for t, g, u, i in zip(dresidual, dnormed1, unit_attn, inverse_attn, strict=True)
+    ]
+    layer_out = [
+        after((t + total_of(parts)).astype(BF), *second)
+        for t, parts in zip(residual, mlp_out, strict=True)
+    ]
+    layer_out = rows_out(*layer_out, odd)
+    layer_out = keep_rows(after(layer_out[0], *input_grad), layer_out[1], odd, BF)
+    sent = by_bit(odd, *input_grad), by_bit(odd, *input_grad[::-1])
+    input_got = rows_back(sent)
+
+    own = after(jnp.concatenate([*both_wgrads, *down_wgrads], axis=1), *second)
+    own = own.reshape(2, 2, width // 16, -1)
+    own = after(trade(own, c_bit, over_c, 1), attn_wgrad, *third)
+    own_got = over_x(pick(own, 1 - x_bit, 0))
+    swapped = join(pick(own, x_bit, 0), own_got, x_bit, 0).reshape(4, width // 16, -1)
+    input_grad = keep_rows(*input_got, odd, F32)
     gate_parts, upward_parts, down_parts = [], [], []
     for q in range(4):
-        for at, (first, last) in enumerate(CHUNKS):
-            for tile in range(last - first):
-                cut = lambda i: slice(i * UNIT_TILE, (i + 1) * UNIT_TILE)
-                gate_parts.append(swapped[at][q][:, cut(2 * tile)])
-                upward_parts.append(swapped[at][q][:, cut(2 * tile + 1)])
-                down_parts.append(swapped[len(CHUNKS) + at][q][:, cut(tile)])
+        for tile in range(quarter // UNIT_TILE):
+            cut = lambda i: swapped[q][:, i * UNIT_TILE : (i + 1) * UNIT_TILE]
+            gate_parts.append(cut(2 * tile))
+            upward_parts.append(cut(2 * tile + 1))
+            down_parts.append(cut(2 * (quarter // UNIT_TILE) + tile))
     gate_wgrad, upward_wgrad, down_wgrad = (
         jnp.concatenate(parts, axis=1).astype(F32) for parts in (gate_parts, upward_parts, down_parts)
     )
@@ -780,13 +830,6 @@
     query_wgrad = jnp.concatenate([qkv_wgrad[i][:, :q_cols] for i in range(8)], axis=1).astype(F32)
     key_wgrad = jnp.concatenate([qkv_wgrad[i][:, q_cols : q_cols + head] for i in range(8)], axis=1).astype(F32)
     value_wgrad = jnp.concatenate([qkv_wgrad[i][:, q_cols + head :] for i in range(8)], axis=1).astype(F32)
-
-    gain_attn_grad = sum(jnp.sum(g * u, axis=0) for g, u in zip(dnormed1, unit_attn, strict=True))
-    input_grad = [
-        t + norm_back(g, u, i, gain_attn)
-        for t, g, u, i in zip(dresidual, dnormed1, unit_attn, inverse_attn, strict=True)
-    ]
-    input_grad = rows_out(*[t.astype(BF) for t in input_grad], odd, F32)
 
     dgains = jnp.sum(dgains, axis=0)
     small_grads = jnp.concatenate(
@@ -798,7 +841,7 @@
         ],
         axis=1,
     )
-    small_grads = small_scatter(small_grads, coords, z)
+    small_grads = small_scatter(small_grads, coords, z, (own_got,))
     return (
         layer_out,
         input_grad,

time: 728 us -> 690 us (0.948)
  matrix products: 104 us -> 86.3 us
  other arithmetic: 92.1 us -> 80.4 us
    ppermute x34 -> x30, starting transfers between devices: 23.5 us -> 5.82 us  [over_c(): return lax.ppermute(value, 'dp', SWAP_C)]
    dot_general x6 -> x3, matrix products: 48.7 us -> 31.1 us  [wgrad(): lax.dot_general(rows, columns, COLS_C, preferred_element_type=F32)]
    ppermute x22, waiting for transfers between devices: 136 us -> 153 us  [over_y(): return lax.ppermute(value, 'fsdp', SWAP_Y)]
    ppermute x4, starting transfers between devices: 5.83 us -> 20.5 us  [swap_z(): return lax.ppermute(value, 'blk', [(z, z ^ step) for z in range(4)])]
    ppermute x4, waiting for transfers between devices: 22.5 us -> 12.4 us  [swap_z(): return lax.ppermute(value, 'blk', [(z, z ^ step) for z in range(4)])]
    dot_general x18 -> x12, matrix products: 55.8 us -> 46.5 us  [product(): out = lax.dot_general(part, matrix, dims, preferred_element_type=F32)]
    dot_general x0 -> x1, matrix products: none -> 8.65 us  [scaled_wgrad(): out = lax.dot_general(rows, columns, COLS_C, preferred_element_type=F32)]
    select_n x25 -> x16, other arithmetic: 27.6 us -> 20 us  [by_bit(): return jnp.where(bit == 1, one, zero)]
  transfers between devices with their start and end apart: 104 -> 91, of which waited for: 49 -> 43; matrix products, arithmetic and copies ran while one was open for 31% -> 27% of each run, Pallas kernels for 14% -> 9%
where the time goes in v2:
time: 690 us; the launch traced here: 682 us
  waiting for transfers between devices  249 us (36%)
  Pallas kernels  97.7 us (14%)
  starting transfers between devices  96.9 us (14%)
  matrix products  86.3 us (13%)
  other arithmetic  80.4 us (12%)
  local copies, waits for them, and re-layouts  55 us (8%)
  between operations  16.3 us (2%)
    ppermute x22, waiting for transfers between devices, over_y(): return lax.ppermute(value, 'fsdp', SWAP_Y)  153 us
    ppermute x22, waiting for transfers between devices, over_x(): return lax.ppermute(value, 'dp', SWAP_X)  62.8 us
    dot_general x12, matrix products, product(): out = lax.dot_general(part, matrix, dims, preferred_element_type=F32)  46.5 us
    pallas_call x1, Pallas kernels, units_pass(): pl.pallas_call(functools.partial(units_kernel, given=given), grid=(tiles,...  34.5 us
    pallas_call x2, Pallas kernels, attend(): pl.pallas_call(functools.partial(attend_back_kernel if back else attend_k...  32.4 us
    dot_general x3, matrix products, wgrad(): lax.dot_general(rows, columns, COLS_C, preferred_element_type=F32)  31.1 us
    unnamed x223, local copies, waits for them, and re-layouts  26.4 us
    ppermute x22, starting transfers between devices, over_x(): return lax.ppermute(value, 'dp', SWAP_X)  22 us
  transfers between devices with their start and end apart: 91, of which 43 were waited for; matrix products, arithmetic and copies ran while one was open for 27% of the time, Pallas kernels for 9%

profile of v2, /device:TPU:0, one launch (start us, length us, event | category | flops | bytes accessed | tf_op | source)
XLA Modules:
  0.0 681.7 jit_solution(15087294016954380526)
XLA Ops:
  9.7 3.0 collective-permute-start.5
  12.8 5.4 collective-permute-start.6
  20.5 5.4 collective-permute-start
  39.0 7.6 %collective-permute-done.3 = bf16[2,2,64,512]{3,2,1,0:T(8,128)(2,1)S(1)} collective-permute-done((bf16[2,2,64,512]{3,2,1,0:T(8,128)(2,1)S(1)}, bf16[2,2,64,512]{3,2,1,0:T(8,128)(2,1)S(1)}, u32[]{:S(2)}, u32[]{:S(2)}) %collective-permute-start.3) | collective-permute-done | bytes 262176 | tf_op jit(solution)/shard_map/ppermute | solution.py:42
  49.0 11.4 %collective-permute-done.12 = f32[2,2,2,144]{3,2,1,0:T(2,128)S(1)} collective-permute-done((f32[2,2,2,144]{3,2,1,0:T(2,128)S(1)}, f32[2,2,2,144]{3,2,1,0:T(2,128)S(1)}, u32[]{:S(2)}, u32[]{:S(2)}) %collective-permute-start.12) | collective-permute-done | bytes 4640 | tf_op jit(solution)/shard_map/ppermute | solution.py:136
  67.6 20.3 %collective-permute-done.7 = bf16[2,128,2304]{2,1,0:T(8,128)(2,1)S(1)} collective-permute-done((bf16[2,128,2304]{2,1,0:T(8,128)(2,1)}, bf16[2,128,2304]{2,1,0:T(8,128)(2,1)S(1)}, u32[]{:S(2)}, u32[]{:S(2)}) %collective-permute-start.7) | collective-permute-done | bytes 1179680 | tf_op jit(solution)/shard_map/ppermute | solution.py:34
  95.2 12.4 %collective-permute-done.15 = bf16[128,2048]{1,0:T(8,128)(2,1)S(1)} collective-permute-done((bf16[128,2048]{1,0:T(8,128)(2,1)S(1)}, bf16[128,2048]{1,0:T(8,128)(2,1)S(1)}, u32[]{:S(2)}, u32[]{:S(2)}) %collective-permute-start.15) | collective-permute-done | bytes 524320 | tf_op jit(solution)/shard_map/ppermute | solution.py:42
  112.5 21.2 %collective-permute-done.16.refs_1_ = bf16[256,2048]{1,0:T(8,128)(2,1)} collective-permute-done((bf16[256,2048]{1,0:T(8,128)(2,1)S(1)}, bf16[256,2048]{1,0:T(8,128)(2,1)}, u32[]{:S(2)}, u32[]{:S(2)}) %collective-permute-start.16) | collective-permute-done | bytes 1048608 | tf_op jit(solution)/shard_map/ppermute | solution.py:42
  136.3 3.7 fusion.48
  141.3 5.9 collective-permute-done.23
  157.2 9.5 %shard_map.239 = (f32[2048,512]{1,0:T(8,128)S(1)}, bf16[2048,2048]{1,0:T(8,128)(2,1)}) custom-call(bf16[2048,512]{1,0:T(8,128)(2,1)S(1)} %multiply_convert_fusion.1.matrix_ref, bf16[256,2048]{1,0:T(8,128)(2,1)S(1)} %get-tuple-element.145.refs_0_, bf16[256,2048]{1,0:T(8,128)(2,1)} %collective-permute-done.16.refs_1_, ...), custom_call_target="tpu_custom_call" | custom-call | flops 4294967296 | bytes 20971520 | tf_op jit(solution)/shard_map/pallas_call | solution.py:475
  177.0 11.4 %shard_map.240 = bf16[2048,256]{1,0:T(8,128)(2,1)S(1)} custom-call(s32[10]{0:T(128)S(1)} %pad_add_fusion.2.scalars, f32[2,1024,128]{2,1,0:T(8,128)S(1)} %get-tuple-element.439.cos_ref, f32[2,1024,128]{2,1,0:T(8,128)S(1)} %get-tuple-element.440.sine_ref, f32[8,128]{1,0:T(8,128)S(1)} %maximum_maximum_fusion.gain_ref, f32[2048,512]{1,0:T(8,128)S(1)} %copy-done.18), custom_call_target="tpu_custom_call" | custom-call | flops 1342177280 | bytes 12582912 | tf_op jit(solution)/shard_map/pallas_call | solution.py:432
  200.1 3.0 collective-permute-done.27
  206.7 22.6 %collective-permute-done.29 = bf16[256,2048]{1,0:T(8,128)(2,1)S(1)} collective-permute-done((bf16[256,2048]{1,0:T(8,128)(2,1)S(1)}, bf16[256,2048]{1,0:T(8,128)(2,1)S(1)}, u32[]{:S(2)}, u32[]{:S(2)}) %collective-permute-start.29) | collective-permute-done | bytes 1048608 | tf_op jit(solution)/shard_map/ppermute | solution.py:42
  234.3 10.6 %collective-permute-done.31 = bf16[128,2048]{1,0:T(8,128)(2,1)} collective-permute-done((bf16[128,2048]{1,0:T(8,128)(2,1)}, bf16[128,2048]{1,0:T(8,128)(2,1)}, u32[]{:S(2)}, u32[]{:S(2)}) %collective-permute-start.31) | collective-permute-done | bytes 524320 | tf_op jit(solution)/shard_map/ppermute | solution.py:34
  246.2 3.0 multiply_reduce_fusion.5
  251.1 11.6 %collective-permute-done.38 = bf16[128,2048]{1,0:T(8,128)(2,1)S(1)} collective-permute-done((bf16[128,2048]{1,0:T(8,128)(2,1)S(1)}, bf16[128,2048]{1,0:T(8,128)(2,1)S(1)}, u32[]{:S(2)}, u32[]{:S(2)}) %collective-permute-start.38) | collective-permute-done | bytes 524320 | tf_op jit(solution)/shard_map/ppermute | solution.py:42
  267.8 19.5 %collective-permute-done.39.refs_1_ = bf16[256,2048]{1,0:T(8,128)(2,1)S(1)} collective-permute-done((bf16[256,2048]{1,0:T(8,128)(2,1)S(1)}, bf16[256,2048]{1,0:T(8,128)(2,1)S(1)}, u32[]{:S(2)}, u32[]{:S(2)}) %collective-permute-start.39) | collective-permute-done | bytes 1048608 | tf_op jit(solution)/shard_map/ppermute | solution.py:42
  294.0 3.0 all-gather.5.cloned.1.call-done.both_ref.down_ref
  302.0 34.5 %shard_map.242 = (bf16[2048,768]{1,0:T(8,128)(2,1)}, bf16[2048,1536]{1,0:T(8,128)(2,1)}, bf16[2048,2048]{1,0:T(8,128)(2,1)}, bf16[2048,2048]{1,0:T(8,128)(2,1)}) custom-call(bf16[2048,2304]{1,0:T(8,128)(2,1)} %all-gather.5.cloned.1.call-done.both_ref.down_ref, bf16[2048,2304]{1,0:T(8,128)(2,1)} %all-gather.5.cloned.1.call-done.both_ref.down_ref, ...), custom_call_target="tpu_custom_call" | custom-call | flops 19327352832 | bytes 52428800 | tf_op jit(solution)/shard_map/pallas_call | solution.py:563
  336.4 11.4 %convolution_convert_fusion.4 = bf16[2048,768]{1,0:T(8,128)(2,1)} fusion(bf16[2048,2048]{1,0:T(8,128)(2,1)} %get-tuple-element.184, bf16[2048,768]{1,0:T(8,128)(2,1)} %get-tuple-element.199), kind=kOutput, calls=%fused_computation.13 | convolution fusion | flops 6444023808 | bytes 14680064 | tf_op jit(solution)/shard_map/dot_general | solution.py:606
  348.1 8.2 %fusion.12 = bf16[512,2048]{1,0:T(8,128)(2,1)} fusion(bf16[2048,2304]{1,0:T(8,128)(2,1)} %all-gather.5.cloned.1.call-done.both_ref.down_ref, bf16[2048,1536]{1,0:T(8,128)(2,1)} %get-tuple-element.185), kind=kOutput, calls=%fused_computation.18 | convolution fusion | flops 3222274048 | bytes 9961472 | tf_op jit(solution)/shard_map/dot_general | solution.py:115
  356.4 8.2 %fusion.9 = bf16[512,2048]{1,0:T(8,128)(2,1)} fusion(bf16[2048,2304]{1,0:T(8,128)(2,1)} %all-gather.5.cloned.1.call-done.both_ref.down_ref, bf16[2048,1536]{1,0:T(8,128)(2,1)} %get-tuple-element.185), kind=kOutput, calls=%fused_computation.17 | convolution fusion | flops 3222274048 | bytes 9961472 | tf_op jit(solution)/shard_map/dot_general | solution.py:115
  365.4 6.9 %fusion.6 = bf16[1024,2048]{1,0:T(8,128)(2,1)S(1)} fusion(bf16[1024,1536]{1,0:T(8,128)(2,1)S(1)} %slice.885, bf16[2048,2304]{1,0:T(8,128)(2,1)S(1)} %bitcast.220), kind=kOutput, calls=%fused_computation.9 | convolution fusion | flops 6444548096 | bytes 13631488 | tf_op jit(solution)/shard_map/dot_general | solution.py:115
  379.3 17.4 %convolution_convert_fusion = bf16[2048,1536]{1,0:T(8,128)(2,1)} fusion(bf16[2048,2048]{1,0:T(8,128)(2,1)} %get-tuple-element.194, bf16[2048,1536]{1,0:T(8,128)(2,1)S(1)} %bitcast.185), kind=kOutput, calls=%fused_computation | convolution fusion | flops 12888047616 | bytes 20971520 | tf_op jit(solution)/shard_map/dot_general | solution.py:606
  397.2 4.6 collective-permute-done.47
  407.4 10.7 %collective-permute-done.49 = bf16[128,2048]{1,0:T(8,128)(2,1)S(1)} collective-permute-done((bf16[128,2048]{1,0:T(8,128)(2,1)S(1)}, bf16[128,2048]{1,0:T(8,128)(2,1)S(1)}, u32[]{:S(2)}, u32[]{:S(2)}) %collective-permute-start.49) | collective-permute-done | bytes 524320 | tf_op jit(solution)/shard_map/ppermute | solution.py:34
  419.3 3.0 multiply_reduce_fusion
  422.3 2.9 fusion.62
  426.6 10.2 %collective-permute-done.52 = bf16[128,2048]{1,0:T(8,128)(2,1)S(1)} collective-permute-done((bf16[128,2048]{1,0:T(8,128)(2,1)S(1)}, bf16[128,2048]{1,0:T(8,128)(2,1)S(1)}, u32[]{:S(2)}, u32[]{:S(2)}) %collective-permute-start.52) | collective-permute-done | bytes 524320 | tf_op jit(solution)/shard_map/ppermute | solution.py:42
  439.7 3.1 convolution_convert_fusion.9
  442.8 3.1 convolution_convert_fusion.10
  446.0 13.8 %collective-permute-done.53.refs_1_ = bf16[256,2048]{1,0:T(8,128)(2,1)} collective-permute-done((bf16[256,2048]{1,0:T(8,128)(2,1)S(1)}, bf16[256,2048]{1,0:T(8,128)(2,1)}, u32[]{:S(2)}, u32[]{:S(2)}) %collective-permute-start.53) | collective-permute-done | bytes 1048608 | tf_op jit(solution)/shard_map/ppermute | solution.py:42
  460.8 5.2 convolution_convert_fusion.3
  474.8 7.1 %shard_map.243 = (bf16[2048,256]{1,0:T(8,128)(2,1)S(1)}, bf16[2048,2048]{1,0:T(8,128)(2,1)S(1)}) custom-call(bf16[256,2048]{1,0:T(8,128)(2,1)S(1)} %copy-done, bf16[256,2048]{1,0:T(8,128)(2,1)S(1)} %copy-done.2, bf16[256,2048]{1,0:T(8,128)(2,1)} %collective-permute-done.53.refs_1_, bf16[256,2048]{1,0:T(8,128)(2,1)S(1)} %pad_maximum_fusion.13.refs_2_, ...), custom_call_target="tpu_custom_call" | custom-call | flops 2147483648 | bytes 18874368 | tf_op jit(solution)/shard_map/pallas_call | solution.py:475
  482.0 3.8 add_convert_fusion.2
  492.7 21.0 %shard_map.244 = (bf16[2048,512]{1,0:T(8,128)(2,1)S(1)}, f32[2,8,128]{2,1,0:T(8,128)S(1)}) custom-call(s32[10]{0:T(128)S(1)} %pad_add_fusion.2.scalars, f32[2,1024,128]{2,1,0:T(8,128)S(1)} %copy-done.4, f32[2,1024,128]{2,1,0:T(8,128)S(1)} %copy-done.6, f32[8,128]{1,0:T(8,128)S(1)} %maximum_maximum_fusion.gain_ref, f32[2048,512]{1,0:T(8,128)S(1)} %copy-done.19, ...), custom_call_target="tpu_custom_call" | custom-call | flops 3355443200 | bytes 41943040 | tf_op jit(solution)/shard_map/pallas_call | solution.py:432
  513.7 3.6 add_convert_fusion.12
  528.9 8.6 %multiply_convert_fusion = bf16[2048,512]{1,0:T(8,128)(2,1)S(1)} fusion(bf16[2048,2048]{1,0:T(8,128)(2,1)} %get-tuple-element.230, bf16[2048,512]{1,0:T(8,128)(2,1)S(1)} %get-tuple-element.231, f32[2048]{0:T(1024)S(1)} %mul.220), kind=kOutput, calls=%fused_computation.7 | convolution fusion | flops 4297064448 | bytes 12591104 | tf_op jit(solution)/shard_map/dot_general | solution.py:610
  543.7 5.2 add_convert_fusion
  551.5 3.1 add_convert_fusion.10
  554.9 19.4 %collective-permute-done.68 = bf16[256,2048]{1,0:T(8,128)(2,1)S(1)} collective-permute-done((bf16[256,2048]{1,0:T(8,128)(2,1)}, bf16[256,2048]{1,0:T(8,128)(2,1)S(1)}, u32[]{:S(2)}, u32[]{:S(2)}) %collective-permute-start.68) | collective-permute-done | bytes 1048608 | tf_op jit(solution)/shard_map/ppermute | solution.py:42
  582.2 5.7 collective-permute-start.67
  595.8 4.8 broadcast_select_fusion
  601.5 5.4 collective-permute-start.73
  618.4 5.1 collective-permute-done.74.second_ref
  638.9 11.1 %collective-permute-done.80 = bf16[2,128,2304]{2,1,0:T(8,128)(2,1)S(1)} collective-permute-done((bf16[2,128,2304]{2,1,0:T(8,128)(2,1)}, bf16[2,128,2304]{2,1,0:T(8,128)(2,1)S(1)}, u32[]{:S(2)}, u32[]{:S(2)}) %collective-permute-start.80) | collective-permute-done | bytes 1179680 | tf_op jit(solution)/shard_map/ppermute | solution.py:34
  650.6 17.6 %collective-permute-start.81 = (f32[2,136]{1,0:T(2,128)S(1)}, f32[2,136]{1,0:T(2,128)S(1)}, u32[]{:S(2)}, u32[]{:S(2)}) collective-permute-start(f32[2,136]{1,0:T(2,128)S(1)} %fusion.58), channel_id=1, source_target_pairs={{0,4},{2,6},{4,0},{6,2},{1,5},{3,7},{5,1},{7,3},{8,12},{10,14},{12... | collective-permute-start | bytes 3272 | tf_op jit(solution)/shard_map/ppermute | solution.py:136
  (587 shorter events, 209.9 us)
Async XLA Ops:
  7.2 146.4 %all-gather.3.cloned.1.call-start = ((), (), s32[]{:S(2)}) async-start(), calls=%async_computation.3 | async-start | bytes 3932160 | tf_op jit(solution)/shard_map/all_gather | solution.py:128
  9.7 51.2 %collective-permute-start.5 = (bf16[128,2048]{1,0:T(8,128)(2,1)}, bf16[128,2048]{1,0:T(8,128)(2,1)}, u32[]{:S(2)}, u32[]{:S(2)}) collective-permute-start(bf16[128,2048]{1,0:T(8,128)(2,1)} %get-tuple-element.136), channel_id=1, source_target_pairs={{0,2},{1,3},{2,0},{3,1},{4,10},{5,11},{6,8},{7,9},{8,6},{9,7},{10,... | collective-permute-start | bytes 1572872 | tf_op jit(solution)/shard_map/ppermute | solution.py:260
  12.8 50.3 %collective-permute-start.6 = (bf16[128,2048]{1,0:T(8,128)(2,1)}, bf16[128,2048]{1,0:T(8,128)(2,1)}, u32[]{:S(2)}, u32[]{:S(2)}) collective-permute-start(bf16[128,2048]{1,0:T(8,128)(2,1)} %get-tuple-element.135), channel_id=1, source_target_pairs={{0,0},{1,1},{2,2},{3,3},{4,8},{5,9},{6,10},{7,11},{8,4},{9,5},{10,... | collective-permute-start | bytes 1572872 | tf_op jit(solution)/shard_map/ppermute | solution.py:259
  20.5 44.8 %collective-permute-start = (bf16[128,2048]{1,0:T(8,128)(2,1)}, bf16[128,2048]{1,0:T(8,128)(2,1)}, u32[]{:S(2)}, u32[]{:S(2)}) collective-permute-start(bf16[128,2048]{1,0:T(8,128)(2,1)} %get-tuple-element.133), channel_id=1, source_target_pairs={{0,0},{1,1},{2,2},{3,3},{4,8},{5,9},{6,10},{7,11},{8,4},{9,5},{10,... | collective-permute-start | bytes 1572872 | tf_op jit(solution)/shard_map/ppermute | solution.py:259
  46.8 18.6 %collective-permute-start.1 = (bf16[128,2048]{1,0:T(8,128)(2,1)S(1)}, bf16[128,2048]{1,0:T(8,128)(2,1)S(1)}, u32[]{:S(2)}, u32[]{:S(2)}) collective-permute-start(bf16[128,2048]{1,0:T(8,128)(2,1)S(1)} %copy-done.85), channel_id=1, source_target_pairs={{0,2},{1,3},{2,0},{3,1},{4,10},{5,11},{6,8},{7,9},{8,6},{9,7},{10,... | collective-permute-start | bytes 1572872 | tf_op jit(solution)/shard_map/ppermute | solution.py:260
  60.4 27.5 %collective-permute-start.7 = (bf16[2,128,2304]{2,1,0:T(8,128)(2,1)}, bf16[2,128,2304]{2,1,0:T(8,128)(2,1)S(1)}, u32[]{:S(2)}, u32[]{:S(2)}) collective-permute-start(bf16[2,128,2304]{2,1,0:T(8,128)(2,1)} %bitcast.15), channel_id=1, source_target_pairs={{0,16},{16,0},{8,24},{24,8},{1,17},{17,1},{9,25},{25,9},{2,18},{18... | collective-permute-start | bytes 3538952 | tf_op jit(solution)/shard_map/ppermute | solution.py:34
  67.5 229.5 %all-gather.5.cloned.1.call-start = ((), (), s32[]{:S(2)}) async-start(), calls=%async_computation.4 | async-start | bytes 11796480 | tf_op jit(solution)/shard_map/all_gather | solution.py:128
  109.4 24.3 %collective-permute-start.16 = (bf16[256,2048]{1,0:T(8,128)(2,1)S(1)}, bf16[256,2048]{1,0:T(8,128)(2,1)}, u32[]{:S(2)}, u32[]{:S(2)}) collective-permute-start(bf16[256,2048]{1,0:T(8,128)(2,1)S(1)} %get-tuple-element.145.refs_0_), channel_id=1, source_target_pairs={{0,1},{1,0},{2,3},{3,2},{4,5},{5,4},{6,7},{7,6},{8,9},{9,8},{10,11... | collective-permute-start | bytes 3145736 | tf_op jit(solution)/shard_map/ppermute | solution.py:42
  111.0 24.2 %collective-permute-start.17 = (bf16[256,2048]{1,0:T(8,128)(2,1)}, bf16[256,2048]{1,0:T(8,128)(2,1)}, u32[]{:S(2)}, u32[]{:S(2)}) collective-permute-start(bf16[256,2048]{1,0:T(8,128)(2,1)} %get-tuple-element.146.refs_2_), channel_id=1, source_target_pairs={{0,16},{16,0},{8,24},{24,8},{1,17},{17,1},{9,25},{25,9},{2,18},{18... | collective-permute-start | bytes 3145736 | tf_op jit(solution)/shard_map/ppermute | solution.py:34
  111.5 428.0 %reduce-scatter.6.cloned.1.call-start = ((), (), s32[]{:S(2)}) async-start(), calls=%async_computation.6 | async-start | bytes 3932160 | tf_op jit(solution)/shard_map/reduce_scatter | solution.py:132
  140.7 16.0 %collective-permute-start.18 = (bf16[256,2048]{1,0:T(8,128)(2,1)S(1)}, bf16[256,2048]{1,0:T(8,128)(2,1)}, u32[]{:S(2)}, u32[]{:S(2)}) collective-permute-start(bf16[256,2048]{1,0:T(8,128)(2,1)S(1)} %get-tuple-element.145.refs_0_), channel_id=1, source_target_pairs={{0,8},{8,0},{16,24},{24,16},{1,9},{9,1},{17,25},{25,17},{2,10},{10... | collective-permute-start | bytes 3145736 | tf_op jit(solution)/shard_map/ppermute | solution.py:38
  140.7 16.4 %collective-permute-start.20 = (bf16[256,2048]{1,0:T(8,128)(2,1)}, bf16[256,2048]{1,0:T(8,128)(2,1)}, u32[]{:S(2)}, u32[]{:S(2)}) collective-permute-start(bf16[256,2048]{1,0:T(8,128)(2,1)} %get-tuple-element.146.refs_2_), channel_id=1, source_target_pairs={{0,8},{8,0},{16,24},{24,16},{1,9},{9,1},{17,25},{25,17},{2,10},{10... | collective-permute-start | bytes 3145736 | tf_op jit(solution)/shard_map/ppermute | solution.py:38
  141.2 15.9 %collective-permute-start.21 = (bf16[256,2048]{1,0:T(8,128)(2,1)}, bf16[256,2048]{1,0:T(8,128)(2,1)}, u32[]{:S(2)}, u32[]{:S(2)}) collective-permute-start(bf16[256,2048]{1,0:T(8,128)(2,1)} %collective-permute-done.17.refs_3_), channel_id=1, source_target_pairs={{0,8},{8,0},{16,24},{24,16},{1,9},{9,1},{17,25},{25,17},{2,10},{10... | collective-permute-start | bytes 3145736 | tf_op jit(solution)/shard_map/ppermute | solution.py:38
  152.1 41.8 %collective-permute-start.24 = (bf16[256,2048]{1,0:T(8,128)(2,1)}, bf16[256,2048]{1,0:T(8,128)(2,1)}, u32[]{:S(2)}, u32[]{:S(2)}) collective-permute-start(bf16[256,2048]{1,0:T(8,128)(2,1)} %pad_maximum_fusion.8.refs_8_), channel_id=1, source_target_pairs={{0,1},{1,0},{2,3},{3,2},{4,5},{5,4},{6,7},{7,6},{8,9},{9,8},{10,11... | collective-permute-start | bytes 3145736 | tf_op jit(solution)/shard_map/ppermute | solution.py:42
  156.6 37.2 %collective-permute-start.25 = (bf16[256,2048]{1,0:T(8,128)(2,1)}, bf16[256,2048]{1,0:T(8,128)(2,1)}, u32[]{:S(2)}, u32[]{:S(2)}) collective-permute-start(bf16[256,2048]{1,0:T(8,128)(2,1)} %pad_maximum_fusion.9.refs_10_), channel_id=1, source_target_pairs={{0,16},{16,0},{8,24},{24,8},{1,17},{17,1},{9,25},{25,9},{2,18},{18... | collective-permute-start | bytes 3145736 | tf_op jit(solution)/shard_map/ppermute | solution.py:34
  173.8 15.1 %collective-permute-start.26 = (bf16[2,64,2048]{2,1,0:T(8,128)(2,1)}, bf16[2,64,2048]{2,1,0:T(8,128)(2,1)}, u32[]{:S(2)}, u32[]{:S(2)}) collective-permute-start(bf16[2,64,2048]{2,1,0:T(8,128)(2,1)} %get-tuple-element.319), channel_id=1, source_target_pairs={{0,1},{1,0},{2,3},{3,2},{4,5},{5,4},{6,7},{7,6},{8,9},{9,8},{10,11... | collective-permute-start | bytes 1572872 | tf_op jit(solution)/shard_map/ppermute | solution.py:42
  204.1 25.3 %collective-permute-start.29 = (bf16[256,2048]{1,0:T(8,128)(2,1)S(1)}, bf16[256,2048]{1,0:T(8,128)(2,1)S(1)}, u32[]{:S(2)}, u32[]{:S(2)}) collective-permute-start(bf16[256,2048]{1,0:T(8,128)(2,1)S(1)} %get-tuple-element.165), channel_id=1, source_target_pairs={{0,1},{1,0},{2,3},{3,2},{4,5},{5,4},{6,7},{7,6},{8,9},{9,8},{10,11... | collective-permute-start | bytes 3145736 | tf_op jit(solution)/shard_map/ppermute | solution.py:42
  205.2 24.9 %collective-permute-start.30 = (bf16[256,2048]{1,0:T(8,128)(2,1)S(1)}, bf16[256,2048]{1,0:T(8,128)(2,1)S(1)}, u32[]{:S(2)}, u32[]{:S(2)}) collective-permute-start(bf16[256,2048]{1,0:T(8,128)(2,1)S(1)} %get-tuple-element.166), channel_id=1, source_target_pairs={{0,16},{16,0},{8,24},{24,8},{1,17},{17,1},{9,25},{25,9},{2,18},{18... | collective-permute-start | bytes 3145736 | tf_op jit(solution)/shard_map/ppermute | solution.py:34
  233.8 15.7 %collective-permute-start.33 = (bf16[256,2048]{1,0:T(8,128)(2,1)}, bf16[256,2048]{1,0:T(8,128)(2,1)S(1)}, u32[]{:S(2)}, u32[]{:S(2)}) collective-permute-start(bf16[256,2048]{1,0:T(8,128)(2,1)} %pad_maximum_fusion.8.refs_8_), channel_id=1, source_target_pairs={{0,8},{8,0},{16,24},{24,16},{1,9},{9,1},{17,25},{25,17},{2,10},{10... | collective-permute-start | bytes 3145736 | tf_op jit(solution)/shard_map/ppermute | solution.py:38
  233.8 15.7 %collective-permute-start.35 = (bf16[256,2048]{1,0:T(8,128)(2,1)}, bf16[256,2048]{1,0:T(8,128)(2,1)S(1)}, u32[]{:S(2)}, u32[]{:S(2)}) collective-permute-start(bf16[256,2048]{1,0:T(8,128)(2,1)} %pad_maximum_fusion.9.refs_10_), channel_id=1, source_target_pairs={{0,8},{8,0},{16,24},{24,16},{1,9},{9,1},{17,25},{25,17},{2,10},{10... | collective-permute-start | bytes 3145736 | tf_op jit(solution)/shard_map/ppermute | solution.py:38
  234.3 15.2 %collective-permute-start.34 = (bf16[256,2048]{1,0:T(8,128)(2,1)}, bf16[256,2048]{1,0:T(8,128)(2,1)S(1)}, u32[]{:S(2)}, u32[]{:S(2)}) collective-permute-start(bf16[256,2048]{1,0:T(8,128)(2,1)} %collective-permute-done.24.refs_9_), channel_id=1, source_target_pairs={{0,8},{8,0},{16,24},{24,16},{1,9},{9,1},{17,25},{25,17},{2,10},{10... | collective-permute-start | bytes 3145736 | tf_op jit(solution)/shard_map/ppermute | solution.py:38
  263.7 23.6 %collective-permute-start.39 = (bf16[256,2048]{1,0:T(8,128)(2,1)S(1)}, bf16[256,2048]{1,0:T(8,128)(2,1)S(1)}, u32[]{:S(2)}, u32[]{:S(2)}) collective-permute-start(bf16[256,2048]{1,0:T(8,128)(2,1)S(1)} %pad_maximum_fusion.10.refs_0_), channel_id=1, source_target_pairs={{0,1},{1,0},{2,3},{3,2},{4,5},{5,4},{6,7},{7,6},{8,9},{9,8},{10,11... | collective-permute-start | bytes 3145736 | tf_op jit(solution)/shard_map/ppermute | solution.py:42
  264.8 23.8 %collective-permute-start.40 = (bf16[256,2048]{1,0:T(8,128)(2,1)S(1)}, bf16[256,2048]{1,0:T(8,128)(2,1)S(1)}, u32[]{:S(2)}, u32[]{:S(2)}) collective-permute-start(bf16[256,2048]{1,0:T(8,128)(2,1)S(1)} %pad_maximum_fusion.11.refs_2_), channel_id=1, source_target_pairs={{0,16},{16,0},{8,24},{24,8},{1,17},{17,1},{9,25},{25,9},{2,18},{18... | collective-permute-start | bytes 3145736 | tf_op jit(solution)/shard_map/ppermute | solution.py:34
  266.3 24.7 %collective-permute-start.41 = (bf16[256,2048]{1,0:T(8,128)(2,1)S(1)}, bf16[256,2048]{1,0:T(8,128)(2,1)S(1)}, u32[]{:S(2)}, u32[]{:S(2)}) collective-permute-start(bf16[256,2048]{1,0:T(8,128)(2,1)S(1)} %pad_maximum_fusion.10.refs_0_), channel_id=1, source_target_pairs={{0,8},{8,0},{16,24},{24,16},{1,9},{9,1},{17,25},{25,17},{2,10},{10... | collective-permute-start | bytes 3145736 | tf_op jit(solution)/shard_map/ppermute | solution.py:38
  267.3 24.7 %collective-permute-start.43 = (bf16[256,2048]{1,0:T(8,128)(2,1)S(1)}, bf16[256,2048]{1,0:T(8,128)(2,1)S(1)}, u32[]{:S(2)}, u32[]{:S(2)}) collective-permute-start(bf16[256,2048]{1,0:T(8,128)(2,1)S(1)} %pad_maximum_fusion.11.refs_2_), channel_id=1, source_target_pairs={{0,8},{8,0},{16,24},{24,16},{1,9},{9,1},{17,25},{25,17},{2,10},{10... | collective-permute-start | bytes 3145736 | tf_op jit(solution)/shard_map/ppermute | solution.py:38
  347.8 191.7 %reduce-scatter.4.cloned.1.call-start = ((), (), s32[]{:S(2)}) async-start(), calls=%async_computation.5 | async-start | bytes 7864320 | tf_op jit(solution)/shard_map/reduce_scatter | solution.py:132
  356.3 16.0 %collective-permute-start.46 = (bf16[512,2048]{1,0:T(8,128)(2,1)}, bf16[512,2048]{1,0:T(8,128)(2,1)S(1)}, u32[]{:S(2)}, u32[]{:S(2)}) collective-permute-start(bf16[512,2048]{1,0:T(8,128)(2,1)} %fusion.12), channel_id=1, source_target_pairs={{0,8},{8,0},{16,24},{24,16},{1,9},{9,1},{17,25},{25,17},{2,10},{10... | collective-permute-start | bytes 6291464 | tf_op jit(solution)/shard_map/ppermute | solution.py:38
  376.3 25.4 %collective-permute-start.47 = (bf16[256,2048]{1,0:T(8,128)(2,1)}, bf16[256,2048]{1,0:T(8,128)(2,1)}, u32[]{:S(2)}, u32[]{:S(2)}) collective-permute-start(bf16[256,2048]{1,0:T(8,128)(2,1)} %get-tuple-element.189), channel_id=1, source_target_pairs={{0,1},{1,0},{2,3},{3,2},{4,5},{5,4},{6,7},{7,6},{8,9},{9,8},{10,11... | collective-permute-start | bytes 3145736 | tf_op jit(solution)/shard_map/ppermute | solution.py:42
  377.8 25.1 %collective-permute-start.48 = (bf16[256,2048]{1,0:T(8,128)(2,1)}, bf16[256,2048]{1,0:T(8,128)(2,1)}, u32[]{:S(2)}, u32[]{:S(2)}) collective-permute-start(bf16[256,2048]{1,0:T(8,128)(2,1)} %get-tuple-element.190), channel_id=1, source_target_pairs={{0,16},{16,0},{8,24},{24,8},{1,17},{17,1},{9,25},{25,9},{2,18},{18... | collective-permute-start | bytes 3145736 | tf_op jit(solution)/shard_map/ppermute | solution.py:34
  396.7 210.3 %reduce-scatter.8.cloned.1.call-start = ((), (), s32[]{:S(2)}) async-start(), calls=%async_computation.7 | async-start | bytes 3932160 | tf_op jit(solution)/shard_map/reduce_scatter | solution.py:132
  437.7 22.1 %collective-permute-start.53 = (bf16[256,2048]{1,0:T(8,128)(2,1)S(1)}, bf16[256,2048]{1,0:T(8,128)(2,1)}, u32[]{:S(2)}, u32[]{:S(2)}) collective-permute-start(bf16[256,2048]{1,0:T(8,128)(2,1)S(1)} %pad_maximum_fusion.12.refs_0_), channel_id=1, source_target_pairs={{0,1},{1,0},{2,3},{3,2},{4,5},{5,4},{6,7},{7,6},{8,9},{9,8},{10,11... | collective-permute-start | bytes 3145736 | tf_op jit(solution)/shard_map/ppermute | solution.py:42
  438.9 21.4 %collective-permute-start.54 = (bf16[256,2048]{1,0:T(8,128)(2,1)S(1)}, bf16[256,2048]{1,0:T(8,128)(2,1)}, u32[]{:S(2)}, u32[]{:S(2)}) collective-permute-start(bf16[256,2048]{1,0:T(8,128)(2,1)S(1)} %pad_maximum_fusion.13.refs_2_), channel_id=1, source_target_pairs={{0,16},{16,0},{8,24},{24,8},{1,17},{17,1},{9,25},{25,9},{2,18},{18... | collective-permute-start | bytes 3145736 | tf_op jit(solution)/shard_map/ppermute | solution.py:34
  442.8 23.7 %collective-permute-start.59 = (bf16[256,2048]{1,0:T(8,128)(2,1)S(1)}, bf16[256,2048]{1,0:T(8,128)(2,1)S(1)}, u32[]{:S(2)}, u32[]{:S(2)}) collective-permute-start(bf16[256,2048]{1,0:T(8,128)(2,1)S(1)} %pad_maximum_fusion.12.refs_0_), channel_id=1, source_target_pairs={{0,8},{8,0},{16,24},{24,16},{1,9},{9,1},{17,25},{25,17},{2,10},{10... | collective-permute-start | bytes 3145736 | tf_op jit(solution)/shard_map/ppermute | solution.py:38
  460.3 21.6 %collective-permute-start.56 = (bf16[512,2048]{1,0:T(8,128)(2,1)}, bf16[512,2048]{1,0:T(8,128)(2,1)}, u32[]{:S(2)}, u32[]{:S(2)}) collective-permute-start(bf16[512,2048]{1,0:T(8,128)(2,1)} %convolution_convert_fusion.9), channel_id=1, source_target_pairs={{0,8},{8,0},{16,24},{24,16},{1,9},{9,1},{17,25},{25,17},{2,10},{10... | collective-permute-start | bytes 6291464 | tf_op jit(solution)/shard_map/ppermute | solution.py:38
  460.3 21.6 %collective-permute-start.55 = (bf16[512,2048]{1,0:T(8,128)(2,1)}, bf16[512,2048]{1,0:T(8,128)(2,1)}, u32[]{:S(2)}, u32[]{:S(2)}) collective-permute-start(bf16[512,2048]{1,0:T(8,128)(2,1)} %convolution_convert_fusion.10), channel_id=1, source_target_pairs={{0,8},{8,0},{16,24},{24,16},{1,9},{9,1},{17,25},{25,17},{2,10},{10... | collective-permute-start | bytes 6291464 | tf_op jit(solution)/shard_map/ppermute | solution.py:38
  485.8 27.9 %collective-permute-start.57 = (bf16[256,2048]{1,0:T(8,128)(2,1)}, bf16[256,2048]{1,0:T(8,128)(2,1)S(1)}, u32[]{:S(2)}, u32[]{:S(2)}) collective-permute-start(bf16[256,2048]{1,0:T(8,128)(2,1)} %get-tuple-element.214), channel_id=1, source_target_pairs={{0,1},{1,0},{2,3},{3,2},{4,5},{5,4},{6,7},{7,6},{8,9},{9,8},{10,11... | collective-permute-start | bytes 3145736 | tf_op jit(solution)/shard_map/ppermute | solution.py:42
  487.0 26.7 %collective-permute-start.58 = (bf16[256,2048]{1,0:T(8,128)(2,1)}, bf16[256,2048]{1,0:T(8,128)(2,1)}, u32[]{:S(2)}, u32[]{:S(2)}) collective-permute-start(bf16[256,2048]{1,0:T(8,128)(2,1)} %get-tuple-element.215), channel_id=1, source_target_pairs={{0,16},{16,0},{8,24},{24,8},{1,17},{17,1},{9,25},{25,9},{2,18},{18... | collective-permute-start | bytes 3145736 | tf_op jit(solution)/shard_map/ppermute | solution.py:34
  491.8 33.7 %collective-permute-start.79 = (bf16[2,64,2048]{2,1,0:T(8,128)(2,1)}, bf16[2,64,2048]{2,1,0:T(8,128)(2,1)}, u32[]{:S(2)}, u32[]{:S(2)}) collective-permute-start(bf16[2,64,2048]{2,1,0:T(8,128)(2,1)} %get-tuple-element.316), channel_id=1, source_target_pairs={{0,1},{1,0},{2,3},{3,2},{4,5},{5,4},{6,7},{7,6},{8,9},{9,8},{10,11... | collective-permute-start | bytes 1572872 | tf_op jit(solution)/shard_map/ppermute | solution.py:42
  523.7 27.8 %collective-permute-start.63 = (bf16[128,2048]{1,0:T(8,128)(2,1)}, bf16[128,2048]{1,0:T(8,128)(2,1)}, u32[]{:S(2)}, u32[]{:S(2)}) collective-permute-start(bf16[128,2048]{1,0:T(8,128)(2,1)} %get-tuple-element.226), channel_id=1, source_target_pairs={{0,16},{16,0},{8,24},{24,8},{1,17},{17,1},{9,25},{25,9},{2,18},{18... | collective-permute-start | bytes 1572872 | tf_op jit(solution)/shard_map/ppermute | solution.py:34
  524.4 27.2 %collective-permute-start.64 = (bf16[128,2048]{1,0:T(8,128)(2,1)}, bf16[128,2048]{1,0:T(8,128)(2,1)}, u32[]{:S(2)}, u32[]{:S(2)}) collective-permute-start(bf16[128,2048]{1,0:T(8,128)(2,1)} %get-tuple-element.227), channel_id=1, source_target_pairs={{0,1},{1,0},{2,3},{3,2},{4,5},{5,4},{6,7},{7,6},{8,9},{9,8},{10,11... | collective-permute-start | bytes 1572872 | tf_op jit(solution)/shard_map/ppermute | solution.py:42
  549.0 25.3 %collective-permute-start.68 = (bf16[256,2048]{1,0:T(8,128)(2,1)}, bf16[256,2048]{1,0:T(8,128)(2,1)S(1)}, u32[]{:S(2)}, u32[]{:S(2)}) collective-permute-start(bf16[256,2048]{1,0:T(8,128)(2,1)} %get-tuple-element.235), channel_id=1, source_target_pairs={{0,1},{1,0},{2,3},{3,2},{4,5},{5,4},{6,7},{7,6},{8,9},{9,8},{10,11... | collective-permute-start | bytes 3145736 | tf_op jit(solution)/shard_map/ppermute | solution.py:42
  549.8 25.1 %collective-permute-start.69 = (bf16[256,2048]{1,0:T(8,128)(2,1)}, bf16[256,2048]{1,0:T(8,128)(2,1)}, u32[]{:S(2)}, u32[]{:S(2)}) collective-permute-start(bf16[256,2048]{1,0:T(8,128)(2,1)} %get-tuple-element.236), channel_id=1, source_target_pairs={{0,16},{16,0},{8,24},{24,8},{1,17},{17,1},{9,25},{25,9},{2,18},{18... | collective-permute-start | bytes 3145736 | tf_op jit(solution)/shard_map/ppermute | solution.py:34
  581.1 31.7 %collective-permute-start.78 = (bf16[2,128,2304]{2,1,0:T(8,128)(2,1)}, bf16[2,128,2304]{2,1,0:T(8,128)(2,1)}, u32[]{:S(2)}, u32[]{:S(2)}) collective-permute-start(bf16[2,128,2304]{2,1,0:T(8,128)(2,1)} %get-tuple-element.309), channel_id=1, source_target_pairs={{0,8},{8,0},{16,24},{24,16},{1,9},{9,1},{17,25},{25,17},{2,10},{10... | collective-permute-start | bytes 3538952 | tf_op jit(solution)/shard_map/ppermute | solution.py:38
  582.2 29.5 %collective-permute-start.67 = (bf16[128,2048]{1,0:T(8,128)(2,1)}, bf16[128,2048]{1,0:T(8,128)(2,1)}, u32[]{:S(2)}, u32[]{:S(2)}) collective-permute-start(bf16[128,2048]{1,0:T(8,128)(2,1)} %get-tuple-element.318), channel_id=1, source_target_pairs={{0,0},{1,1},{2,2},{3,3},{8,4},{9,5},{10,6},{11,7},{4,8},{5,9},{6,1... | collective-permute-start | bytes 1572872 | tf_op jit(solution)/shard_map/ppermute | solution.py:266
  587.9 28.1 %collective-permute-start.72 = (bf16[128,2048]{1,0:T(8,128)(2,1)}, bf16[128,2048]{1,0:T(8,128)(2,1)}, u32[]{:S(2)}, u32[]{:S(2)}) collective-permute-start(bf16[128,2048]{1,0:T(8,128)(2,1)} %get-tuple-element.317), channel_id=1, source_target_pairs={{2,0},{3,1},{0,2},{1,3},{10,4},{11,5},{8,6},{9,7},{6,8},{7,9},{4,1... | collective-permute-start | bytes 1572872 | tf_op jit(solution)/shard_map/ppermute | solution.py:266
  601.5 16.9 %collective-permute-start.73 = (bf16[128,2048]{1,0:T(8,128)(2,1)}, bf16[128,2048]{1,0:T(8,128)(2,1)}, u32[]{:S(2)}, u32[]{:S(2)}) collective-permute-start(bf16[128,2048]{1,0:T(8,128)(2,1)} %broadcast_select_fusion.1), channel_id=1, source_target_pairs={{0,0},{1,1},{2,2},{3,3},{8,4},{9,5},{10,6},{11,7},{4,8},{5,9},{6,1... | collective-permute-start | bytes 1572872 | tf_op jit(solution)/shard_map/ppermute | solution.py:266
  629.8 20.2 %collective-permute-start.80 = (bf16[2,128,2304]{2,1,0:T(8,128)(2,1)}, bf16[2,128,2304]{2,1,0:T(8,128)(2,1)S(1)}, u32[]{:S(2)}, u32[]{:S(2)}) collective-permute-start(bf16[2,128,2304]{2,1,0:T(8,128)(2,1)} %get-tuple-element.308), channel_id=1, source_target_pairs={{0,16},{16,0},{8,24},{24,8},{1,17},{17,1},{9,25},{25,9},{2,18},{18... | collective-permute-start | bytes 3538952 | tf_op jit(solution)/shard_map/ppermute | solution.py:34
  650.6 19.2 %collective-permute-start.81 = (f32[2,136]{1,0:T(2,128)S(1)}, f32[2,136]{1,0:T(2,128)S(1)}, u32[]{:S(2)}, u32[]{:S(2)}) collective-permute-start(f32[2,136]{1,0:T(2,128)S(1)} %fusion.58), channel_id=1, source_target_pairs={{0,4},{2,6},{4,0},{6,2},{1,5},{3,7},{5,1},{7,3},{8,12},{10,14},{12... | collective-permute-start | bytes 3272 | tf_op jit(solution)/shard_map/ppermute | solution.py:136
  (138 other events, 1293.2 us)
Sparse Core Ops, SparseCore 0:
  67.6 62.3 all-gather.2
  131.6 165.4 all-gather.4
  348.0 58.4 reduce-scatter.5
  408.6 110.7 reduce-scatter.3
  539.7 66.7 reduce-scatter.7

commit v3 on v2

--- a/solution.py
+++ b/solution.py
@@ -520,14 +520,8 @@
             other.start()
 
     per = TOKEN_TILE // size
-    for tile in range(normed_s.shape[0] // TOKEN_TILE):
-
-        @pl.when(at == 0)
-        def _(tile=tile):
-            for piece in range(tile * per, (tile + 1) * per):
-                copies[0][piece].wait()
-                copies[1][piece].wait()
-
+
+    def work(tile):
         rows = slice(tile * TOKEN_TILE, (tile + 1) * TOKEN_TILE)
         both = jnp.dot(normed_s[rows, :], both_ref[...], preferred_element_type=F32)
         gate, upward = both[:, :UNIT_TILE], both[:, UNIT_TILE:]
@@ -538,6 +532,19 @@
         dgate = dhidden * upward * (logistic * (1.0 + gate * (1.0 - logistic)))
         dboth_ref[rows, :UNIT_TILE] = dgate.astype(BF)
         dboth_ref[rows, UNIT_TILE:] = (dhidden * swish).astype(BF)
+
+    @pl.when(at == 0)
+    def _():
+        for tile in range(normed_s.shape[0] // TOKEN_TILE):
+            for piece in range(tile * per, (tile + 1) * per):
+                copies[0][piece].wait()
+                copies[1][piece].wait()
+            work(tile)
+
+    @pl.when(at > 0)
+    def _():
+        for tile in range(normed_s.shape[0] // TOKEN_TILE):
+            work(tile)
 
     if outs:
 
@@ -812,7 +819,7 @@
     own = after(trade(own, c_bit, over_c, 1), attn_wgrad, *third)
     own_got = over_x(pick(own, 1 - x_bit, 0))
     swapped = join(pick(own, x_bit, 0), own_got, x_bit, 0).reshape(4, width // 16, -1)
-    input_grad = keep_rows(*input_got, odd, F32)
+    input_grad = keep_rows(after(input_got[0], own_got), input_got[1], odd, F32)
     gate_parts, upward_parts, down_parts = [], [], []
     for q in range(4):
         for tile in range(quarter // UNIT_TILE):

time: 690 us -> 681 us (0.987)
  waiting for transfers between devices: 249 us -> 267 us
  starting transfers between devices: 96.9 us -> 81.8 us
    ppermute x4, starting transfers between devices: 20.5 us -> 6.12 us  [swap_z(): return lax.ppermute(value, 'blk', [(z, z ^ step) for z in range(4)])]
    reduce_scatter x3, waiting for transfers between devices: 0.06 us -> 12 us  [blk_scatter(): return lax.psum_scatter(partial, 'blk', scatter_dimension=0, tiled=True)]
    ppermute x22, waiting for transfers between devices: 62.8 us -> 74.3 us  [over_x(): return lax.ppermute(value, 'dp', SWAP_X)]
    unnamed x223 -> x221, local copies, waits for them, and re-layouts: 26.4 us -> 27.3 us
  transfers between devices with their start and end apart: 91 -> 91, of which waited for: 43 -> 43; matrix products, arithmetic and copies ran while one was open for 27% -> 26% of each run, Pallas kernels for 9% -> 9%
where the time goes in v3:
time: 681 us; the launch traced here: 673 us
  waiting for transfers between devices  267 us (39%)
  Pallas kernels  92.7 us (14%)
  matrix products  84 us (12%)
  starting transfers between devices  81.8 us (12%)
  other arithmetic  78 us (11%)
  local copies, waits for them, and re-layouts  52.7 us (8%)
  between operations  16.1 us (2%)
    ppermute x22, waiting for transfers between devices, over_y(): return lax.ppermute(value, 'fsdp', SWAP_Y)  153 us
    ppermute x22, waiting for transfers between devices, over_x(): return lax.ppermute(value, 'dp', SWAP_X)  74.3 us
    dot_general x12, matrix products, product(): out = lax.dot_general(part, matrix, dims, preferred_element_type=F32)  46.5 us
    pallas_call x2, Pallas kernels, attend(): pl.pallas_call(functools.partial(attend_back_kernel if back else attend_k...  32.1 us
    dot_general x3, matrix products, wgrad(): lax.dot_general(rows, columns, COLS_C, preferred_element_type=F32)  31.6 us
    pallas_call x1, Pallas kernels, units_pass(): pl.pallas_call(functools.partial(units_kernel, given=given), grid=(tiles,...  29.7 us
    unnamed x221, local copies, waits for them, and re-layouts  27.3 us
    ppermute x22, starting transfers between devices, over_x(): return lax.ppermute(value, 'dp', SWAP_X)  22.3 us
  transfers between devices with their start and end apart: 91, of which 43 were waited for; matrix products, arithmetic and copies ran while one was open for 26% of the time, Pallas kernels for 9%

profile of v3, /device:TPU:0, one launch (start us, length us, event | category | flops | bytes accessed | tf_op | source)
XLA Modules:
  0.0 672.7 jit_solution(12709696962937747481)
XLA Ops:
  9.7 3.0 collective-permute-start.5
  12.8 5.3 collective-permute-start.6
  20.5 5.4 collective-permute-start
  39.0 7.6 %collective-permute-done.3 = bf16[2,2,64,512]{3,2,1,0:T(8,128)(2,1)S(1)} collective-permute-done((bf16[2,2,64,512]{3,2,1,0:T(8,128)(2,1)S(1)}, bf16[2,2,64,512]{3,2,1,0:T(8,128)(2,1)S(1)}, u32[]{:S(2)}, u32[]{:S(2)}) %collective-permute-start.3) | collective-permute-done | bytes 262176 | tf_op jit(solution)/shard_map/ppermute | solution.py:42
  49.0 11.4 %collective-permute-done.12 = f32[2,2,2,144]{3,2,1,0:T(2,128)S(1)} collective-permute-done((f32[2,2,2,144]{3,2,1,0:T(2,128)S(1)}, f32[2,2,2,144]{3,2,1,0:T(2,128)S(1)}, u32[]{:S(2)}, u32[]{:S(2)}) %collective-permute-start.12) | collective-permute-done | bytes 4640 | tf_op jit(solution)/shard_map/ppermute | solution.py:136
  67.5 20.3 %collective-permute-done.7 = bf16[2,128,2304]{2,1,0:T(8,128)(2,1)S(1)} collective-permute-done((bf16[2,128,2304]{2,1,0:T(8,128)(2,1)}, bf16[2,128,2304]{2,1,0:T(8,128)(2,1)S(1)}, u32[]{:S(2)}, u32[]{:S(2)}) %collective-permute-start.7) | collective-permute-done | bytes 1179680 | tf_op jit(solution)/shard_map/ppermute | solution.py:34
  95.1 12.4 %collective-permute-done.15 = bf16[128,2048]{1,0:T(8,128)(2,1)S(1)} collective-permute-done((bf16[128,2048]{1,0:T(8,128)(2,1)S(1)}, bf16[128,2048]{1,0:T(8,128)(2,1)S(1)}, u32[]{:S(2)}, u32[]{:S(2)}) %collective-permute-start.15) | collective-permute-done | bytes 524320 | tf_op jit(solution)/shard_map/ppermute | solution.py:42
  112.8 20.9 %collective-permute-done.16.refs_1_ = bf16[256,2048]{1,0:T(8,128)(2,1)} collective-permute-done((bf16[256,2048]{1,0:T(8,128)(2,1)S(1)}, bf16[256,2048]{1,0:T(8,128)(2,1)}, u32[]{:S(2)}, u32[]{:S(2)}) %collective-permute-start.16) | collective-permute-done | bytes 1048608 | tf_op jit(solution)/shard_map/ppermute | solution.py:42
  136.3 3.7 fusion.48
  141.3 5.9 collective-permute-done.23
  157.1 9.4 %shard_map.239 = (f32[2048,512]{1,0:T(8,128)S(1)}, bf16[2048,2048]{1,0:T(8,128)(2,1)}) custom-call(bf16[2048,512]{1,0:T(8,128)(2,1)S(1)} %multiply_convert_fusion.1.matrix_ref, bf16[256,2048]{1,0:T(8,128)(2,1)S(1)} %get-tuple-element.146.refs_0_, bf16[256,2048]{1,0:T(8,128)(2,1)} %collective-permute-done.16.refs_1_, ...), custom_call_target="tpu_custom_call" | custom-call | flops 4294967296 | bytes 20971520 | tf_op jit(solution)/shard_map/pallas_call | solution.py:475
  176.9 11.1 %shard_map.240 = bf16[2048,256]{1,0:T(8,128)(2,1)S(1)} custom-call(s32[10]{0:T(128)S(1)} %pad_add_fusion.2.scalars, f32[2,1024,128]{2,1,0:T(8,128)S(1)} %get-tuple-element.441.cos_ref, f32[2,1024,128]{2,1,0:T(8,128)S(1)} %get-tuple-element.442.sine_ref, f32[8,128]{1,0:T(8,128)S(1)} %maximum_maximum_fusion.gain_ref, f32[2048,512]{1,0:T(8,128)S(1)} %copy-done.18), custom_call_target="tpu_custom_call" | custom-call | flops 1342177280 | bytes 12582912 | tf_op jit(solution)/shard_map/pallas_call | solution.py:432
  200.1 3.0 collective-permute-done.27
  206.3 23.0 %collective-permute-done.29 = bf16[256,2048]{1,0:T(8,128)(2,1)S(1)} collective-permute-done((bf16[256,2048]{1,0:T(8,128)(2,1)S(1)}, bf16[256,2048]{1,0:T(8,128)(2,1)S(1)}, u32[]{:S(2)}, u32[]{:S(2)}) %collective-permute-start.29) | collective-permute-done | bytes 1048608 | tf_op jit(solution)/shard_map/ppermute | solution.py:42
  233.9 10.7 %collective-permute-done.31 = bf16[128,2048]{1,0:T(8,128)(2,1)} collective-permute-done((bf16[128,2048]{1,0:T(8,128)(2,1)}, bf16[128,2048]{1,0:T(8,128)(2,1)}, u32[]{:S(2)}, u32[]{:S(2)}) %collective-permute-start.31) | collective-permute-done | bytes 524320 | tf_op jit(solution)/shard_map/ppermute | solution.py:34
  245.8 3.0 multiply_reduce_fusion.5
  251.1 11.3 %collective-permute-done.38 = bf16[128,2048]{1,0:T(8,128)(2,1)S(1)} collective-permute-done((bf16[128,2048]{1,0:T(8,128)(2,1)S(1)}, bf16[128,2048]{1,0:T(8,128)(2,1)S(1)}, u32[]{:S(2)}, u32[]{:S(2)}) %collective-permute-start.38) | collective-permute-done | bytes 524320 | tf_op jit(solution)/shard_map/ppermute | solution.py:42
  267.4 20.2 %collective-permute-done.39.refs_1_ = bf16[256,2048]{1,0:T(8,128)(2,1)S(1)} collective-permute-done((bf16[256,2048]{1,0:T(8,128)(2,1)S(1)}, bf16[256,2048]{1,0:T(8,128)(2,1)S(1)}, u32[]{:S(2)}, u32[]{:S(2)}) %collective-permute-start.39) | collective-permute-done | bytes 1048608 | tf_op jit(solution)/shard_map/ppermute | solution.py:42
  293.6 3.4 all-gather.5.cloned.1.call-done.both_ref.down_ref
  301.9 29.7 %shard_map.242 = (bf16[2048,768]{1,0:T(8,128)(2,1)}, bf16[2048,1536]{1,0:T(8,128)(2,1)}, bf16[2048,2048]{1,0:T(8,128)(2,1)}, bf16[2048,2048]{1,0:T(8,128)(2,1)}) custom-call(bf16[2048,2304]{1,0:T(8,128)(2,1)} %all-gather.5.cloned.1.call-done.both_ref.down_ref, bf16[2048,2304]{1,0:T(8,128)(2,1)} %all-gather.5.cloned.1.call-done.both_ref.down_ref, ...), custom_call_target="tpu_custom_call" | custom-call | flops 19327352832 | bytes 52428800 | tf_op jit(solution)/shard_map/pallas_call | solution.py:570
  331.6 11.9 %convolution_convert_fusion.4 = bf16[2048,768]{1,0:T(8,128)(2,1)} fusion(bf16[2048,2048]{1,0:T(8,128)(2,1)} %get-tuple-element.185, bf16[2048,768]{1,0:T(8,128)(2,1)} %get-tuple-element.200), kind=kOutput, calls=%fused_computation.13 | convolution fusion | flops 6444023808 | bytes 14680064 | tf_op jit(solution)/shard_map/dot_general | solution.py:613
  343.6 8.2 %fusion.12 = bf16[512,2048]{1,0:T(8,128)(2,1)} fusion(bf16[2048,2304]{1,0:T(8,128)(2,1)} %all-gather.5.cloned.1.call-done.both_ref.down_ref, bf16[2048,1536]{1,0:T(8,128)(2,1)} %get-tuple-element.186), kind=kOutput, calls=%fused_computation.18 | convolution fusion | flops 3222274048 | bytes 9961472 | tf_op jit(solution)/shard_map/dot_general | solution.py:115
  351.8 8.2 %fusion.9 = bf16[512,2048]{1,0:T(8,128)(2,1)} fusion(bf16[2048,2304]{1,0:T(8,128)(2,1)} %all-gather.5.cloned.1.call-done.both_ref.down_ref, bf16[2048,1536]{1,0:T(8,128)(2,1)} %get-tuple-element.186), kind=kOutput, calls=%fused_computation.17 | convolution fusion | flops 3222274048 | bytes 9961472 | tf_op jit(solution)/shard_map/dot_general | solution.py:115
  360.8 7.1 %fusion.6 = bf16[1024,2048]{1,0:T(8,128)(2,1)S(1)} fusion(bf16[1024,1536]{1,0:T(8,128)(2,1)S(1)} %slice.885, bf16[2048,2304]{1,0:T(8,128)(2,1)S(1)} %bitcast.223), kind=kOutput, calls=%fused_computation.9 | convolution fusion | flops 6444548096 | bytes 13631488 | tf_op jit(solution)/shard_map/dot_general | solution.py:115
  374.9 17.4 %convolution_convert_fusion = bf16[2048,1536]{1,0:T(8,128)(2,1)} fusion(bf16[2048,2048]{1,0:T(8,128)(2,1)} %get-tuple-element.195, bf16[2048,1536]{1,0:T(8,128)(2,1)S(1)} %bitcast.185), kind=kOutput, calls=%fused_computation | convolution fusion | flops 12888047616 | bytes 20971520 | tf_op jit(solution)/shard_map/dot_general | solution.py:613
  392.5 4.8 collective-permute-done.47
  403.0 10.7 %collective-permute-done.49 = bf16[128,2048]{1,0:T(8,128)(2,1)S(1)} collective-permute-done((bf16[128,2048]{1,0:T(8,128)(2,1)S(1)}, bf16[128,2048]{1,0:T(8,128)(2,1)S(1)}, u32[]{:S(2)}, u32[]{:S(2)}) %collective-permute-start.49) | collective-permute-done | bytes 524320 | tf_op jit(solution)/shard_map/ppermute | solution.py:34
  414.8 3.0 multiply_reduce_fusion
  417.9 2.9 fusion.62
  422.2 10.2 %collective-permute-done.52 = bf16[128,2048]{1,0:T(8,128)(2,1)S(1)} collective-permute-done((bf16[128,2048]{1,0:T(8,128)(2,1)S(1)}, bf16[128,2048]{1,0:T(8,128)(2,1)S(1)}, u32[]{:S(2)}, u32[]{:S(2)}) %collective-permute-start.52) | collective-permute-done | bytes 524320 | tf_op jit(solution)/shard_map/ppermute | solution.py:42
  435.3 3.1 convolution_convert_fusion.9
  438.4 3.1 convolution_convert_fusion.10
  441.6 13.8 %collective-permute-done.53.refs_1_ = bf16[256,2048]{1,0:T(8,128)(2,1)} collective-permute-done((bf16[256,2048]{1,0:T(8,128)(2,1)S(1)}, bf16[256,2048]{1,0:T(8,128)(2,1)}, u32[]{:S(2)}, u32[]{:S(2)}) %collective-permute-start.53) | collective-permute-done | bytes 1048608 | tf_op jit(solution)/shard_map/ppermute | solution.py:42
  456.4 5.1 convolution_convert_fusion.3
  470.3 7.2 %shard_map.243 = (bf16[2048,256]{1,0:T(8,128)(2,1)S(1)}, bf16[2048,2048]{1,0:T(8,128)(2,1)S(1)}) custom-call(bf16[256,2048]{1,0:T(8,128)(2,1)S(1)} %copy-done, bf16[256,2048]{1,0:T(8,128)(2,1)S(1)} %copy-done.2, bf16[256,2048]{1,0:T(8,128)(2,1)} %collective-permute-done.53.refs_1_, bf16[256,2048]{1,0:T(8,128)(2,1)S(1)} %pad_maximum_fusion.13.refs_2_, ...), custom_call_target="tpu_custom_call" | custom-call | flops 2147483648 | bytes 18874368 | tf_op jit(solution)/shard_map/pallas_call | solution.py:475
  477.5 3.8 add_convert_fusion.2
  488.1 21.0 %shard_map.244 = (bf16[2048,512]{1,0:T(8,128)(2,1)S(1)}, f32[2,8,128]{2,1,0:T(8,128)S(1)}) custom-call(s32[10]{0:T(128)S(1)} %pad_add_fusion.2.scalars, f32[2,1024,128]{2,1,0:T(8,128)S(1)} %copy-done.4, f32[2,1024,128]{2,1,0:T(8,128)S(1)} %copy-done.6, f32[8,128]{1,0:T(8,128)S(1)} %maximum_maximum_fusion.gain_ref, f32[2048,512]{1,0:T(8,128)S(1)} %copy-done.19, ...), custom_call_target="tpu_custom_call" | custom-call | flops 3355443200 | bytes 41943040 | tf_op jit(solution)/shard_map/pallas_call | solution.py:432
  509.4 3.5 add_convert_fusion.12
  520.6 5.9 multiply_convert_fusion
  528.4 3.5 pad_maximum_fusion
  536.2 3.9 add_convert_fusion
  544.2 3.1 add_convert_fusion.10
  547.3 18.0 %collective-permute-done.68 = bf16[256,2048]{1,0:T(8,128)(2,1)S(1)} collective-permute-done((bf16[256,2048]{1,0:T(8,128)(2,1)S(1)}, bf16[256,2048]{1,0:T(8,128)(2,1)S(1)}, u32[]{:S(2)}, u32[]{:S(2)}) %collective-permute-start.68) | collective-permute-done | bytes 1048608 | tf_op jit(solution)/shard_map/ppermute | solution.py:42
  571.7 5.3 collective-permute-start.67
  586.9 4.9 broadcast_select_fusion
  592.0 12.0 %reduce-scatter.8.cloned.1.call-done = bf16[768,512]{1,0:T(8,128)(2,1)} async-done(((bf16[3072,512]{1,0:T(8,128)(2,1)}), bf16[768,512]{1,0:T(8,128)(2,1)}) %reduce-scatter.8.cloned.1.call-update) | async-done | bytes 786448 | tf_op jit(solution)/shard_map/reduce_scatter | solution.py:132
  609.3 5.5 collective-permute-start.73
  631.8 20.5 %collective-permute-done.76 = bf16[2,128,2304]{2,1,0:T(8,128)(2,1)S(1)} collective-permute-done((bf16[2,128,2304]{2,1,0:T(8,128)(2,1)}, bf16[2,128,2304]{2,1,0:T(8,128)(2,1)S(1)}, u32[]{:S(2)}, u32[]{:S(2)}) %collective-permute-start.76) | collective-permute-done | bytes 1179680 | tf_op jit(solution)/shard_map/ppermute | solution.py:34
  (586 shorter events, 208.4 us)
Async XLA Ops:
  7.2 146.3 %all-gather.3.cloned.1.call-start = ((), (), s32[]{:S(2)}) async-start(), calls=%async_computation.3 | async-start | bytes 3932160 | tf_op jit(solution)/shard_map/all_gather | solution.py:128
  9.7 51.2 %collective-permute-start.5 = (bf16[128,2048]{1,0:T(8,128)(2,1)}, bf16[128,2048]{1,0:T(8,128)(2,1)}, u32[]{:S(2)}, u32[]{:S(2)}) collective-permute-start(bf16[128,2048]{1,0:T(8,128)(2,1)} %get-tuple-element.137), channel_id=1, source_target_pairs={{0,2},{1,3},{2,0},{3,1},{4,10},{5,11},{6,8},{7,9},{8,6},{9,7},{10,... | collective-permute-start | bytes 1572872 | tf_op jit(solution)/shard_map/ppermute | solution.py:260
  12.8 50.3 %collective-permute-start.6 = (bf16[128,2048]{1,0:T(8,128)(2,1)}, bf16[128,2048]{1,0:T(8,128)(2,1)}, u32[]{:S(2)}, u32[]{:S(2)}) collective-permute-start(bf16[128,2048]{1,0:T(8,128)(2,1)} %get-tuple-element.136), channel_id=1, source_target_pairs={{0,0},{1,1},{2,2},{3,3},{4,8},{5,9},{6,10},{7,11},{8,4},{9,5},{10,... | collective-permute-start | bytes 1572872 | tf_op jit(solution)/shard_map/ppermute | solution.py:259
  20.5 44.8 %collective-permute-start = (bf16[128,2048]{1,0:T(8,128)(2,1)}, bf16[128,2048]{1,0:T(8,128)(2,1)}, u32[]{:S(2)}, u32[]{:S(2)}) collective-permute-start(bf16[128,2048]{1,0:T(8,128)(2,1)} %get-tuple-element.134), channel_id=1, source_target_pairs={{0,0},{1,1},{2,2},{3,3},{4,8},{5,9},{6,10},{7,11},{8,4},{9,5},{10,... | collective-permute-start | bytes 1572872 | tf_op jit(solution)/shard_map/ppermute | solution.py:259
  46.7 18.5 %collective-permute-start.1 = (bf16[128,2048]{1,0:T(8,128)(2,1)S(1)}, bf16[128,2048]{1,0:T(8,128)(2,1)S(1)}, u32[]{:S(2)}, u32[]{:S(2)}) collective-permute-start(bf16[128,2048]{1,0:T(8,128)(2,1)S(1)} %copy-done.82), channel_id=1, source_target_pairs={{0,2},{1,3},{2,0},{3,1},{4,10},{5,11},{6,8},{7,9},{8,6},{9,7},{10,... | collective-permute-start | bytes 1572872 | tf_op jit(solution)/shard_map/ppermute | solution.py:260
  60.3 27.5 %collective-permute-start.7 = (bf16[2,128,2304]{2,1,0:T(8,128)(2,1)}, bf16[2,128,2304]{2,1,0:T(8,128)(2,1)S(1)}, u32[]{:S(2)}, u32[]{:S(2)}) collective-permute-start(bf16[2,128,2304]{2,1,0:T(8,128)(2,1)} %bitcast.15), channel_id=1, source_target_pairs={{0,16},{16,0},{8,24},{24,8},{1,17},{17,1},{9,25},{25,9},{2,18},{18... | collective-permute-start | bytes 3538952 | tf_op jit(solution)/shard_map/ppermute | solution.py:34
  67.5 229.6 %all-gather.5.cloned.1.call-start = ((), (), s32[]{:S(2)}) async-start(), calls=%async_computation.4 | async-start | bytes 11796480 | tf_op jit(solution)/shard_map/all_gather | solution.py:128
  93.5 14.0 %collective-permute-start.15 = (bf16[128,2048]{1,0:T(8,128)(2,1)S(1)}, bf16[128,2048]{1,0:T(8,128)(2,1)S(1)}, u32[]{:S(2)}, u32[]{:S(2)}) collective-permute-start(bf16[128,2048]{1,0:T(8,128)(2,1)S(1)} %fusion.28), channel_id=1, source_target_pairs={{0,1},{1,0},{2,3},{3,2},{4,5},{5,4},{6,7},{7,6},{8,9},{9,8},{10,11... | collective-permute-start | bytes 1572872 | tf_op jit(solution)/shard_map/ppermute | solution.py:42
  94.5 13.8 %collective-permute-start.14 = (bf16[128,2048]{1,0:T(8,128)(2,1)S(1)}, bf16[128,2048]{1,0:T(8,128)(2,1)S(1)}, u32[]{:S(2)}, u32[]{:S(2)}) collective-permute-start(bf16[128,2048]{1,0:T(8,128)(2,1)S(1)} %fusion.24), channel_id=1, source_target_pairs={{0,16},{16,0},{8,24},{24,8},{1,17},{17,1},{9,25},{25,9},{2,18},{18... | collective-permute-start | bytes 1572872 | tf_op jit(solution)/shard_map/ppermute | solution.py:34
  109.4 24.3 %collective-permute-start.16 = (bf16[256,2048]{1,0:T(8,128)(2,1)S(1)}, bf16[256,2048]{1,0:T(8,128)(2,1)}, u32[]{:S(2)}, u32[]{:S(2)}) collective-permute-start(bf16[256,2048]{1,0:T(8,128)(2,1)S(1)} %get-tuple-element.146.refs_0_), channel_id=1, source_target_pairs={{0,1},{1,0},{2,3},{3,2},{4,5},{5,4},{6,7},{7,6},{8,9},{9,8},{10,11... | collective-permute-start | bytes 3145736 | tf_op jit(solution)/shard_map/ppermute | solution.py:42
  110.9 24.2 %collective-permute-start.17 = (bf16[256,2048]{1,0:T(8,128)(2,1)}, bf16[256,2048]{1,0:T(8,128)(2,1)}, u32[]{:S(2)}, u32[]{:S(2)}) collective-permute-start(bf16[256,2048]{1,0:T(8,128)(2,1)} %get-tuple-element.147.refs_2_), channel_id=1, source_target_pairs={{0,16},{16,0},{8,24},{24,8},{1,17},{17,1},{9,25},{25,9},{2,18},{18... | collective-permute-start | bytes 3145736 | tf_op jit(solution)/shard_map/ppermute | solution.py:34
  111.5 420.8 %reduce-scatter.6.cloned.1.call-start = ((), (), s32[]{:S(2)}) async-start(), calls=%async_computation.6 | async-start | bytes 3932160 | tf_op jit(solution)/shard_map/reduce_scatter | solution.py:132
  140.6 16.0 %collective-permute-start.18 = (bf16[256,2048]{1,0:T(8,128)(2,1)S(1)}, bf16[256,2048]{1,0:T(8,128)(2,1)}, u32[]{:S(2)}, u32[]{:S(2)}) collective-permute-start(bf16[256,2048]{1,0:T(8,128)(2,1)S(1)} %get-tuple-element.146.refs_0_), channel_id=1, source_target_pairs={{0,8},{8,0},{16,24},{24,16},{1,9},{9,1},{17,25},{25,17},{2,10},{10... | collective-permute-start | bytes 3145736 | tf_op jit(solution)/shard_map/ppermute | solution.py:38
  140.7 16.4 %collective-permute-start.20 = (bf16[256,2048]{1,0:T(8,128)(2,1)}, bf16[256,2048]{1,0:T(8,128)(2,1)}, u32[]{:S(2)}, u32[]{:S(2)}) collective-permute-start(bf16[256,2048]{1,0:T(8,128)(2,1)} %get-tuple-element.147.refs_2_), channel_id=1, source_target_pairs={{0,8},{8,0},{16,24},{24,16},{1,9},{9,1},{17,25},{25,17},{2,10},{10... | collective-permute-start | bytes 3145736 | tf_op jit(solution)/shard_map/ppermute | solution.py:38
  141.2 15.9 %collective-permute-start.21 = (bf16[256,2048]{1,0:T(8,128)(2,1)}, bf16[256,2048]{1,0:T(8,128)(2,1)}, u32[]{:S(2)}, u32[]{:S(2)}) collective-permute-start(bf16[256,2048]{1,0:T(8,128)(2,1)} %collective-permute-done.17.refs_3_), channel_id=1, source_target_pairs={{0,8},{8,0},{16,24},{24,16},{1,9},{9,1},{17,25},{25,17},{2,10},{10... | collective-permute-start | bytes 3145736 | tf_op jit(solution)/shard_map/ppermute | solution.py:38
  152.0 41.8 %collective-permute-start.24 = (bf16[256,2048]{1,0:T(8,128)(2,1)}, bf16[256,2048]{1,0:T(8,128)(2,1)}, u32[]{:S(2)}, u32[]{:S(2)}) collective-permute-start(bf16[256,2048]{1,0:T(8,128)(2,1)} %pad_maximum_fusion.8.refs_8_), channel_id=1, source_target_pairs={{0,1},{1,0},{2,3},{3,2},{4,5},{5,4},{6,7},{7,6},{8,9},{9,8},{10,11... | collective-permute-start | bytes 3145736 | tf_op jit(solution)/shard_map/ppermute | solution.py:42
  156.6 37.2 %collective-permute-start.25 = (bf16[256,2048]{1,0:T(8,128)(2,1)}, bf16[256,2048]{1,0:T(8,128)(2,1)}, u32[]{:S(2)}, u32[]{:S(2)}) collective-permute-start(bf16[256,2048]{1,0:T(8,128)(2,1)} %pad_maximum_fusion.9.refs_10_), channel_id=1, source_target_pairs={{0,16},{16,0},{8,24},{24,8},{1,17},{17,1},{9,25},{25,9},{2,18},{18... | collective-permute-start | bytes 3145736 | tf_op jit(solution)/shard_map/ppermute | solution.py:34
  173.7 15.2 %collective-permute-start.26 = (bf16[2,64,2048]{2,1,0:T(8,128)(2,1)}, bf16[2,64,2048]{2,1,0:T(8,128)(2,1)}, u32[]{:S(2)}, u32[]{:S(2)}) collective-permute-start(bf16[2,64,2048]{2,1,0:T(8,128)(2,1)} %get-tuple-element.321), channel_id=1, source_target_pairs={{0,1},{1,0},{2,3},{3,2},{4,5},{5,4},{6,7},{7,6},{8,9},{9,8},{10,11... | collective-permute-start | bytes 1572872 | tf_op jit(solution)/shard_map/ppermute | solution.py:42
  204.0 25.3 %collective-permute-start.29 = (bf16[256,2048]{1,0:T(8,128)(2,1)S(1)}, bf16[256,2048]{1,0:T(8,128)(2,1)S(1)}, u32[]{:S(2)}, u32[]{:S(2)}) collective-permute-start(bf16[256,2048]{1,0:T(8,128)(2,1)S(1)} %get-tuple-element.166), channel_id=1, source_target_pairs={{0,1},{1,0},{2,3},{3,2},{4,5},{5,4},{6,7},{7,6},{8,9},{9,8},{10,11... | collective-permute-start | bytes 3145736 | tf_op jit(solution)/shard_map/ppermute | solution.py:42
  204.8 24.9 %collective-permute-start.30 = (bf16[256,2048]{1,0:T(8,128)(2,1)S(1)}, bf16[256,2048]{1,0:T(8,128)(2,1)S(1)}, u32[]{:S(2)}, u32[]{:S(2)}) collective-permute-start(bf16[256,2048]{1,0:T(8,128)(2,1)S(1)} %get-tuple-element.167), channel_id=1, source_target_pairs={{0,16},{16,0},{8,24},{24,8},{1,17},{17,1},{9,25},{25,9},{2,18},{18... | collective-permute-start | bytes 3145736 | tf_op jit(solution)/shard_map/ppermute | solution.py:34
  233.4 15.7 %collective-permute-start.33 = (bf16[256,2048]{1,0:T(8,128)(2,1)}, bf16[256,2048]{1,0:T(8,128)(2,1)S(1)}, u32[]{:S(2)}, u32[]{:S(2)}) collective-permute-start(bf16[256,2048]{1,0:T(8,128)(2,1)} %pad_maximum_fusion.8.refs_8_), channel_id=1, source_target_pairs={{0,8},{8,0},{16,24},{24,16},{1,9},{9,1},{17,25},{25,17},{2,10},{10... | collective-permute-start | bytes 3145736 | tf_op jit(solution)/shard_map/ppermute | solution.py:38
  233.4 15.7 %collective-permute-start.35 = (bf16[256,2048]{1,0:T(8,128)(2,1)}, bf16[256,2048]{1,0:T(8,128)(2,1)S(1)}, u32[]{:S(2)}, u32[]{:S(2)}) collective-permute-start(bf16[256,2048]{1,0:T(8,128)(2,1)} %pad_maximum_fusion.9.refs_10_), channel_id=1, source_target_pairs={{0,8},{8,0},{16,24},{24,16},{1,9},{9,1},{17,25},{25,17},{2,10},{10... | collective-permute-start | bytes 3145736 | tf_op jit(solution)/shard_map/ppermute | solution.py:38
  233.9 15.2 %collective-permute-start.34 = (bf16[256,2048]{1,0:T(8,128)(2,1)}, bf16[256,2048]{1,0:T(8,128)(2,1)S(1)}, u32[]{:S(2)}, u32[]{:S(2)}) collective-permute-start(bf16[256,2048]{1,0:T(8,128)(2,1)} %collective-permute-done.24.refs_9_), channel_id=1, source_target_pairs={{0,8},{8,0},{16,24},{24,16},{1,9},{9,1},{17,25},{25,17},{2,10},{10... | collective-permute-start | bytes 3145736 | tf_op jit(solution)/shard_map/ppermute | solution.py:38
  263.7 23.9 %collective-permute-start.39 = (bf16[256,2048]{1,0:T(8,128)(2,1)S(1)}, bf16[256,2048]{1,0:T(8,128)(2,1)S(1)}, u32[]{:S(2)}, u32[]{:S(2)}) collective-permute-start(bf16[256,2048]{1,0:T(8,128)(2,1)S(1)} %pad_maximum_fusion.10.refs_0_), channel_id=1, source_target_pairs={{0,1},{1,0},{2,3},{3,2},{4,5},{5,4},{6,7},{7,6},{8,9},{9,8},{10,11... | collective-permute-start | bytes 3145736 | tf_op jit(solution)/shard_map/ppermute | solution.py:42
  264.5 23.7 %collective-permute-start.40 = (bf16[256,2048]{1,0:T(8,128)(2,1)S(1)}, bf16[256,2048]{1,0:T(8,128)(2,1)S(1)}, u32[]{:S(2)}, u32[]{:S(2)}) collective-permute-start(bf16[256,2048]{1,0:T(8,128)(2,1)S(1)} %pad_maximum_fusion.11.refs_2_), channel_id=1, source_target_pairs={{0,16},{16,0},{8,24},{24,8},{1,17},{17,1},{9,25},{25,9},{2,18},{18... | collective-permute-start | bytes 3145736 | tf_op jit(solution)/shard_map/ppermute | solution.py:34
  266.0 24.7 %collective-permute-start.41 = (bf16[256,2048]{1,0:T(8,128)(2,1)S(1)}, bf16[256,2048]{1,0:T(8,128)(2,1)S(1)}, u32[]{:S(2)}, u32[]{:S(2)}) collective-permute-start(bf16[256,2048]{1,0:T(8,128)(2,1)S(1)} %pad_maximum_fusion.10.refs_0_), channel_id=1, source_target_pairs={{0,8},{8,0},{16,24},{24,16},{1,9},{9,1},{17,25},{25,17},{2,10},{10... | collective-permute-start | bytes 3145736 | tf_op jit(solution)/shard_map/ppermute | solution.py:38
  266.9 24.7 %collective-permute-start.43 = (bf16[256,2048]{1,0:T(8,128)(2,1)S(1)}, bf16[256,2048]{1,0:T(8,128)(2,1)S(1)}, u32[]{:S(2)}, u32[]{:S(2)}) collective-permute-start(bf16[256,2048]{1,0:T(8,128)(2,1)S(1)} %pad_maximum_fusion.11.refs_2_), channel_id=1, source_target_pairs={{0,8},{8,0},{16,24},{24,16},{1,9},{9,1},{17,25},{25,17},{2,10},{10... | collective-permute-start | bytes 3145736 | tf_op jit(solution)/shard_map/ppermute | solution.py:38
  343.5 188.8 %reduce-scatter.4.cloned.1.call-start = ((), (), s32[]{:S(2)}) async-start(), calls=%async_computation.5 | async-start | bytes 7864320 | tf_op jit(solution)/shard_map/reduce_scatter | solution.py:132
  351.7 16.2 %collective-permute-start.46 = (bf16[512,2048]{1,0:T(8,128)(2,1)}, bf16[512,2048]{1,0:T(8,128)(2,1)S(1)}, u32[]{:S(2)}, u32[]{:S(2)}) collective-permute-start(bf16[512,2048]{1,0:T(8,128)(2,1)} %fusion.12), channel_id=1, source_target_pairs={{0,8},{8,0},{16,24},{24,16},{1,9},{9,1},{17,25},{25,17},{2,10},{10... | collective-permute-start | bytes 6291464 | tf_op jit(solution)/shard_map/ppermute | solution.py:38
  371.9 25.4 %collective-permute-start.47 = (bf16[256,2048]{1,0:T(8,128)(2,1)}, bf16[256,2048]{1,0:T(8,128)(2,1)}, u32[]{:S(2)}, u32[]{:S(2)}) collective-permute-start(bf16[256,2048]{1,0:T(8,128)(2,1)} %get-tuple-element.190), channel_id=1, source_target_pairs={{0,1},{1,0},{2,3},{3,2},{4,5},{5,4},{6,7},{7,6},{8,9},{9,8},{10,11... | collective-permute-start | bytes 3145736 | tf_op jit(solution)/shard_map/ppermute | solution.py:42
  373.4 25.1 %collective-permute-start.48 = (bf16[256,2048]{1,0:T(8,128)(2,1)}, bf16[256,2048]{1,0:T(8,128)(2,1)}, u32[]{:S(2)}, u32[]{:S(2)}) collective-permute-start(bf16[256,2048]{1,0:T(8,128)(2,1)} %get-tuple-element.191), channel_id=1, source_target_pairs={{0,16},{16,0},{8,24},{24,8},{1,17},{17,1},{9,25},{25,9},{2,18},{18... | collective-permute-start | bytes 3145736 | tf_op jit(solution)/shard_map/ppermute | solution.py:34
  392.3 211.7 %reduce-scatter.8.cloned.1.call-start = ((), (), s32[]{:S(2)}) async-start(), calls=%async_computation.7 | async-start | bytes 3932160 | tf_op jit(solution)/shard_map/reduce_scatter | solution.py:132
  433.3 22.1 %collective-permute-start.53 = (bf16[256,2048]{1,0:T(8,128)(2,1)S(1)}, bf16[256,2048]{1,0:T(8,128)(2,1)}, u32[]{:S(2)}, u32[]{:S(2)}) collective-permute-start(bf16[256,2048]{1,0:T(8,128)(2,1)S(1)} %pad_maximum_fusion.12.refs_0_), channel_id=1, source_target_pairs={{0,1},{1,0},{2,3},{3,2},{4,5},{5,4},{6,7},{7,6},{8,9},{9,8},{10,11... | collective-permute-start | bytes 3145736 | tf_op jit(solution)/shard_map/ppermute | solution.py:42
  434.4 21.4 %collective-permute-start.54 = (bf16[256,2048]{1,0:T(8,128)(2,1)S(1)}, bf16[256,2048]{1,0:T(8,128)(2,1)}, u32[]{:S(2)}, u32[]{:S(2)}) collective-permute-start(bf16[256,2048]{1,0:T(8,128)(2,1)S(1)} %pad_maximum_fusion.13.refs_2_), channel_id=1, source_target_pairs={{0,16},{16,0},{8,24},{24,8},{1,17},{17,1},{9,25},{25,9},{2,18},{18... | collective-permute-start | bytes 3145736 | tf_op jit(solution)/shard_map/ppermute | solution.py:34
  438.4 23.5 %collective-permute-start.59 = (bf16[256,2048]{1,0:T(8,128)(2,1)S(1)}, bf16[256,2048]{1,0:T(8,128)(2,1)S(1)}, u32[]{:S(2)}, u32[]{:S(2)}) collective-permute-start(bf16[256,2048]{1,0:T(8,128)(2,1)S(1)} %pad_maximum_fusion.12.refs_0_), channel_id=1, source_target_pairs={{0,8},{8,0},{16,24},{24,16},{1,9},{9,1},{17,25},{25,17},{2,10},{10... | collective-permute-start | bytes 3145736 | tf_op jit(solution)/shard_map/ppermute | solution.py:38
  455.9 21.6 %collective-permute-start.56 = (bf16[512,2048]{1,0:T(8,128)(2,1)}, bf16[512,2048]{1,0:T(8,128)(2,1)}, u32[]{:S(2)}, u32[]{:S(2)}) collective-permute-start(bf16[512,2048]{1,0:T(8,128)(2,1)} %convolution_convert_fusion.9), channel_id=1, source_target_pairs={{0,8},{8,0},{16,24},{24,16},{1,9},{9,1},{17,25},{25,17},{2,10},{10... | collective-permute-start | bytes 6291464 | tf_op jit(solution)/shard_map/ppermute | solution.py:38
  455.9 21.6 %collective-permute-start.55 = (bf16[512,2048]{1,0:T(8,128)(2,1)}, bf16[512,2048]{1,0:T(8,128)(2,1)}, u32[]{:S(2)}, u32[]{:S(2)}) collective-permute-start(bf16[512,2048]{1,0:T(8,128)(2,1)} %convolution_convert_fusion.10), channel_id=1, source_target_pairs={{0,8},{8,0},{16,24},{24,16},{1,9},{9,1},{17,25},{25,17},{2,10},{10... | collective-permute-start | bytes 6291464 | tf_op jit(solution)/shard_map/ppermute | solution.py:38
  481.3 28.0 %collective-permute-start.57 = (bf16[256,2048]{1,0:T(8,128)(2,1)}, bf16[256,2048]{1,0:T(8,128)(2,1)}, u32[]{:S(2)}, u32[]{:S(2)}) collective-permute-start(bf16[256,2048]{1,0:T(8,128)(2,1)} %get-tuple-element.215), channel_id=1, source_target_pairs={{0,1},{1,0},{2,3},{3,2},{4,5},{5,4},{6,7},{7,6},{8,9},{9,8},{10,11... | collective-permute-start | bytes 3145736 | tf_op jit(solution)/shard_map/ppermute | solution.py:42
  482.6 26.8 %collective-permute-start.58 = (bf16[256,2048]{1,0:T(8,128)(2,1)}, bf16[256,2048]{1,0:T(8,128)(2,1)}, u32[]{:S(2)}, u32[]{:S(2)}) collective-permute-start(bf16[256,2048]{1,0:T(8,128)(2,1)} %get-tuple-element.216), channel_id=1, source_target_pairs={{0,16},{16,0},{8,24},{24,8},{1,17},{17,1},{9,25},{25,9},{2,18},{18... | collective-permute-start | bytes 3145736 | tf_op jit(solution)/shard_map/ppermute | solution.py:34
  487.3 40.3 %collective-permute-start.75 = (bf16[2,64,2048]{2,1,0:T(8,128)(2,1)}, bf16[2,64,2048]{2,1,0:T(8,128)(2,1)S(1)}, u32[]{:S(2)}, u32[]{:S(2)}) collective-permute-start(bf16[2,64,2048]{2,1,0:T(8,128)(2,1)} %get-tuple-element.318), channel_id=1, source_target_pairs={{0,1},{1,0},{2,3},{3,2},{4,5},{5,4},{6,7},{7,6},{8,9},{9,8},{10,11... | collective-permute-start | bytes 1572872 | tf_op jit(solution)/shard_map/ppermute | solution.py:42
  540.1 25.2 %collective-permute-start.68 = (bf16[256,2048]{1,0:T(8,128)(2,1)S(1)}, bf16[256,2048]{1,0:T(8,128)(2,1)S(1)}, u32[]{:S(2)}, u32[]{:S(2)}) collective-permute-start(bf16[256,2048]{1,0:T(8,128)(2,1)S(1)} %get-tuple-element.236), channel_id=1, source_target_pairs={{0,1},{1,0},{2,3},{3,2},{4,5},{5,4},{6,7},{7,6},{8,9},{9,8},{10,11... | collective-permute-start | bytes 3145736 | tf_op jit(solution)/shard_map/ppermute | solution.py:42
  541.1 24.8 %collective-permute-start.69 = (bf16[256,2048]{1,0:T(8,128)(2,1)S(1)}, bf16[256,2048]{1,0:T(8,128)(2,1)S(1)}, u32[]{:S(2)}, u32[]{:S(2)}) collective-permute-start(bf16[256,2048]{1,0:T(8,128)(2,1)S(1)} %get-tuple-element.237), channel_id=1, source_target_pairs={{0,16},{16,0},{8,24},{24,8},{1,17},{17,1},{9,25},{25,9},{2,18},{18... | collective-permute-start | bytes 3145736 | tf_op jit(solution)/shard_map/ppermute | solution.py:34
  542.9 34.2 %collective-permute-start.74 = (bf16[2,128,2304]{2,1,0:T(8,128)(2,1)S(1)}, bf16[2,128,2304]{2,1,0:T(8,128)(2,1)S(1)}, u32[]{:S(2)}, u32[]{:S(2)}) collective-permute-start(bf16[2,128,2304]{2,1,0:T(8,128)(2,1)S(1)} %get-tuple-element.311), channel_id=1, source_target_pairs={{0,8},{8,0},{16,24},{24,16},{1,9},{9,1},{17,25},{25,17},{2,10},{10... | collective-permute-start | bytes 3538952 | tf_op jit(solution)/shard_map/ppermute | solution.py:38
  571.7 43.2 %collective-permute-start.67 = (bf16[128,2048]{1,0:T(8,128)(2,1)}, bf16[128,2048]{1,0:T(8,128)(2,1)}, u32[]{:S(2)}, u32[]{:S(2)}) collective-permute-start(bf16[128,2048]{1,0:T(8,128)(2,1)} %get-tuple-element.320), channel_id=1, source_target_pairs={{0,0},{1,1},{2,2},{3,3},{8,4},{9,5},{10,6},{11,7},{4,8},{5,9},{6,1... | collective-permute-start | bytes 1572872 | tf_op jit(solution)/shard_map/ppermute | solution.py:266
  577.1 37.9 %collective-permute-start.72 = (bf16[128,2048]{1,0:T(8,128)(2,1)}, bf16[128,2048]{1,0:T(8,128)(2,1)}, u32[]{:S(2)}, u32[]{:S(2)}) collective-permute-start(bf16[128,2048]{1,0:T(8,128)(2,1)} %get-tuple-element.319), channel_id=1, source_target_pairs={{2,0},{3,1},{0,2},{1,3},{10,4},{11,5},{8,6},{9,7},{6,8},{7,9},{4,1... | collective-permute-start | bytes 1572872 | tf_op jit(solution)/shard_map/ppermute | solution.py:266
  609.3 52.7 %collective-permute-start.73 = (bf16[128,2048]{1,0:T(8,128)(2,1)}, bf16[128,2048]{1,0:T(8,128)(2,1)}, u32[]{:S(2)}, u32[]{:S(2)}) collective-permute-start(bf16[128,2048]{1,0:T(8,128)(2,1)} %broadcast_select_fusion.1), channel_id=1, source_target_pairs={{0,0},{1,1},{2,2},{3,3},{8,4},{9,5},{10,6},{11,7},{4,8},{5,9},{6,1... | collective-permute-start | bytes 1572872 | tf_op jit(solution)/shard_map/ppermute | solution.py:266
  614.9 47.2 %collective-permute-start.77 = (bf16[128,2048]{1,0:T(8,128)(2,1)}, bf16[128,2048]{1,0:T(8,128)(2,1)}, u32[]{:S(2)}, u32[]{:S(2)}) collective-permute-start(bf16[128,2048]{1,0:T(8,128)(2,1)} %get-tuple-element.270), channel_id=1, source_target_pairs={{2,0},{3,1},{0,2},{1,3},{10,4},{11,5},{8,6},{9,7},{6,8},{7,9},{4,1... | collective-permute-start | bytes 1572872 | tf_op jit(solution)/shard_map/ppermute | solution.py:266
  620.9 31.4 %collective-permute-start.76 = (bf16[2,128,2304]{2,1,0:T(8,128)(2,1)}, bf16[2,128,2304]{2,1,0:T(8,128)(2,1)S(1)}, u32[]{:S(2)}, u32[]{:S(2)}) collective-permute-start(bf16[2,128,2304]{2,1,0:T(8,128)(2,1)} %get-tuple-element.310), channel_id=1, source_target_pairs={{0,16},{16,0},{8,24},{24,8},{1,17},{17,1},{9,25},{25,9},{2,18},{18... | collective-permute-start | bytes 3538952 | tf_op jit(solution)/shard_map/ppermute | solution.py:34
  (137 other events, 1331.7 us)
Sparse Core Ops, SparseCore 0:
  67.6 62.3 all-gather.2
  131.6 165.4 all-gather.4
  343.6 58.4 reduce-scatter.5
  404.2 110.7 reduce-scatter.3
  532.5 71.4 reduce-scatter.7
